TPU v7x, 256 devices: a whole 4x4x8 slice. The times are simulated.
256 devices in a mesh: replica: 16 (over z_lo, y), fsdp: 16 (over z_hi, x, core).
Axes of the slice: x: 4, y: 4, z: 8 (z_hi: 2, z_lo: 4; z = z_hi * 4 + z_lo), core: 2. Of those that a mesh axis runs over, the one named last changes fastest.
Arguments:
- tokens: bfloat16 [65536, 8192], P(('replica', 'fsdp')), may hold values from -24 to 24
- cotangent: bfloat16 [65536, 512], P(('replica', 'fsdp')), may hold values from -6 to 6
- w_value: bfloat16 [16, 8192, 512], P('replica', 'fsdp'), may hold values from -0.0625 to 0.0625
- outer_global: float32 [8, 256, 1024], P(None, 'fsdp'), may hold values from -6 to 6
- outer_momentum: float32 [8, 256, 1024], P(None, 'fsdp'), may hold values from -6 to 6
- local_params: float32 [16, 8, 256, 1024], P('replica', None, 'fsdp'), may hold values from -6 to 6
- outer_delta: float32 [16, 256, 1024], P('replica', 'fsdp'), may hold values from -6 to 6
- fragment: int32 [1], replicated, may hold values from 0 to 7
Outputs:
- values: bfloat16 [65536, 512], P(('replica', 'fsdp'))
- grad_tokens: bfloat16 [65536, 8192], P(('replica', 'fsdp'))
- grad_weight: float32 [16, 8192, 512], P('replica', 'fsdp')
- new_global: float32 [256, 1024], P('fsdp')
- new_momentum: float32 [256, 1024], P('fsdp')
- new_local: float32 [16, 256, 1024], P('replica', 'fsdp')
All inputs are finite; a program needn't handle non-finite values.
Results may differ from a plain program's by a relative error of at most 0.01.
Values may be sent and summed in bfloat16 or wider, within the bound.
No kernel may reach another device: no remote copies, remote signals or barrier semaphores. Data moves between devices by JAX's collectives and lax.ppermute only.
A program may use at most 128 MiB of HBM per device.

v0:
```python
import jax
import jax.numpy as jnp
from jax import lax
from jax.sharding import PartitionSpec as P

outer_rate = 0.7
momentum_decay = 0.9
mix_weight = 0.5


def nesterov(averaged, moment, global_part):
    moment_next = momentum_decay * moment + averaged
    global_next = global_part - outer_rate * (averaged + momentum_decay * moment_next)
    return (global_next, moment_next)


def body(
    tokens, cotangent, w_value, outer_global, outer_momentum, local_params, outer_delta, fragment
):
    whole_weight = lax.all_gather(w_value[0], "fsdp", axis=0, tiled=True)
    values = jnp.dot(tokens, whole_weight, preferred_element_type=jnp.float32).astype(jnp.bfloat16)
    grad_tokens = lax.dot_general(
        cotangent, whole_weight, (((1,), (1,)), ((), ())), preferred_element_type=jnp.float32
    ).astype(jnp.bfloat16)
    grad_weight = lax.psum_scatter(
        lax.dot_general(
            tokens, cotangent, (((0,), (0,)), ((), ())), preferred_element_type=jnp.float32
        ),
        "fsdp",
        scatter_dimension=0,
        tiled=True,
    )
    fragment_id = fragment[0]
    chosen_global = lax.dynamic_index_in_dim(outer_global, fragment_id, 0, keepdims=False)
    chosen_moment = lax.dynamic_index_in_dim(outer_momentum, fragment_id, 0, keepdims=False)
    chosen_local = lax.dynamic_index_in_dim(local_params[0], fragment_id, 0, keepdims=False)
    replicas = lax.axis_size("replica")
    summed = lax.psum(outer_delta[0].astype(jnp.bfloat16), "replica").astype(jnp.float32)
    new_global, new_momentum = nesterov(summed / replicas, chosen_moment, chosen_global)
    new_local = mix_weight * chosen_local + (1.0 - mix_weight) * new_global
    return (values, grad_tokens, grad_weight[None], new_global, new_momentum, new_local[None])


def solution(mesh):
    in_specs = (
        P(("replica", "fsdp"), None),
        P(("replica", "fsdp"), None),
        P("replica", "fsdp", None),
        P(None, "fsdp", None),
        P(None, "fsdp", None),
        P("replica", None, "fsdp", None),
        P("replica", "fsdp", None),
        P(),
    )
    out_specs = (
        P(("replica", "fsdp"), None),
        P(("replica", "fsdp"), None),
        P("replica", "fsdp", None),
        P("fsdp", None),
        P("fsdp", None),
        P("replica", "fsdp", None),
    )
    return jax.shard_map(body, mesh=mesh, in_specs=in_specs, out_specs=out_specs, check_vma=False)
```

profile of v0, /device:TPU:8, one launch (start us, length us, event | category | flops | bytes accessed | tf_op | source)
XLA Modules:
  0.0 351.1 jit_solution(11885710622492923398)
XLA Ops:
  7.2 0.0 copy-start
  7.2 0.0 all-gather.3.cloned.1.call-start
  7.2 0.7 all-gather.3.cloned.1.call-update
  7.9 0.0 reduce-scatter.2.cloned.1.call-start
  8.0 0.2 copy-done
  8.1 10.3 %fusion.8 = f32[8192,512]{1,0:T(8,128)} fusion(bf16[256,8192]{1,0:T(8,128)(2,1)} %param.8, bf16[256,512]{1,0:T(8,128)(2,1)S(1)} %copy-done), kind=kOutput, calls=%fused_computation.12 | convolution fusion | flops 2147483648 | bytes 21233664 | tf_op jit(solution)/shard_map/dot_general | solution.py:26
  18.4 0.0 copy-start.2
  18.4 0.0 reduce-scatter.2.cloned.1.call-update
  19.1 0.1 copy-done.2
  19.3 83.3 %psum.7 = bf16[16,1024]{1,0:T(8,128)(2,1)S(1)} all-reduce(bf16[16,1024]{1,0:T(8,128)(2,1)S(1)} %convert_bitcast_fusion), channel_id=1, replica_groups=mesh['replica'=16,'fsdp'=16] {'replica'}, use_global_device_ids=true, to_apply=%region_1.2 | all-reduce | flops 16384 | bytes 65536 | tf_op jit(solution)/shard_map/psum | solution.py:38
  102.5 1.6 fusion.7
  104.1 18.0 %all-gather.3.cloned.1.call-done = bf16[1,8192,512]{2,1,0:T(8,128)(2,1)} async-done(((bf16[1,512,512]{2,1,0:T(8,128)(2,1)}), bf16[1,8192,512]{2,1,0:T(8,128)(2,1)}) %all-gather.3.cloned.1.call-update) | async-done | bytes 8388624 | tf_op jit(solution)/shard_map/all_gather | solution.py:20
  122.1 0.0 copy-start.1
  122.1 0.0 copy-start.3
  122.1 7.9 %convolution_convert_fusion = bf16[256,8192]{1,0:T(8,128)(2,1)} fusion(bf16[256,512]{1,0:T(8,128)(2,1)S(1)} %copy-done, bf16[1,8192,512]{2,1,0:T(8,128)(2,1)} %all-gather.3.cloned.1.call-done), kind=kOutput, calls=%fused_computation | convolution fusion | flops 2149580800 | bytes 12845056 | tf_op jit(solution)/shard_map/dot_general | solution.py:22
  130.0 0.0 copy-done.1
  130.0 0.0 copy-done.3
  130.0 3.0 fusion.3
  133.0 211.2 %reduce-scatter.2.cloned.1.call-done = f32[512,512]{1,0:T(8,128)} async-done(((f32[8192,512]{1,0:T(8,128)}), f32[512,512]{1,0:T(8,128)}) %reduce-scatter.2.cloned.1.call-update) | async-done | bytes 1048592 | tf_op jit(solution)/shard_map/reduce_scatter | solution.py:25
  (1 shorter events, 0.0 us)
Async XLA Ops:
  7.2 1.0 copy-start
  7.2 114.9 %all-gather.3.cloned.1.call-start = ((), (), s32[]{:S(2)}) async-start(), calls=%async_computation.2 | async-start | bytes 8912896 | tf_op jit(solution)/shard_map/all_gather | solution.py:20
  7.9 336.4 %reduce-scatter.2.cloned.1.call-start = ((), (), s32[]{:S(2)}) async-start(), calls=%async_computation.1 | async-start | bytes 17825792 | tf_op jit(solution)/shard_map/reduce_scatter | solution.py:25
  18.4 0.8 copy-start.2
  122.1 7.9 %copy-start.1 = (bf16[256,8192]{1,0:T(8,128)(2,1)S(1)}, bf16[256,8192]{1,0:T(8,128)(2,1)}, u32[]{:S(2)}) copy-start(bf16[256,8192]{1,0:T(8,128)(2,1)} %param.8) | copy-start | bytes 12582916
  122.1 7.9 %copy-start.3 = (bf16[1,8192,512]{2,1,0:T(8,128)(2,1)S(1)}, bf16[1,8192,512]{2,1,0:T(8,128)(2,1)}, u32[]{:S(2)}) copy-start(bf16[1,8192,512]{2,1,0:T(8,128)(2,1)} %all-gather.3.cloned.1.call-done) | copy-start | bytes 25165828
Sparse Core Ops, SparseCore 0:
  10.7 111.2 all-gather.2
  127.3 216.9 reduce-scatter.1
where the time goes:
time: 352 us; the launch traced here: 351 us
  waiting for transfers between devices  230 us (65%)
  blocking collectives  83.3 us (24%)
  matrix products  21.2 us (6%)
  between operations  14.7 us (4%)
    reduce_scatter x1, waiting for transfers between devices, body(): lax.psum_scatter(lax.dot_general(tokens, cotangent, (((0,), (0,)), ((), (...  211 us
    psum x1, blocking collectives, body(): lax.psum(outer_delta[0].astype(jnp.bfloat16), 'replica').astype(jnp.float32)  83.3 us
    all_gather x1, waiting for transfers between devices, body(): whole_weight = lax.all_gather(w_value[0], 'fsdp', axis=0, tiled=True)  18 us
    dot_general x1, matrix products, body(): lax.dot_general(tokens, cotangent, (((0,), (0,)), ((), ())), preferred_el...  10.3 us
    dot_general x1, matrix products, body(): lax.dot_general(cotangent, whole_weight, (((1,), (1,)), ((), ())), prefer...  7.92 us
  transfers between devices with their start and end apart: 2, of which 2 were waited for; matrix products, arithmetic and copies ran while one was open for 7% of the time, Pallas kernels for 0%

commit v1 on v0

v1 whole, which is shorter than its diff:
```python
import jax
import jax.numpy as jnp
from jax import lax
from jax.experimental import pallas as pl
from jax.experimental.pallas import tpu as pltpu
from jax.sharding import PartitionSpec as P

outer_rate = 0.7
momentum_decay = 0.9
mix_weight = 0.5

f32, bf16 = jnp.float32, jnp.bfloat16
VMEM_LIMIT = 32 * 1024 * 1024
NX, NZ, NC = 4, 2, 2


def fsdp_perm(dz, dx, dc):
    pairs = []
    for z in range(NZ):
        for x in range(NX):
            for c in range(NC):
                there = (((z + dz) % NZ) * NX + (x + dx) % NX) * NC + (c + dc) % NC
                pairs.append(((z * NX + x) * NC + c, there))
    return pairs


PLUS, MINUS = fsdp_perm(0, 1, 0), fsdp_perm(0, -1, 0)
ACROSS, OTHER_CORE = fsdp_perm(1, 0, 0), fsdp_perm(0, 0, 1)


def send(array, pairs):
    return lax.ppermute(array, "fsdp", pairs)


def params(**more):
    return pltpu.CompilerParams(vmem_limit_bytes=VMEM_LIMIT, **more)


def dot(a, b, ca, cb):
    return lax.dot_general(a, b, (((ca,), (cb,)), ((), ())), preferred_element_type=f32)


def select_kernel(places, tokens, cotangent, out):
    step = pl.program_id(0)

    @pl.when(step < 8)
    def _():
        out[0] = tokens[...]

    @pl.when(step == 8)
    def _():
        out[0] = cotangent[...]


def select(places, tokens, cotangent):
    rows, width = cotangent.shape
    return pl.pallas_call(
        select_kernel,
        grid_spec=pltpu.PrefetchScalarGridSpec(
            num_scalar_prefetch=1,
            grid=(9,),
            in_specs=[
                pl.BlockSpec((rows, width), lambda i, p: (0, p[i])),
                pl.BlockSpec((rows, width), lambda i, p: (0, 0)),
            ],
            out_specs=pl.BlockSpec((1, rows, width), lambda i, p: (i, 0, 0)),
        ),
        out_shape=jax.ShapeDtypeStruct((9, rows, width), bf16),
        compiler_params=params(),
        cost_estimate=pl.CostEstimate(flops=0, bytes_accessed=18 * rows * width * 2, transcendentals=0),
        name="select",
    )(places, tokens, cotangent)


def far_kernel(places, tokens, cot, par, par_cot, top, bottom):
    block = dot(tokens[...], cot[...], 0, 0) + dot(par[0], par_cot[0], 0, 0)
    half = block.shape[0] // 2
    top[0] = block[:half].astype(bf16)
    bottom[0] = block[half:].astype(bf16)


def far_partials(places, tokens, cot, swapped):
    rows, width = cot.shape
    half = width // 2
    order = lambda i: 6 - 4 * i
    return pl.pallas_call(
        far_kernel,
        grid_spec=pltpu.PrefetchScalarGridSpec(
            num_scalar_prefetch=1,
            grid=(2,),
            in_specs=[
                pl.BlockSpec((rows, width), lambda i, p: (0, p[order(i)])),
                pl.BlockSpec((rows, width), lambda i, p: (0, 0)),
                pl.BlockSpec((1, rows, width), lambda i, p: (order(i), 0, 0)),
                pl.BlockSpec((1, rows, width), lambda i, p: (8, 0, 0)),
            ],
            out_specs=[pl.BlockSpec((1, half, width), lambda i, p: (i, 0, 0))] * 2,
        ),
        out_shape=[jax.ShapeDtypeStruct((2, half, width), bf16)] * 2,
        compiler_params=params(),
        cost_estimate=pl.CostEstimate(
            flops=2 * 4 * rows * width * width, bytes_accessed=10 * rows * width * 2, transcendentals=0
        ),
        name="far_partials",
    )(places, tokens, cot, swapped, swapped)


def near_kernel(places, tokens, cot, par, par_cot, out):
    out[0] = dot(tokens[...], cot[...], 0, 0) + dot(par[0], par_cot[0], 0, 0)


def near_partials(places, tokens, cot, swapped):
    rows, width = cot.shape

    def order(i):
        k = lax.rem(i, 3)
        return jnp.where(i < 3, 4, 0) + jnp.where(k == 0, 1, jnp.where(k == 1, 3, 0))

    return pl.pallas_call(
        near_kernel,
        grid_spec=pltpu.PrefetchScalarGridSpec(
            num_scalar_prefetch=1,
            grid=(6,),
            in_specs=[
                pl.BlockSpec((rows, width), lambda i, p: (0, p[order(i)])),
                pl.BlockSpec((rows, width), lambda i, p: (0, 0)),
                pl.BlockSpec((1, rows, width), lambda i, p: (order(i), 0, 0)),
                pl.BlockSpec((1, rows, width), lambda i, p: (8, 0, 0)),
            ],
            out_specs=pl.BlockSpec((1, width, width), lambda i, p: (i, 0, 0)),
        ),
        out_shape=jax.ShapeDtypeStruct((6, width, width), f32),
        compiler_params=params(),
        cost_estimate=pl.CostEstimate(
            flops=6 * 4 * rows * width * width,
            bytes_accessed=26 * rows * width * 2 + 6 * width * width * 4,
            transcendentals=0,
        ),
        name="near_partials",
    )(places, tokens, cot, swapped, swapped)


def relay_kernel(near, top, bottom, plus, minus):
    half = top.shape[1]
    plus[:half] = (near[0, :half] + top[0].astype(f32)).astype(bf16)
    plus[half:] = near[0, half:].astype(bf16)
    minus[:half] = near[1, :half].astype(bf16)
    minus[half:] = (near[1, half:] + bottom[0].astype(f32)).astype(bf16)


def relay(near, top, bottom, part):
    width = near.shape[1]
    half = width // 2
    return pl.pallas_call(
        relay_kernel,
        grid=(1,),
        in_specs=[
            pl.BlockSpec((3, width, width), lambda i: (part, 0, 0)),
            pl.BlockSpec((1, half, width), lambda i: (part, 0, 0)),
            pl.BlockSpec((1, half, width), lambda i: (part, 0, 0)),
        ],
        out_specs=[pl.BlockSpec((width, width), lambda i: (0, 0))] * 2,
        out_shape=[jax.ShapeDtypeStruct((width, width), bf16)] * 2,
        compiler_params=params(),
        cost_estimate=pl.CostEstimate(flops=width * width, bytes_accessed=7 * width * width * 2, transcendentals=0),
        name="relay",
    )(near, top, bottom)


def apply_kernel(first, places, tokens, par, cot, par_cot, w0, w1, w2a, w2b, w3, *rest):
    if first:
        v_own, v_par, grad, grad_par = rest
    else:
        v_own_in, v_par_in, _, v_own, v_par, grad, grad_par = rest
    step = pl.program_id(0)
    half = w2a.shape[0]

    @pl.when(step == 0)
    def _():
        if first:
            v_own[...] = jnp.zeros_like(v_own)
            v_par[...] = jnp.zeros_like(v_par)
        else:
            v_own[...] = v_own_in[...]
            v_par[...] = v_par_in[...]

    for k, w in ((0, w0), (1, w1), (3, w3)):

        @pl.when(step == k)
        def _(w=w):
            v_own[...] += dot(tokens[...], w[...], 1, 0)
            v_par[...] += dot(par[0], w[...], 1, 0)
            grad[...] = dot(cot[...], w[...], 1, 1).astype(bf16)
            grad_par[0] = dot(par_cot[0], w[...], 1, 1).astype(bf16)

    @pl.when(step == 2)
    def _():
        v_own[...] += dot(tokens[:, :half], w2a[...], 1, 0) + dot(tokens[:, half:], w2b[...], 1, 0)
        v_par[...] += dot(par[0, :, :half], w2a[...], 1, 0) + dot(par[0, :, half:], w2b[...], 1, 0)
        grad[:, :half] = dot(cot[...], w2a[...], 1, 1).astype(bf16)
        grad[:, half:] = dot(cot[...], w2b[...], 1, 1).astype(bf16)
        grad_par[0, :, :half] = dot(par_cot[0], w2a[...], 1, 1).astype(bf16)
        grad_par[0, :, half:] = dot(par_cot[0], w2b[...], 1, 1).astype(bf16)


def apply_weight(places, tokens, swapped, cot, pieces, carry, part):
    rows, width = cot.shape
    first = carry is None
    base = 4 * part
    full = lambda shape: pl.BlockSpec(shape, lambda i, p: (0,) * len(shape))
    v_spec = full((rows, width))
    grad_spec = pl.BlockSpec((rows, width), lambda i, p: (0, p[base + i]))
    in_specs = [
        pl.BlockSpec((rows, width), lambda i, p: (0, p[base + i])),
        pl.BlockSpec((1, rows, width), lambda i, p: (base + i, 0, 0)),
        full((rows, width)),
        pl.BlockSpec((1, rows, width), lambda i, p: (8, 0, 0)),
    ] + [full(w.shape) for w in pieces]
    operands = [places, tokens, swapped, cot, swapped, *pieces]
    aliases = {}
    if not first:
        aliases = {len(operands): 0, len(operands) + 1: 1, len(operands) + 2: 2}
        in_specs += [v_spec, v_spec, pl.BlockSpec(memory_space=pl.ANY)]
        operands += carry
    return pl.pallas_call(
        lambda *refs: apply_kernel(first, *refs),
        grid_spec=pltpu.PrefetchScalarGridSpec(
            num_scalar_prefetch=1,
            grid=(4,),
            in_specs=in_specs,
            out_specs=[v_spec, v_spec, grad_spec, pl.BlockSpec((1, rows, width), lambda i, p: (i, 0, 0))],
        ),
        out_shape=[
            jax.ShapeDtypeStruct((rows, width), f32),
            jax.ShapeDtypeStruct((rows, width), f32),
            jax.ShapeDtypeStruct(tokens.shape, bf16),
            jax.ShapeDtypeStruct((4, rows, width), bf16),
        ],
        input_output_aliases=aliases,
        compiler_params=params(),
        cost_estimate=pl.CostEstimate(
            flops=4 * 8 * rows * width * width,
            bytes_accessed=16 * rows * width * 2 + 4 * width * width * 2 + 8 * rows * width * 2,
            transcendentals=0,
        ),
        name="apply_weight",
    )(*operands)


def place_kernel(places, blocks, _, out):
    out[...] = blocks[0]


def place(places, blocks, whole, part):
    count, rows, width = blocks.shape
    return pl.pallas_call(
        place_kernel,
        grid_spec=pltpu.PrefetchScalarGridSpec(
            num_scalar_prefetch=1,
            grid=(count,),
            in_specs=[
                pl.BlockSpec((1, rows, width), lambda i, p: (i, 0, 0)),
                pl.BlockSpec(memory_space=pl.ANY),
            ],
            out_specs=pl.BlockSpec((rows, width), lambda i, p: (0, p[4 * part + i])),
        ),
        out_shape=jax.ShapeDtypeStruct(whole.shape, bf16),
        input_output_aliases={2: 0},
        compiler_params=params(),
        cost_estimate=pl.CostEstimate(flops=0, bytes_accessed=2 * count * rows * width * 2, transcendentals=0),
        name="place",
    )(places, blocks, whole)


def gather_pieces(shard):
    half = shard.shape[0] // 2
    behind = send(shard, PLUS)
    ahead = send(shard, MINUS)
    far_top = send(behind[:half], PLUS)
    far_bottom = send(ahead[half:], MINUS)
    return (shard, ahead, far_top, far_bottom, behind)


def replica_sum(part):
    for bit in (1, 2, 4, 8):
        part = part + lax.ppermute(part, "replica", [(i, i ^ bit) for i in range(16)])
    return part


def nesterov(averaged, moment, global_part):
    moment_next = momentum_decay * moment + averaged
    global_next = global_part - outer_rate * (averaged + momentum_decay * moment_next)
    return (global_next, moment_next)


def body(
    tokens, cotangent, w_value, outer_global, outer_momentum, local_params, outer_delta, fragment
):
    me = lax.axis_index("fsdp")
    core, x, z = lax.rem(me, NC), lax.rem(me // NC, NX), me // (NC * NX)
    steps = jnp.arange(8, dtype=jnp.int32)
    chips = lax.rem(z + steps // NX, NZ) * NX + lax.rem(x + steps, NX)
    own = chips * NC + core
    other = chips * NC + (1 - core)

    shard = w_value[0]
    shard_across = send(shard, ACROSS)
    pieces = gather_pieces(shard)
    outgoing = select(jnp.concatenate([other, other[:1]]), tokens, cotangent)
    swapped = send(outgoing, OTHER_CORE)

    top, bottom = far_partials(own, tokens, cotangent, swapped)
    top, bottom = send(top, PLUS), send(bottom, MINUS)
    near = near_partials(own, tokens, cotangent, swapped)
    plus, minus = relay(near, top, bottom, 0)
    from_left, from_right = send(plus, PLUS), send(minus, MINUS)
    across = (near[2] + from_left.astype(f32) + from_right.astype(f32)).astype(bf16)
    from_across = send(across, ACROSS)

    v_own, v_par, grad, grad_par = apply_weight(own, tokens, swapped, cotangent, pieces, None, 0)
    grad_back = send(grad_par, OTHER_CORE)

    pieces = gather_pieces(shard_across)
    plus, minus = relay(near, top, bottom, 1)
    from_left, from_right = send(plus, PLUS), send(minus, MINUS)

    grad = place(other, grad_back, grad, 0)
    v_own, v_par, grad, grad_par = apply_weight(
        own, tokens, swapped, cotangent, pieces, [v_own, v_par, grad], 1
    )
    v_back = send(v_par, OTHER_CORE)
    grad = place(other, send(grad_par, OTHER_CORE), grad, 1)
    values = (v_own + v_back).astype(bf16)
    grad_weight = (
        near[5] + from_left.astype(f32) + from_right.astype(f32) + from_across.astype(f32)
    )

    fragment_id = fragment[0]
    chosen_global = lax.dynamic_index_in_dim(outer_global, fragment_id, 0, keepdims=False)
    chosen_moment = lax.dynamic_index_in_dim(outer_momentum, fragment_id, 0, keepdims=False)
    chosen_local = lax.dynamic_index_in_dim(local_params[0], fragment_id, 0, keepdims=False)
    replicas = lax.axis_size("replica")
    summed = replica_sum(outer_delta[0])
    new_global, new_momentum = nesterov(summed / replicas, chosen_moment, chosen_global)
    new_local = mix_weight * chosen_local + (1.0 - mix_weight) * new_global
    return (values, grad, grad_weight[None], new_global, new_momentum, new_local[None])


def solution(mesh):
    in_specs = (
        P(("replica", "fsdp"), None),
        P(("replica", "fsdp"), None),
        P("replica", "fsdp", None),
        P(None, "fsdp", None),
        P(None, "fsdp", None),
        P("replica", None, "fsdp", None),
        P("replica", "fsdp", None),
        P(),
    )
    out_specs = (
        P(("replica", "fsdp"), None),
        P(("replica", "fsdp"), None),
        P("replica", "fsdp", None),
        P("fsdp", None),
        P("fsdp", None),
        P("replica", "fsdp", None),
    )
    return jax.shard_map(body, mesh=mesh, in_specs=in_specs, out_specs=out_specs, check_vma=False)
```

time: 352 us -> 128 us (0.36)
  the two profiles are of different devices: /device:TPU:8 before, /device:TPU:81 now
where the time goes in v1:
time: 128 us
  waiting for transfers between devices  61.2 us (48%)
  starting transfers between devices  33.3 us (26%)
  Pallas kernels  20.9 us (16%)
  other arithmetic  7.54 us (6%)
  local copies, waits for them, and re-layouts  3.23 us (3%)
  between operations  1.56 us (1%)
    ppermute x20, waiting for transfers between devices, send(): return lax.ppermute(array, 'fsdp', pairs)  61.2 us
    ppermute x20, starting transfers between devices, send(): return lax.ppermute(array, 'fsdp', pairs)  31.6 us
    pallas_call x2, Pallas kernels, apply_weight(): pl.pallas_call(lambda *refs: apply_kernel(first, *refs), grid_spec=pltpu....  9.01 us
    pallas_call x2, Pallas kernels, place(): pl.pallas_call(place_kernel, grid_spec=pltpu.PrefetchScalarGridSpec(num_s...  4.18 us
    pallas_call x1, Pallas kernels, near_partials(): pl.pallas_call(near_kernel, grid_spec=pltpu.PrefetchScalarGridSpec(num_sc...  3.71 us
    unnamed x14, local copies, waits for them, and re-layouts  3.16 us
    broadcast_in_dim x1, other arithmetic, body(): grad_weight[None]  2.91 us
  transfers between devices with their start and end apart: 24, of which 5 were waited for; matrix products, arithmetic and copies ran while one was open for 6% of the time, Pallas kernels for 14%

profile of v1, /device:TPU:81, one launch (start us, length us, event | category | flops | bytes accessed | tf_op | source)
XLA Modules:
  0.0 127.8 jit_solution(589393538769732979)
XLA Ops:
  0.8 2.2 %copy-done = bf16[256,8192]{1,0:T(8,128)(2,1)S(1)} copy-done((bf16[256,8192]{1,0:T(8,128)(2,1)S(1)}, bf16[256,8192]{1,0:T(8,128)(2,1)}, u32[]{:S(2)}) %copy-start) | copy-done | bytes 4194328
  3.0 0.9 copy-done.3
  3.9 1.1 select.19
  5.1 0.8 collective-permute-start
  5.8 1.2 collective-permute-start.7
  7.1 1.5 %collective-permute-start.6 = (bf16[512,512]{1,0:T(8,128)(2,1)S(1)}, bf16[512,512]{1,0:T(8,128)(2,1)S(1)}, u32[]{:S(2)}, u32[]{:S(2)}) collective-permute-start(bf16[512,512]{1,0:T(8,128)(2,1)S(1)} %bitcast.43), channel_id=1, source_target_pairs={{0,6},{1,7},{2,0},{3,1},{4,2},{5,3},{6,4},{7,5},{8,14},{9,15},{10,... | collective-permute-start | bytes 1572872 | tf_op jit(solution)/shard_map/ppermute | solution.py:32
  8.5 12.0 %collective-permute-done.7.refs_9_ = bf16[512,512]{1,0:T(8,128)(2,1)S(1)} collective-permute-done((bf16[512,512]{1,0:T(8,128)(2,1)S(1)}, bf16[512,512]{1,0:T(8,128)(2,1)S(1)}, u32[]{:S(2)}, u32[]{:S(2)}) %collective-permute-start.7) | collective-permute-done | bytes 524320 | tf_op jit(solution)/shard_map/ppermute | solution.py:32
  20.7 2.7 %collective-permute-start.9 = (bf16[256,512]{1,0:T(8,128)(2,1)S(1)}, bf16[256,512]{1,0:T(8,128)(2,1)S(1)}, u32[]{:S(2)}, u32[]{:S(2)}) collective-permute-start(bf16[256,512]{1,0:T(8,128)(2,1)S(1)} %slice.31), channel_id=1, source_target_pairs={{0,6},{1,7},{2,0},{3,1},{4,2},{5,3},{6,4},{7,5},{8,14},{9,15},{10,... | collective-permute-start | bytes 786440 | tf_op jit(solution)/shard_map/ppermute | solution.py:32
  23.4 5.1 %collective-permute-start.1 = (bf16[512,512]{1,0:T(8,128)(2,1)S(1)}, bf16[512,512]{1,0:T(8,128)(2,1)S(1)}, u32[]{:S(2)}, u32[]{:S(2)}) collective-permute-start(bf16[512,512]{1,0:T(8,128)(2,1)S(1)} %bitcast.44), channel_id=1, source_target_pairs={{0,8},{1,9},{2,10},{3,11},{4,12},{5,13},{6,14},{7,15},{8,0},{9,1},... | collective-permute-start | bytes 1572872 | tf_op jit(solution)/shard_map/ppermute | solution.py:32
  28.5 1.0 collective-permute-start.20
  29.6 4.5 %apply_weight.2 = (f32[256,512]{1,0:T(8,128)S(1)}, f32[256,512]{1,0:T(8,128)S(1)}, bf16[256,8192]{1,0:T(8,128)(2,1)}, bf16[4,256,512]{2,1,0:T(8,128)(2,1)S(1)}) custom-call(s32[8]{0:T(128)S(1)} %broadcast_add_fusion.1.refs_0_.places, bf16[256,8192]{1,0:T(8,128)(2,1)S(1)} %copy-done.1, ...), custom_call_target="tpu_custom_call" | custom-call | flops 2147483648 | bytes 8388608 | tf_op jit(solution)/shard_map/apply_weight/pallas_call | solution.py:225
  34.1 2.0 %collective-permute-start.10 = (bf16[4,256,512]{2,1,0:T(8,128)(2,1)S(1)}, bf16[4,256,512]{2,1,0:T(8,128)(2,1)S(1)}, u32[]{:S(2)}, u32[]{:S(2)}) collective-permute-start(bf16[4,256,512]{2,1,0:T(8,128)(2,1)S(1)} %get-tuple-element.22), channel_id=1, source_target_pairs={{0,1},{1,0},{2,3},{3,2},{4,5},{5,4},{6,7},{7,6},{8,9},{9,8},{10,11... | collective-permute-start | bytes 3145736 | tf_op jit(solution)/shard_map/ppermute | solution.py:32
  36.0 1.6 %far_partials.1 = (bf16[2,256,512]{2,1,0:T(8,128)(2,1)S(1)}, bf16[2,256,512]{2,1,0:T(8,128)(2,1)S(1)}) custom-call(s32[8]{0:T(128)S(1)} %broadcast_add_fusion.1.refs_0_.places, bf16[256,8192]{1,0:T(8,128)(2,1)S(1)} %copy-done.1, bf16[256,512]{1,0:T(8,128)(2,1)S(1)} %copy-done.4, bf16[9,256,512]{2,1,0:T(8,128)(2,1)S(1)} %collective-permute-done.refs_2_.refs_4_.par.par_cot, ...), custom_call_target="tpu_custom_call" | custom-call | flops 536870912 | bytes 2621440 | tf_op jit(solution)/shard_map/far_partials/pallas_call | solution.py:86
  38.2 2.7 %collective-permute-start.14 = (bf16[2,256,512]{2,1,0:T(8,128)(2,1)S(1)}, bf16[2,256,512]{2,1,0:T(8,128)(2,1)S(1)}, u32[]{:S(2)}, u32[]{:S(2)}) collective-permute-start(bf16[2,256,512]{2,1,0:T(8,128)(2,1)S(1)} %get-tuple-element.29), channel_id=1, source_target_pairs={{0,6},{1,7},{2,0},{3,1},{4,2},{5,3},{6,4},{7,5},{8,14},{9,15},{10,... | collective-permute-start | bytes 1572872 | tf_op jit(solution)/shard_map/ppermute | solution.py:32
  40.8 10.9 %collective-permute-done.1.refs_5_ = bf16[512,512]{1,0:T(8,128)(2,1)S(1)} collective-permute-done((bf16[512,512]{1,0:T(8,128)(2,1)S(1)}, bf16[512,512]{1,0:T(8,128)(2,1)S(1)}, u32[]{:S(2)}, u32[]{:S(2)}) %collective-permute-start.1) | collective-permute-done | bytes 524320 | tf_op jit(solution)/shard_map/ppermute | solution.py:32
  51.7 2.7 %collective-permute-start.2 = (bf16[512,512]{1,0:T(8,128)(2,1)S(1)}, bf16[512,512]{1,0:T(8,128)(2,1)S(1)}, u32[]{:S(2)}, u32[]{:S(2)}) collective-permute-start(bf16[512,512]{1,0:T(8,128)(2,1)S(1)} %collective-permute-done.1.refs_5_), channel_id=1, source_target_pairs={{0,6},{1,7},{2,0},{3,1},{4,2},{5,3},{6,4},{7,5},{8,14},{9,15},{10,... | collective-permute-start | bytes 1572872 | tf_op jit(solution)/shard_map/ppermute | solution.py:32
  54.7 3.7 %near_partials.1.near = f32[6,512,512]{2,1,0:T(8,128)S(1)} custom-call(s32[8]{0:T(128)S(1)} %broadcast_add_fusion.1.refs_0_.places, bf16[256,8192]{1,0:T(8,128)(2,1)S(1)} %copy-done.1, bf16[256,512]{1,0:T(8,128)(2,1)S(1)} %copy-done.4, bf16[9,256,512]{2,1,0:T(8,128)(2,1)S(1)} %collective-permute-done.refs_2_.refs_4_.par.par_cot, ...), custom_call_target="tpu_custom_call" | custom-call | flops 1610612736 | bytes 13107200 | tf_op jit(solution)/shard_map/near_partials/pallas_call | solution.py:119
  58.7 6.3 %collective-permute-done.3.refs_9_ = bf16[512,512]{1,0:T(8,128)(2,1)S(1)} collective-permute-done((bf16[512,512]{1,0:T(8,128)(2,1)S(1)}, bf16[512,512]{1,0:T(8,128)(2,1)S(1)}, u32[]{:S(2)}, u32[]{:S(2)}) %collective-permute-start.3) | collective-permute-done | bytes 524320 | tf_op jit(solution)/shard_map/ppermute | solution.py:32
  65.1 2.7 %collective-permute-start.5 = (bf16[256,512]{1,0:T(8,128)(2,1)S(1)}, bf16[256,512]{1,0:T(8,128)(2,1)S(1)}, u32[]{:S(2)}, u32[]{:S(2)}) collective-permute-start(bf16[256,512]{1,0:T(8,128)(2,1)S(1)} %slice.29), channel_id=1, source_target_pairs={{0,6},{1,7},{2,0},{3,1},{4,2},{5,3},{6,4},{7,5},{8,14},{9,15},{10,... | collective-permute-start | bytes 786440 | tf_op jit(solution)/shard_map/ppermute | solution.py:32
  67.9 1.2 relay.2
  69.1 2.1 %place.2.refs_12_ = bf16[256,8192]{1,0:T(8,128)(2,1)} custom-call(s32[8]{0:T(128)S(1)} %broadcast_add_fusion.places, bf16[4,256,512]{2,1,0:T(8,128)(2,1)S(1)} %collective-permute-done.10.blocks, bf16[256,8192]{1,0:T(8,128)(2,1)} %get-tuple-element.23._), custom_call_target="tpu_custom_call", output_to_operand_aliasing={{}: (2, {})} | custom-call | bytes 2097152 | tf_op jit(solution)/shard_map/place/pallas_call | solution.py:256
  71.2 11.8 %collective-permute-done.4.refs_7_ = bf16[256,512]{1,0:T(8,128)(2,1)S(1)} collective-permute-done((bf16[256,512]{1,0:T(8,128)(2,1)S(1)}, bf16[256,512]{1,0:T(8,128)(2,1)S(1)}, u32[]{:S(2)}, u32[]{:S(2)}) %collective-permute-start.4) | collective-permute-done | bytes 262176 | tf_op jit(solution)/shard_map/ppermute | solution.py:32
  82.9 1.5 %collective-permute-start.15 = (bf16[512,512]{1,0:T(8,128)(2,1)}, bf16[512,512]{1,0:T(8,128)(2,1)}, u32[]{:S(2)}, u32[]{:S(2)}) collective-permute-start(bf16[512,512]{1,0:T(8,128)(2,1)} %get-tuple-element.30), channel_id=1, source_target_pairs={{0,2},{1,3},{2,4},{3,5},{4,6},{5,7},{6,0},{7,1},{8,10},{9,11},{10,... | collective-permute-start | bytes 1572872 | tf_op jit(solution)/shard_map/ppermute | solution.py:32
  84.4 4.5 %apply_weight.3 = (f32[256,512]{1,0:T(8,128)S(1)}, f32[256,512]{1,0:T(8,128)S(1)}, bf16[256,8192]{1,0:T(8,128)(2,1)}, bf16[4,256,512]{2,1,0:T(8,128)(2,1)S(1)}) custom-call(s32[8]{0:T(128)S(1)} %broadcast_add_fusion.1.refs_0_.places, bf16[256,8192]{1,0:T(8,128)(2,1)S(1)} %copy-done.1, ...), custom_call_target="tpu_custom_call", output_to_operand_aliasing={{0}: (10, {}), {1}: (11, {}), {2}: (12, {})} | custom-call | flops 2147483648 | bytes 8388608 | tf_op jit(solution)/shard_map/apply_weight/pallas_call | solution.py:225
  89.0 3.8 %collective-permute-start.11 = (f32[256,512]{1,0:T(8,128)S(1)}, f32[256,512]{1,0:T(8,128)}, u32[]{:S(2)}, u32[]{:S(2)}) collective-permute-start(f32[256,512]{1,0:T(8,128)S(1)} %get-tuple-element.25), channel_id=1, source_target_pairs={{0,1},{1,0},{2,3},{3,2},{4,5},{5,4},{6,7},{7,6},{8,9},{9,8},{10,11... | collective-permute-start | bytes 1572872 | tf_op jit(solution)/shard_map/ppermute | solution.py:32
  92.8 1.0 fusion.2
  93.8 4.6 %collective-permute-start.19 = (bf16[512,512]{1,0:T(8,128)(2,1)}, bf16[512,512]{1,0:T(8,128)(2,1)}, u32[]{:S(2)}, u32[]{:S(2)}) collective-permute-start(bf16[512,512]{1,0:T(8,128)(2,1)} %fusion.2), channel_id=1, source_target_pairs={{0,8},{1,9},{2,10},{3,11},{4,12},{5,13},{6,14},{7,15},{8,0},{9,1},... | collective-permute-start | bytes 1572872 | tf_op jit(solution)/shard_map/ppermute | solution.py:32
  99.1 1.6 %fusion.8 = (f32[1,16,1024]{2,1,0:T(8,128)}, f32[16,1024]{1,0:T(8,128)}, f32[16,1024]{1,0:T(8,128)}) fusion(f32[1,8,16,1024]{3,2,1,0:T(8,128)} %param.13, s32[]{:T(128)S(6)} %select_n.22, f32[16,1024]{1,0:T(8,128)S(1)} %add.94, f32[16,1024]{1,0:T(8,128)S(1)} %collective-permute-done.23, f32[8,16,1024]{2,1,0:T(8,128)} %param.11, f32[8,16,1024]{2,1,0:T(8,128)} %param.12), kind=kLoop, calls=%fused_computation.12 | loop fusion | flops 163840 | bytes 524292 | tf_op jit(solution)/shard_map/broadcast_in_dim | solution.py:346
  100.7 1.8 %add_convert_fusion = bf16[256,512]{1,0:T(8,128)(2,1)} fusion(f32[256,512]{1,0:T(8,128)S(1)} %get-tuple-element.24, f32[256,512]{1,0:T(8,128)} %collective-permute-done.11), kind=kLoop, calls=%fused_computation.9 | loop fusion | flops 262144 | bytes 1310720 | tf_op jit(solution)/shard_map/convert_element_type | solution.py:333
  102.5 20.2 %collective-permute-done.19 = bf16[512,512]{1,0:T(8,128)(2,1)} collective-permute-done((bf16[512,512]{1,0:T(8,128)(2,1)}, bf16[512,512]{1,0:T(8,128)(2,1)}, u32[]{:S(2)}, u32[]{:S(2)}) %collective-permute-start.19) | collective-permute-done | bytes 524320 | tf_op jit(solution)/shard_map/ppermute | solution.py:32
  122.8 2.9 %fusion.6 = f32[1,512,512]{2,1,0:T(8,128)} fusion(f32[6,512,512]{2,1,0:T(8,128)} %copy-done.2, bf16[512,512]{1,0:T(8,128)(2,1)} %collective-permute-done.19, bf16[512,512]{1,0:T(8,128)(2,1)} %collective-permute-done.16, bf16[512,512]{1,0:T(8,128)(2,1)} %collective-permute-done.15), kind=kLoop, calls=%fused_computation.8 | loop fusion | flops 1572864 | bytes 3670016 | tf_op jit(solution)/shard_map/broadcast_in_dim | solution.py:346
  125.7 2.1 %place.3 = bf16[256,8192]{1,0:T(8,128)(2,1)} custom-call(s32[8]{0:T(128)S(1)} %broadcast_add_fusion.places, bf16[4,256,512]{2,1,0:T(8,128)(2,1)S(1)} %collective-permute-done.12.blocks, bf16[256,8192]{1,0:T(8,128)(2,1)} %get-tuple-element.27._), custom_call_target="tpu_custom_call", output_to_operand_aliasing={{}: (2, {})} | custom-call | bytes 2097152 | tf_op jit(solution)/shard_map/place/pallas_call | solution.py:256
  (53 shorter events, 1.6 us)
Async XLA Ops:
  0.6 27.9 %copy-start.6 = (f32[1,16,1024]{2,1,0:T(8,128)S(1)}, f32[1,16,1024]{2,1,0:T(8,128)}, u32[]{:S(2)}) copy-start(f32[1,16,1024]{2,1,0:T(8,128)} %param.14) | copy-start | bytes 196612
  0.8 2.2 %copy-start = (bf16[256,8192]{1,0:T(8,128)(2,1)S(1)}, bf16[256,8192]{1,0:T(8,128)(2,1)}, u32[]{:S(2)}) copy-start(bf16[256,8192]{1,0:T(8,128)(2,1)} %tokens.5) | copy-start | bytes 12582916
  3.0 0.9 copy-start.3
  3.9 1.9 %copy-start.5 = (bf16[1,512,512]{2,1,0:T(8,128)(2,1)S(1)}, bf16[1,512,512]{2,1,0:T(8,128)(2,1)}, u32[]{:S(2)}) copy-start(bf16[1,512,512]{2,1,0:T(8,128)(2,1)} %param.10) | copy-start | bytes 1572868
  3.9 25.6 %copy-start.1 = (bf16[256,8192]{1,0:T(8,128)(2,1)S(1)}, bf16[256,8192]{1,0:T(8,128)(2,1)}, u32[]{:S(2)}) copy-start(bf16[256,8192]{1,0:T(8,128)(2,1)} %tokens.5) | copy-start | bytes 12582916
  3.9 25.6 %copy-start.4 = (bf16[256,512]{1,0:T(8,128)(2,1)S(1)}, bf16[256,512]{1,0:T(8,128)(2,1)}, u32[]{:S(2)}) copy-start(bf16[256,512]{1,0:T(8,128)(2,1)} %cot.3) | copy-start | bytes 786436
  5.1 24.5 %collective-permute-start = (bf16[9,256,512]{2,1,0:T(8,128)(2,1)S(1)}, bf16[9,256,512]{2,1,0:T(8,128)(2,1)S(1)}, u32[]{:S(2)}, u32[]{:S(2)}) collective-permute-start(bf16[9,256,512]{2,1,0:T(8,128)(2,1)S(1)} %select.19), channel_id=1, source_target_pairs={{0,1},{1,0},{2,3},{3,2},{4,5},{5,4},{6,7},{7,6},{8,9},{9,8},{10,11... | collective-permute-start | bytes 7077896 | tf_op jit(solution)/shard_map/ppermute | solution.py:32
  5.8 14.7 %collective-permute-start.7 = (bf16[512,512]{1,0:T(8,128)(2,1)S(1)}, bf16[512,512]{1,0:T(8,128)(2,1)S(1)}, u32[]{:S(2)}, u32[]{:S(2)}) collective-permute-start(bf16[512,512]{1,0:T(8,128)(2,1)S(1)} %bitcast.42), channel_id=1, source_target_pairs={{0,2},{1,3},{2,4},{3,5},{4,6},{5,7},{6,0},{7,1},{8,10},{9,11},{10,... | collective-permute-start | bytes 1572872 | tf_op jit(solution)/shard_map/ppermute | solution.py:32
  7.1 13.6 %collective-permute-start.6 = (bf16[512,512]{1,0:T(8,128)(2,1)S(1)}, bf16[512,512]{1,0:T(8,128)(2,1)S(1)}, u32[]{:S(2)}, u32[]{:S(2)}) collective-permute-start(bf16[512,512]{1,0:T(8,128)(2,1)S(1)} %bitcast.43), channel_id=1, source_target_pairs={{0,6},{1,7},{2,0},{3,1},{4,2},{5,3},{6,4},{7,5},{8,14},{9,15},{10,... | collective-permute-start | bytes 1572872 | tf_op jit(solution)/shard_map/ppermute | solution.py:32
  20.5 9.0 %collective-permute-start.8 = (bf16[256,512]{1,0:T(8,128)(2,1)S(1)}, bf16[256,512]{1,0:T(8,128)(2,1)S(1)}, u32[]{:S(2)}, u32[]{:S(2)}) collective-permute-start(bf16[256,512]{1,0:T(8,128)(2,1)S(1)} %slice.30), channel_id=1, source_target_pairs={{0,2},{1,3},{2,4},{3,5},{4,6},{5,7},{6,0},{7,1},{8,10},{9,11},{10,... | collective-permute-start | bytes 786440 | tf_op jit(solution)/shard_map/ppermute | solution.py:32
  20.7 8.9 %collective-permute-start.9 = (bf16[256,512]{1,0:T(8,128)(2,1)S(1)}, bf16[256,512]{1,0:T(8,128)(2,1)S(1)}, u32[]{:S(2)}, u32[]{:S(2)}) collective-permute-start(bf16[256,512]{1,0:T(8,128)(2,1)S(1)} %slice.31), channel_id=1, source_target_pairs={{0,6},{1,7},{2,0},{3,1},{4,2},{5,3},{6,4},{7,5},{8,14},{9,15},{10,... | collective-permute-start | bytes 786440 | tf_op jit(solution)/shard_map/ppermute | solution.py:32
  23.4 28.3 %collective-permute-start.1 = (bf16[512,512]{1,0:T(8,128)(2,1)S(1)}, bf16[512,512]{1,0:T(8,128)(2,1)S(1)}, u32[]{:S(2)}, u32[]{:S(2)}) collective-permute-start(bf16[512,512]{1,0:T(8,128)(2,1)S(1)} %bitcast.44), channel_id=1, source_target_pairs={{0,8},{1,9},{2,10},{3,11},{4,12},{5,13},{6,14},{7,15},{8,0},{9,1},... | collective-permute-start | bytes 1572872 | tf_op jit(solution)/shard_map/ppermute | solution.py:32
  28.5 9.2 %collective-permute-start.20 = (f32[16,1024]{1,0:T(8,128)S(1)}, f32[16,1024]{1,0:T(8,128)S(1)}, u32[]{:S(2)}, u32[]{:S(2)}) collective-permute-start(f32[16,1024]{1,0:T(8,128)S(1)} %bitcast.47), channel_id=1, source_target_pairs={{0,16},{16,0},{32,48},{48,32},{64,80},{80,64},{96,112},{112,96},{1... | collective-permute-start | bytes 196616 | tf_op jit(solution)/shard_map/ppermute | solution.py:286
  34.1 35.0 %collective-permute-start.10 = (bf16[4,256,512]{2,1,0:T(8,128)(2,1)S(1)}, bf16[4,256,512]{2,1,0:T(8,128)(2,1)S(1)}, u32[]{:S(2)}, u32[]{:S(2)}) collective-permute-start(bf16[4,256,512]{2,1,0:T(8,128)(2,1)S(1)} %get-tuple-element.22), channel_id=1, source_target_pairs={{0,1},{1,0},{2,3},{3,2},{4,5},{5,4},{6,7},{7,6},{8,9},{9,8},{10,11... | collective-permute-start | bytes 3145736 | tf_op jit(solution)/shard_map/ppermute | solution.py:32
  37.6 16.8 %collective-permute-start.13 = (bf16[2,256,512]{2,1,0:T(8,128)(2,1)S(1)}, bf16[2,256,512]{2,1,0:T(8,128)(2,1)S(1)}, u32[]{:S(2)}, u32[]{:S(2)}) collective-permute-start(bf16[2,256,512]{2,1,0:T(8,128)(2,1)S(1)} %get-tuple-element.28), channel_id=1, source_target_pairs={{0,2},{1,3},{2,4},{3,5},{4,6},{5,7},{6,0},{7,1},{8,10},{9,11},{10,... | collective-permute-start | bytes 1572872 | tf_op jit(solution)/shard_map/ppermute | solution.py:32
  37.8 13.9 %collective-permute-start.21 = (f32[16,1024]{1,0:T(8,128)S(1)}, f32[16,1024]{1,0:T(8,128)S(1)}, u32[]{:S(2)}, u32[]{:S(2)}) collective-permute-start(f32[16,1024]{1,0:T(8,128)S(1)} %bitcast_add_fusion.2), channel_id=1, source_target_pairs={{0,32},{16,48},{32,0},{48,16},{64,96},{80,112},{96,64},{112,80},{1... | collective-permute-start | bytes 196616 | tf_op jit(solution)/shard_map/ppermute | solution.py:286
  38.2 20.2 %collective-permute-start.14 = (bf16[2,256,512]{2,1,0:T(8,128)(2,1)S(1)}, bf16[2,256,512]{2,1,0:T(8,128)(2,1)S(1)}, u32[]{:S(2)}, u32[]{:S(2)}) collective-permute-start(bf16[2,256,512]{2,1,0:T(8,128)(2,1)S(1)} %get-tuple-element.29), channel_id=1, source_target_pairs={{0,6},{1,7},{2,0},{3,1},{4,2},{5,3},{6,4},{7,5},{8,14},{9,15},{10,... | collective-permute-start | bytes 1572872 | tf_op jit(solution)/shard_map/ppermute | solution.py:32
  51.7 13.3 %collective-permute-start.3 = (bf16[512,512]{1,0:T(8,128)(2,1)S(1)}, bf16[512,512]{1,0:T(8,128)(2,1)S(1)}, u32[]{:S(2)}, u32[]{:S(2)}) collective-permute-start(bf16[512,512]{1,0:T(8,128)(2,1)S(1)} %collective-permute-done.1.refs_5_), channel_id=1, source_target_pairs={{0,2},{1,3},{2,4},{3,5},{4,6},{5,7},{6,0},{7,1},{8,10},{9,11},{10,... | collective-permute-start | bytes 1572872 | tf_op jit(solution)/shard_map/ppermute | solution.py:32
  51.7 13.3 %collective-permute-start.2 = (bf16[512,512]{1,0:T(8,128)(2,1)S(1)}, bf16[512,512]{1,0:T(8,128)(2,1)S(1)}, u32[]{:S(2)}, u32[]{:S(2)}) collective-permute-start(bf16[512,512]{1,0:T(8,128)(2,1)S(1)} %collective-permute-done.1.refs_5_), channel_id=1, source_target_pairs={{0,6},{1,7},{2,0},{3,1},{4,2},{5,3},{6,4},{7,5},{8,14},{9,15},{10,... | collective-permute-start | bytes 1572872 | tf_op jit(solution)/shard_map/ppermute | solution.py:32
  54.4 10.7 %collective-permute-start.22 = (f32[16,1024]{1,0:T(8,128)S(1)}, f32[16,1024]{1,0:T(8,128)S(1)}, u32[]{:S(2)}, u32[]{:S(2)}) collective-permute-start(f32[16,1024]{1,0:T(8,128)S(1)} %add.93), channel_id=1, source_target_pairs={{0,64},{16,80},{32,96},{48,112},{64,0},{80,16},{96,32},{112,48},{1... | collective-permute-start | bytes 196616 | tf_op jit(solution)/shard_map/ppermute | solution.py:286
  58.4 34.4 %copy-start.2 = (f32[6,512,512]{2,1,0:T(8,128)}, f32[6,512,512]{2,1,0:T(8,128)S(1)}, u32[]{:S(2)}) copy-start(f32[6,512,512]{2,1,0:T(8,128)S(1)} %near_partials.1.near) | copy-start | bytes 18874372
  58.6 30.4 %collective-permute-start.18 = (bf16[512,512]{1,0:T(8,128)(2,1)S(1)}, bf16[512,512]{1,0:T(8,128)(2,1)S(1)}, u32[]{:S(2)}, u32[]{:S(2)}) collective-permute-start(bf16[512,512]{1,0:T(8,128)(2,1)S(1)} %get-tuple-element.33), channel_id=1, source_target_pairs={{0,6},{1,7},{2,0},{3,1},{4,2},{5,3},{6,4},{7,5},{8,14},{9,15},{10,... | collective-permute-start | bytes 1572872 | tf_op jit(solution)/shard_map/ppermute | solution.py:32
  65.0 27.7 %collective-permute-start.17 = (bf16[512,512]{1,0:T(8,128)(2,1)S(1)}, bf16[512,512]{1,0:T(8,128)(2,1)S(1)}, u32[]{:S(2)}, u32[]{:S(2)}) collective-permute-start(bf16[512,512]{1,0:T(8,128)(2,1)S(1)} %get-tuple-element.32), channel_id=1, source_target_pairs={{0,2},{1,3},{2,4},{3,5},{4,6},{5,7},{6,0},{7,1},{8,10},{9,11},{10,... | collective-permute-start | bytes 1572872 | tf_op jit(solution)/shard_map/ppermute | solution.py:32
  65.0 17.9 %collective-permute-start.4 = (bf16[256,512]{1,0:T(8,128)(2,1)S(1)}, bf16[256,512]{1,0:T(8,128)(2,1)S(1)}, u32[]{:S(2)}, u32[]{:S(2)}) collective-permute-start(bf16[256,512]{1,0:T(8,128)(2,1)S(1)} %slice.28), channel_id=1, source_target_pairs={{0,2},{1,3},{2,4},{3,5},{4,6},{5,7},{6,0},{7,1},{8,10},{9,11},{10,... | collective-permute-start | bytes 786440 | tf_op jit(solution)/shard_map/ppermute | solution.py:32
  65.1 17.8 %collective-permute-start.5 = (bf16[256,512]{1,0:T(8,128)(2,1)S(1)}, bf16[256,512]{1,0:T(8,128)(2,1)S(1)}, u32[]{:S(2)}, u32[]{:S(2)}) collective-permute-start(bf16[256,512]{1,0:T(8,128)(2,1)S(1)} %slice.29), channel_id=1, source_target_pairs={{0,6},{1,7},{2,0},{3,1},{4,2},{5,3},{6,4},{7,5},{8,14},{9,15},{10,... | collective-permute-start | bytes 786440 | tf_op jit(solution)/shard_map/ppermute | solution.py:32
  69.1 24.8 %collective-permute-start.23 = (f32[16,1024]{1,0:T(8,128)S(1)}, f32[16,1024]{1,0:T(8,128)S(1)}, u32[]{:S(2)}, u32[]{:S(2)}) collective-permute-start(f32[16,1024]{1,0:T(8,128)S(1)} %add.94), channel_id=1, source_target_pairs={{0,128},{16,144},{32,160},{48,176},{64,192},{80,208},{96,224},{112... | collective-permute-start | bytes 196616 | tf_op jit(solution)/shard_map/ppermute | solution.py:286
  82.9 19.6 %collective-permute-start.16 = (bf16[512,512]{1,0:T(8,128)(2,1)}, bf16[512,512]{1,0:T(8,128)(2,1)}, u32[]{:S(2)}, u32[]{:S(2)}) collective-permute-start(bf16[512,512]{1,0:T(8,128)(2,1)} %get-tuple-element.31), channel_id=1, source_target_pairs={{0,6},{1,7},{2,0},{3,1},{4,2},{5,3},{6,4},{7,5},{8,14},{9,15},{10,... | collective-permute-start | bytes 1572872 | tf_op jit(solution)/shard_map/ppermute | solution.py:32
  82.9 19.6 %collective-permute-start.15 = (bf16[512,512]{1,0:T(8,128)(2,1)}, bf16[512,512]{1,0:T(8,128)(2,1)}, u32[]{:S(2)}, u32[]{:S(2)}) collective-permute-start(bf16[512,512]{1,0:T(8,128)(2,1)} %get-tuple-element.30), channel_id=1, source_target_pairs={{0,2},{1,3},{2,4},{3,5},{4,6},{5,7},{6,0},{7,1},{8,10},{9,11},{10,... | collective-permute-start | bytes 1572872 | tf_op jit(solution)/shard_map/ppermute | solution.py:32
  89.0 11.7 %collective-permute-start.11 = (f32[256,512]{1,0:T(8,128)S(1)}, f32[256,512]{1,0:T(8,128)}, u32[]{:S(2)}, u32[]{:S(2)}) collective-permute-start(f32[256,512]{1,0:T(8,128)S(1)} %get-tuple-element.25), channel_id=1, source_target_pairs={{0,1},{1,0},{2,3},{3,2},{4,5},{5,4},{6,7},{7,6},{8,9},{9,8},{10,11... | collective-permute-start | bytes 1572872 | tf_op jit(solution)/shard_map/ppermute | solution.py:32
  92.7 33.0 %collective-permute-start.12 = (bf16[4,256,512]{2,1,0:T(8,128)(2,1)S(1)}, bf16[4,256,512]{2,1,0:T(8,128)(2,1)S(1)}, u32[]{:S(2)}, u32[]{:S(2)}) collective-permute-start(bf16[4,256,512]{2,1,0:T(8,128)(2,1)S(1)} %get-tuple-element.26), channel_id=1, source_target_pairs={{0,1},{1,0},{2,3},{3,2},{4,5},{5,4},{6,7},{7,6},{8,9},{9,8},{10,11... | collective-permute-start | bytes 3145736 | tf_op jit(solution)/shard_map/ppermute | solution.py:32
  93.8 29.0 %collective-permute-start.19 = (bf16[512,512]{1,0:T(8,128)(2,1)}, bf16[512,512]{1,0:T(8,128)(2,1)}, u32[]{:S(2)}, u32[]{:S(2)}) collective-permute-start(bf16[512,512]{1,0:T(8,128)(2,1)} %fusion.2), channel_id=1, source_target_pairs={{0,8},{1,9},{2,10},{3,11},{4,12},{5,13},{6,14},{7,15},{8,0},{9,1},... | collective-permute-start | bytes 1572872 | tf_op jit(solution)/shard_map/ppermute | solution.py:32

commit v2 on v0

v2 whole, which is shorter than its diff:
```python
import jax
import jax.numpy as jnp
from jax import lax
from jax.experimental import pallas as pl
from jax.experimental.pallas import tpu as pltpu
from jax.sharding import PartitionSpec as P

outer_rate = 0.7
momentum_decay = 0.9
mix_weight = 0.5

f32, bf16 = jnp.float32, jnp.bfloat16
NX, NZ, NC = 4, 2, 2
CUT = 256
HOLD = 14
WHOLE = pl.BlockSpec(memory_space=pltpu.VMEM)
FAR = pl.BlockSpec(memory_space=pltpu.HBM)
INDEX = pl.BlockSpec(memory_space=pltpu.SMEM)
DMAS = pltpu.SemaphoreType.DMA


def fsdp_perm(dz, dx, dc):
    pairs = []
    for z in range(NZ):
        for x in range(NX):
            for c in range(NC):
                there = (((z + dz) % NZ) * NX + (x + dx) % NX) * NC + (c + dc) % NC
                pairs.append(((z * NX + x) * NC + c, there))
    return pairs


PLUS, MINUS = fsdp_perm(0, 1, 0), fsdp_perm(0, -1, 0)
ACROSS, OTHER_CORE, DIAGONAL = fsdp_perm(1, 0, 0), fsdp_perm(0, 0, 1), fsdp_perm(1, 0, 1)


def send(array, pairs):
    return lax.ppermute(array, "fsdp", pairs)


def after(value, *earlier):
    return lax.optimization_barrier((value, *earlier))[0]


def call(kernel, name, in_specs, out_specs, out_shape, operands, scratch=(), aliases={}, limit=16, traffic=2):
    return pl.pallas_call(
        kernel,
        in_specs=in_specs,
        out_specs=out_specs,
        out_shape=out_shape,
        scratch_shapes=scratch,
        input_output_aliases=aliases,
        compiler_params=pltpu.CompilerParams(vmem_limit_bytes=limit * 1024 * 1024),
        cost_estimate=pl.CostEstimate(flops=0, bytes_accessed=traffic * 1024 * 1024, transcendentals=0),
        name=name,
    )(*operands)


def dot(a, b, ca, cb):
    return lax.dot_general(a, b, (((ca,), (cb,)), ((), ())), preferred_element_type=f32)


def columns(whole, place, width):
    return whole.at[:, pl.ds(pl.multiple_of(place * width, width), width)]


FIRST, SECOND = (6, 2), (4, 5, 7, 0, 1, 3)


def select_kernel(places, tokens, cot, first, second, sems):
    width = cot.shape[1]
    copies = [pltpu.make_async_copy(cot, first.at[len(FIRST)], sems.at[8])]
    for out, blocks in ((first, FIRST), (second, SECOND)):
        for i, b in enumerate(blocks):
            copies.append(pltpu.make_async_copy(columns(tokens, places[b], width), out.at[i], sems.at[b]))
    for copy in copies:
        copy.start()
    for copy in copies:
        copy.wait()


def select(places, tokens, cot):
    return call(
        select_kernel,
        "select",
        [INDEX, WHOLE, WHOLE],
        [WHOLE] * 2,
        [jax.ShapeDtypeStruct((count, *cot.shape), bf16) for count in (len(FIRST) + 1, len(SECOND))],
        (places, tokens, cot),
        [DMAS((9,))],
        traffic=4,
    )


def block_of(tokens, place, width):
    return tokens[:, pl.ds(pl.multiple_of(place * width, width), width)]


def partner_block(par, b):
    first, second = par
    return first[FIRST.index(b)] if b in FIRST else second[SECOND.index(b)]


def partial(b, places, tokens, cot, *par):
    own = block_of(tokens, places[b], cot.shape[1])
    return dot(own, cot[...], 0, 0) + dot(partner_block(par, b), par[0][len(FIRST)], 0, 0)


ROWS = [INDEX] + [WHOLE] * 4


def far_kernel(*refs):
    *rows, top, bottom = refs
    half = top.shape[1]
    for i, b in enumerate((6, 2)):
        block = partial(b, *rows)
        top[i] = block[:half].astype(bf16)
        bottom[i] = block[half:].astype(bf16)


def far_partials(*rows):
    width = rows[2].shape[1]
    return call(
        far_kernel,
        "far_partials",
        ROWS,
        [WHOLE] * 2,
        [jax.ShapeDtypeStruct((2, width // 2, width), bf16)] * 2,
        rows,
        traffic=5,
    )


def relay_kernel(part, *refs):
    rows, (top, bottom), outs = refs[:5], refs[5:7], refs[7:]
    plus, minus = outs[: len(outs) // 2], outs[len(outs) // 2 :]
    half = top.shape[1]
    for k, pieces, arrived, at in ((1, plus, top, 0), (3, minus, bottom, half)):
        block = partial(4 - 4 * part + k, *rows)
        row = 0
        for piece in pieces:
            count = piece.shape[0]
            low, high = max(row, at), min(row + count, at + half)
            if row < low:
                piece[: min(low - row, count)] = block[row : min(low, row + count)].astype(bf16)
            if low < high:
                mine = arrived[part, low - at : high - at].astype(f32)
                piece[low - row : high - row] = (block[low:high] + mine).astype(bf16)
            if max(high, row) < row + count and low < row + count:
                start = max(high, row)
                piece[start - row :] = block[start : row + count].astype(bf16)
            row += count


def relay(rows, top, bottom, part, cuts):
    width = rows[2].shape[1]
    return call(
        lambda *refs: relay_kernel(part, *refs),
        "relay",
        ROWS + [WHOLE] * 2,
        [WHOLE] * (2 * len(cuts)),
        [jax.ShapeDtypeStruct((count, width), bf16) for count in cuts] * 2,
        (*rows, top, bottom),
        traffic=5,
    )


def closing_kernel(part, *refs):
    rows, arrived, out = refs[:5], refs[5:-1], refs[-1]
    total = partial(4 - 4 * part, *rows)
    if part:
        total += arrived[0][...].astype(f32)
        arrived = arrived[1:]
    row = 0
    for left, right in zip(arrived[::2], arrived[1::2]):
        at = slice(row, row + left.shape[0])
        out[at] = (total[at] + left[...].astype(f32) + right[...].astype(f32)).astype(out.dtype)
        row += left.shape[0]


def closing(rows, arrived, part, dtype):
    width = rows[2].shape[1]
    return call(
        lambda *refs: closing_kernel(part, *refs),
        "closing",
        ROWS + [WHOLE] * len(arrived),
        WHOLE,
        jax.ShapeDtypeStruct((width, width), dtype),
        (*rows, *arrived),
        traffic=4,
    )


def apply_kernel(part, *refs):
    rows, (w0, w1, w2a, w2b, w3), rest = refs[:5], refs[5:10], refs[10:]
    places, tokens, cot, *par = rows
    if part:
        v_own_in, v_par_in, _, v_own, grad, *back, ready, sems = rest
    else:
        v_own, v_par, grad, *back, ready, sems = rest
    par_cot = par[0].at[len(FIRST)]
    width = cot.shape[1]
    half = w2a.shape[0]
    copies = []
    sums = [v_own_in[...], v_par_in[...]] if part else [0.0, 0.0]
    for k, w in enumerate((w0, w1, None, w3)):
        pieces = [(w, slice(0, width))] if k != 2 else [(w2a, slice(0, half)), (w2b, slice(half, width))]
        b = 4 * part + k
        blocks = (block_of(tokens, places[b], width), partner_block(par, b))
        for n, block in enumerate(blocks):
            sums[n] += sum(dot(block[:, s], p[...], 1, 0) for p, s in pieces)
        for p, s in pieces:
            ready[k, :, s] = dot(cot[...], p[...], 1, 1).astype(bf16)
            returned = dot(par_cot[...], p[...], 1, 1).astype(bf16)
            if part:
                back[k][: returned.shape[0], s] = returned
            else:
                back[k // 2][k % 2, :, s] = returned
        copy = pltpu.make_async_copy(ready.at[k], columns(grad, places[b], width), sems.at[k])
        copy.start()
        copies.append(copy)
    v_own[...] = sums[0]
    if part:
        rows_each = cot.shape[0] // 4
        for k in range(4):
            back[k][cot.shape[0] :] = sums[1][k * rows_each : (k + 1) * rows_each].astype(bf16)
    else:
        v_par[...] = sums[1]
    for copy in copies:
        copy.wait()


def apply_weight(rows, pieces, carry, part):
    tokens, cot = rows[1:3]
    operands = (*rows, *pieces, *carry)
    total = jax.ShapeDtypeStruct(cot.shape, f32)
    whole = jax.ShapeDtypeStruct(tokens.shape, bf16)
    count, width = cot.shape
    shapes = [(count + count // 4, width)] * 4 if part else [(2, count, width)] * 2
    back = [jax.ShapeDtypeStruct(shape, bf16) for shape in shapes]
    return call(
        lambda *refs: apply_kernel(part, *refs),
        "apply_weight",
        ROWS + [WHOLE] * 5 + ([WHOLE, WHOLE, FAR] if part else []),
        [WHOLE] * (2 - part) + [FAR] + [WHOLE] * len(back),
        [total] * (2 - part) + [whole] + back,
        operands,
        [pltpu.VMEM((4, *cot.shape), bf16), DMAS((4,))],
        {len(operands) - 1: 1} if part else {},
        traffic=4,
    )


def place_kernel(part, places, *rest):
    if part:
        *blocks, v_own, _, out, values, sems = rest
        count = v_own.shape[0]
        sources = [block.at[pl.ds(0, count)] for block in blocks]
    else:
        *blocks, _, out, sems = rest
        sources = [block.at[k] for block in blocks for k in range(2)]
    width = sources[0].shape[-1]
    copies = [
        pltpu.make_async_copy(source, columns(out, places[4 * part + k], width), sems.at[k])
        for k, source in enumerate(sources)
    ]
    for copy in copies:
        copy.start()
    if part:
        for k, block in enumerate(blocks):
            at = slice(k * count // 4, (k + 1) * count // 4)
            values[at] = (v_own[at] + block[count:].astype(f32)).astype(bf16)
    for copy in copies:
        copy.wait()


def place(places, blocks, whole, v_own, part):
    operands = (places, *blocks, v_own, whole) if part else (places, *blocks, whole)
    out = jax.ShapeDtypeStruct(whole.shape, bf16)
    return call(
        lambda *refs: place_kernel(part, *refs),
        "place",
        [INDEX] + [WHOLE] * (len(operands) - 2) + [FAR],
        [FAR, WHOLE] if part else FAR,
        [out, jax.ShapeDtypeStruct(v_own.shape, bf16)] if part else out,
        operands,
        [DMAS((4,))],
        {len(operands) - 1: 0},
        traffic=5,
    )


def partner(part, bits):
    return lax.ppermute(part, "replica", [(i, i ^ bits) for i in range(16)])


def outer_kernel(fragment, delta, moment, whole, local, new_global, new_moment, new_local):
    averaged = delta[...] / 16.0
    moment_next = momentum_decay * moment[0] + averaged
    global_next = whole[0] - outer_rate * (averaged + momentum_decay * moment_next)
    new_moment[...] = moment_next
    new_global[...] = global_next
    new_local[0] = mix_weight * local[0, 0] + (1.0 - mix_weight) * global_next


def outer_step(fragment, delta, moment, whole, local):
    rows, width = delta.shape
    flat = pl.BlockSpec((rows, width), lambda i, f: (0, 0))
    chosen = pl.BlockSpec((1, rows, width), lambda i, f: (f[0], 0, 0))
    return pl.pallas_call(
        outer_kernel,
        grid_spec=pltpu.PrefetchScalarGridSpec(
            num_scalar_prefetch=1,
            grid=(1,),
            in_specs=[flat, chosen, chosen, pl.BlockSpec((1, 1, rows, width), lambda i, f: (0, f[0], 0, 0))],
            out_specs=[flat, flat, pl.BlockSpec((1, rows, width), lambda i, f: (0, 0, 0))],
        ),
        out_shape=[jax.ShapeDtypeStruct((rows, width), f32)] * 2 + [jax.ShapeDtypeStruct((1, rows, width), f32)],
        compiler_params=pltpu.CompilerParams(vmem_limit_bytes=8 * 1024 * 1024),
        cost_estimate=pl.CostEstimate(flops=0, bytes_accessed=1024 * 1024, transcendentals=0),
        name="outer_step",
    )(fragment, delta, moment, whole, local)


def hold_kernel(places, _, out):
    for b in range(8):
        out[b] = places[b]


def hold(places, array, traffic):
    return call(
        hold_kernel,
        "hold",
        [INDEX, FAR],
        INDEX,
        jax.ShapeDtypeStruct(places.shape, places.dtype),
        (places, array),
        traffic=traffic,
    )


def body(
    tokens, cotangent, w_value, outer_global, outer_momentum, local_params, outer_delta, fragment
):
    me = lax.axis_index("fsdp")
    core, x, z = lax.rem(me, NC), lax.rem(me // NC, NX), me // (NC * NX)
    steps = jnp.arange(8, dtype=jnp.int32)
    chips = lax.rem(z + steps // NX, NZ) * NX + lax.rem(x + steps, NX)
    own = chips * NC + core
    other = chips * NC + (1 - core)

    shard = w_value[0]
    width = shard.shape[1]
    half = shard.shape[0] // 2
    par = [send(piece, OTHER_CORE) for piece in select(other, tokens, cotangent)]
    behind, ahead = send(shard, PLUS), send(shard, MINUS)
    shard_across = send(shard, ACROSS)

    rows = (own, tokens, cotangent, *par)
    top, bottom = far_partials(*rows)
    delta = after(outer_delta[0], top)
    delta = delta + partner(delta, 1)
    top, bottom = send(top, PLUS), send(bottom, MINUS)
    far_top = send(after(behind[:half], delta), PLUS)
    far_bottom = send(after(ahead[half:], delta), MINUS)

    across_in = hold(own, shard_across, HOLD)
    top, bottom, far_top, far_bottom = lax.optimization_barrier((top, bottom, far_top, far_bottom))
    plus, minus = relay((across_in, *rows[1:]), top, bottom, 0, (width,))
    from_left, from_right = send(plus, PLUS), send(minus, MINUS)
    delta = after(delta, plus)
    delta = sum((partner(delta, bits) for bits in (4, 8, 12)), delta)
    pieces = (shard, ahead, after(far_top, delta), far_bottom, behind)
    v_own, v_par, grad, *back = apply_weight(rows, pieces, (), 0)
    back = [send(piece, OTHER_CORE) for piece in back]

    shard_across = after(shard_across, from_left, from_right, v_own, across_in)
    behind, ahead = send(shard_across, PLUS), send(shard_across, MINUS)
    across = closing((across_in, *rows[1:]), (from_left, from_right), 0, bf16)
    from_across = send(across, ACROSS)
    delta = delta + partner(after(delta, v_own), 2)
    plus, plus_late, minus, minus_late = relay(rows, after(top, across), bottom, 1, (CUT, width - CUT))
    grad = place(other, back, grad, None, 0)

    far_top, far_bottom = send(behind[:half], PLUS), send(ahead[half:], MINUS)
    left, right = send(after(plus, behind), PLUS), send(after(minus, ahead, grad), MINUS)
    pieces = (shard_across, ahead, far_top, far_bottom, behind)
    v_own, grad, *back = apply_weight(rows, pieces, (v_own, v_par, grad), 1)
    everything = (v_own, from_across, delta, left, right)
    left_late = send(after(plus_late, *everything), PLUS)
    right_late = send(after(minus_late, *everything), MINUS)
    back = [send(piece, OTHER_CORE) for piece in back]
    grad, values = place(other, back, grad, v_own, 1)
    rows = (after(own, grad, values), *rows[1:])
    grad_weight = closing(rows, (from_across, left, right, left_late, right_late), 1, f32)

    new_global, new_momentum, new_local = outer_step(
        fragment, delta, outer_momentum, outer_global, local_params
    )
    return (values, grad, grad_weight[None], new_global, new_momentum, new_local)


def solution(mesh):
    in_specs = (
        P(("replica", "fsdp"), None),
        P(("replica", "fsdp"), None),
        P("replica", "fsdp", None),
        P(None, "fsdp", None),
        P(None, "fsdp", None),
        P("replica", None, "fsdp", None),
        P("replica", "fsdp", None),
        P(),
    )
    out_specs = (
        P(("replica", "fsdp"), None),
        P(("replica", "fsdp"), None),
        P("replica", "fsdp", None),
        P("fsdp", None),
        P("fsdp", None),
        P("replica", "fsdp", None),
    )
    return jax.shard_map(body, mesh=mesh, in_specs=in_specs, out_specs=out_specs, check_vma=False)
```

time: 352 us -> 107 us (0.30)
  waiting for transfers between devices: 230 us -> 34.1 us
  blocking collectives: 83.3 us -> 0 us
  starting transfers between devices: 0.08 us -> 47.5 us
  matrix products: 21.2 us -> 0 us
  Pallas kernels: 0 us -> 20.4 us
  between operations: 14.7 us -> 1.63 us
    reduce_scatter x1 -> x0, waiting for transfers between devices: 211 us -> none  [body(): lax.psum_scatter(lax.dot_general(tokens, cotangent, (((0,), (0,)), ((), (...]
    psum x1 -> x0, blocking collectives: 83.3 us -> none  [body(): lax.psum(outer_delta[0].astype(jnp.bfloat16), 'replica').astype(jnp.float32)]
    ppermute x0 -> x31, starting transfers between devices: none -> 47.5 us  [the longest x26 37.7 us: send(): return lax.ppermute(array, 'fsdp', pairs)]
    ppermute x0 -> x31, waiting for transfers between devices: none -> 34.1 us  [the longest x26 24.2 us: send(): return lax.ppermute(array, 'fsdp', pairs)]
    dot_general x3 -> x0, matrix products: 21.2 us -> none  [the longest x1 10.3 us: body(): lax.dot_general(tokens, cotangent, (((0,), (0,)), ((), ())), preferred_el...]
    pallas_call x0 -> x12, Pallas kernels: none -> 20.4 us  [the longest x11 19.7 us: call(): pl.pallas_call(kernel, in_specs=in_specs, out_specs=out_specs, out_shape=...]
    all_gather x1 -> x0, waiting for transfers between devices: 18 us -> none  [body(): whole_weight = lax.all_gather(w_value[0], 'fsdp', axis=0, tiled=True)]
  transfers between devices with their start and end apart: 2 -> 31, of which waited for: 2 -> 14; matrix products, arithmetic and copies ran while one was open for 7% -> 0% of each run, Pallas kernels for 0% -> 15%
where the time goes in v2:
time: 107 us
  starting transfers between devices  47.5 us (44%)
  waiting for transfers between devices  34.1 us (32%)
  Pallas kernels  20.4 us (19%)
  local copies, waits for them, and re-layouts  3.24 us (3%)
  between operations  1.63 us (2%)
    ppermute x26, starting transfers between devices, send(): return lax.ppermute(array, 'fsdp', pairs)  37.7 us
    ppermute x26, waiting for transfers between devices, send(): return lax.ppermute(array, 'fsdp', pairs)  24.2 us
    pallas_call x11, Pallas kernels, call(): pl.pallas_call(kernel, in_specs=in_specs, out_specs=out_specs, out_shape=...  19.7 us
    ppermute x5, waiting for transfers between devices, partner(): return lax.ppermute(part, 'replica', [(i, i ^ bits) for i in range(16)])  9.94 us
    ppermute x5, starting transfers between devices, partner(): return lax.ppermute(part, 'replica', [(i, i ^ bits) for i in range(16)])  9.85 us
    unnamed x18, local copies, waits for them, and re-layouts  3.16 us
  transfers between devices with their start and end apart: 31, of which 14 were waited for; matrix products, arithmetic and copies ran while one was open for 0% of the time, Pallas kernels for 15%

profile of v2, /device:TPU:8, one launch (start us, length us, event | category | flops | bytes accessed | tf_op | source)
XLA Modules:
  0.0 107.0 jit_solution(17706521851637220599)
XLA Ops:
  0.7 2.2 %copy-done = bf16[256,8192]{1,0:T(8,128)(2,1)S(1)} copy-done((bf16[256,8192]{1,0:T(8,128)(2,1)S(1)}, bf16[256,8192]{1,0:T(8,128)(2,1)}, u32[]{:S(2)}) %copy-start) | copy-done | bytes 4194328
  5.3 2.8 %collective-permute-start.8 = (bf16[512,512]{1,0:T(8,128)(2,1)}, bf16[512,512]{1,0:T(8,128)(2,1)S(1)}, u32[]{:S(2)}, u32[]{:S(2)}) collective-permute-start(bf16[512,512]{1,0:T(8,128)(2,1)} %bitcast.3), channel_id=1, source_target_pairs={{0,6},{1,7},{2,0},{3,1},{4,2},{5,3},{6,4},{7,5},{8,14},{9,15},{10,... | collective-permute-start | bytes 1572872 | tf_op jit(solution)/shard_map/ppermute | solution.py:37
  8.0 7.2 %collective-permute-start.2 = (bf16[512,512]{1,0:T(8,128)(2,1)}, bf16[512,512]{1,0:T(8,128)(2,1)S(1)}, u32[]{:S(2)}, u32[]{:S(2)}) collective-permute-start(bf16[512,512]{1,0:T(8,128)(2,1)} %bitcast.5), channel_id=1, source_target_pairs={{0,8},{1,9},{2,10},{3,11},{4,12},{5,13},{6,14},{7,15},{8,0},{9,1},... | collective-permute-start | bytes 1572872 | tf_op jit(solution)/shard_map/ppermute | solution.py:37
  17.4 2.6 %collective-permute-start.4 = (bf16[2,256,512]{2,1,0:T(8,128)(2,1)S(1)}, bf16[2,256,512]{2,1,0:T(8,128)(2,1)S(1)}, u32[]{:S(2)}, u32[]{:S(2)}) collective-permute-start(bf16[2,256,512]{2,1,0:T(8,128)(2,1)S(1)} %get-tuple-element.52), channel_id=1, source_target_pairs={{0,6},{1,7},{2,0},{3,1},{4,2},{5,3},{6,4},{7,5},{8,14},{9,15},{10,... | collective-permute-start | bytes 1572872 | tf_op jit(solution)/shard_map/ppermute | solution.py:37
  20.1 2.4 %collective-permute-start.6 = (f32[16,1024]{1,0:T(8,128)S(1)}, f32[16,1024]{1,0:T(8,128)S(1)}, u32[]{:S(2)}, u32[]{:S(2)}) collective-permute-start(f32[16,1024]{1,0:T(8,128)S(1)} %bitcast.8), channel_id=1, source_target_pairs={{0,16},{16,0},{32,48},{48,32},{64,80},{80,64},{96,112},{112,96},{1... | collective-permute-start | bytes 196616 | tf_op jit(solution)/shard_map/ppermute | solution.py:293
  22.5 1.8 %collective-permute-done.5.refs_9_ = bf16[512,512]{1,0:T(8,128)(2,1)S(1)} collective-permute-done((bf16[512,512]{1,0:T(8,128)(2,1)}, bf16[512,512]{1,0:T(8,128)(2,1)S(1)}, u32[]{:S(2)}, u32[]{:S(2)}) %collective-permute-start.5) | collective-permute-done | bytes 524320 | tf_op jit(solution)/shard_map/ppermute | solution.py:37
  24.7 3.3 %collective-permute-start.9 = (bf16[256,512]{1,0:T(8,128)(2,1)S(1)}, bf16[256,512]{1,0:T(8,128)(2,1)S(1)}, u32[]{:S(2)}, u32[]{:S(2)}) collective-permute-start(bf16[256,512]{1,0:T(8,128)(2,1)S(1)} %slice.17), channel_id=1, source_target_pairs={{0,6},{1,7},{2,0},{3,1},{4,2},{5,3},{6,4},{7,5},{8,14},{9,15},{10,... | collective-permute-start | bytes 786440 | tf_op jit(solution)/shard_map/ppermute | solution.py:37
  28.0 1.6 %collective-permute-done.2._.refs_5_ = bf16[512,512]{1,0:T(8,128)(2,1)S(1)} collective-permute-done((bf16[512,512]{1,0:T(8,128)(2,1)}, bf16[512,512]{1,0:T(8,128)(2,1)S(1)}, u32[]{:S(2)}, u32[]{:S(2)}) %collective-permute-start.2) | collective-permute-done | bytes 524320 | tf_op jit(solution)/shard_map/ppermute | solution.py:37
  30.8 5.7 %collective-permute-done.9.refs_8_ = bf16[256,512]{1,0:T(8,128)(2,1)S(1)} collective-permute-done((bf16[256,512]{1,0:T(8,128)(2,1)S(1)}, bf16[256,512]{1,0:T(8,128)(2,1)S(1)}, u32[]{:S(2)}, u32[]{:S(2)}) %collective-permute-start.9) | collective-permute-done | bytes 262176 | tf_op jit(solution)/shard_map/ppermute | solution.py:37
  36.5 3.4 %collective-permute-done.7.refs_7_ = bf16[256,512]{1,0:T(8,128)(2,1)S(1)} collective-permute-done((bf16[256,512]{1,0:T(8,128)(2,1)S(1)}, bf16[256,512]{1,0:T(8,128)(2,1)S(1)}, u32[]{:S(2)}, u32[]{:S(2)}) %collective-permute-start.7) | collective-permute-done | bytes 262176 | tf_op jit(solution)/shard_map/ppermute | solution.py:37
  41.3 3.2 %collective-permute-start.11 = (bf16[512,512]{1,0:T(8,128)(2,1)S(1)}, bf16[512,512]{1,0:T(8,128)(2,1)S(1)}, u32[]{:S(2)}, u32[]{:S(2)}) collective-permute-start(bf16[512,512]{1,0:T(8,128)(2,1)S(1)} %get-tuple-element.59), channel_id=1, source_target_pairs={{0,6},{1,7},{2,0},{3,1},{4,2},{5,3},{6,4},{7,5},{8,14},{9,15},{10,... | collective-permute-start | bytes 1572872 | tf_op jit(solution)/shard_map/ppermute | solution.py:37
  44.6 1.9 %collective-permute-start.12 = (f32[16,1024]{1,0:T(8,128)S(1)}, f32[16,1024]{1,0:T(8,128)S(1)}, u32[]{:S(2)}, u32[]{:S(2)}) collective-permute-start(f32[16,1024]{1,0:T(8,128)S(1)} %add.54), channel_id=1, source_target_pairs={{0,64},{16,80},{32,96},{48,112},{64,0},{80,16},{96,32},{112,48},{1... | collective-permute-start | bytes 196616 | tf_op jit(solution)/shard_map/ppermute | solution.py:293
  46.5 3.3 %collective-permute-start.13 = (f32[16,1024]{1,0:T(8,128)S(1)}, f32[16,1024]{1,0:T(8,128)S(1)}, u32[]{:S(2)}, u32[]{:S(2)}) collective-permute-start(f32[16,1024]{1,0:T(8,128)S(1)} %add.54), channel_id=1, source_target_pairs={{0,128},{16,144},{32,160},{48,176},{64,192},{80,208},{96,224},{112... | collective-permute-start | bytes 196616 | tf_op jit(solution)/shard_map/ppermute | solution.py:293
  49.8 3.6 %collective-permute-done.13 = f32[16,1024]{1,0:T(8,128)S(1)} collective-permute-done((f32[16,1024]{1,0:T(8,128)S(1)}, f32[16,1024]{1,0:T(8,128)S(1)}, u32[]{:S(2)}, u32[]{:S(2)}) %collective-permute-start.13) | collective-permute-done | bytes 65568 | tf_op jit(solution)/shard_map/ppermute | solution.py:293
  53.4 2.4 %collective-permute-done.14 = f32[16,1024]{1,0:T(8,128)S(1)} collective-permute-done((f32[16,1024]{1,0:T(8,128)S(1)}, f32[16,1024]{1,0:T(8,128)S(1)}, u32[]{:S(2)}, u32[]{:S(2)}) %collective-permute-start.14) | collective-permute-done | bytes 65568 | tf_op jit(solution)/shard_map/ppermute | solution.py:293
  55.8 3.5 %apply_weight.2 = (f32[256,512]{1,0:T(8,128)S(1)}, f32[256,512]{1,0:T(8,128)S(1)}, bf16[256,8192]{1,0:T(8,128)(2,1)}, bf16[2,256,512]{2,1,0:T(8,128)(2,1)S(1)}, bf16[2,256,512]{2,1,0:T(8,128)(2,1)S(1)}) custom-call(s32[8]{0:T(128)S(1)} %broadcast_add_fusion.places.refs_0_, bf16[256,8192]{1,0:T(8,128)(2,1)S(1)} %copy-done.1, bf16[256,512]{1,0:T(8,128)(2,1)S(1)} %copy-done.3, ...), custom_call_target="tpu_custom_call" | custom-call | bytes 4194304 | tf_op jit(solution)/shard_map/apply_weight/pallas_call | solution.py:45
  59.5 3.2 %collective-permute-start.15 = (bf16[512,512]{1,0:T(8,128)(2,1)S(1)}, bf16[512,512]{1,0:T(8,128)(2,1)S(1)}, u32[]{:S(2)}, u32[]{:S(2)}) collective-permute-start(bf16[512,512]{1,0:T(8,128)(2,1)S(1)} %collective-permute-done.2._.refs_5_), channel_id=1, source_target_pairs={{0,6},{1,7},{2,0},{3,1},{4,2},{5,3},{6,4},{7,5},{8,14},{9,15},{10,... | collective-permute-start | bytes 1572872 | tf_op jit(solution)/shard_map/ppermute | solution.py:37
  64.2 4.6 %collective-permute-start.25 = (bf16[512,512]{1,0:T(8,128)(2,1)S(1)}, bf16[512,512]{1,0:T(8,128)(2,1)S(1)}, u32[]{:S(2)}, u32[]{:S(2)}) collective-permute-start(bf16[512,512]{1,0:T(8,128)(2,1)S(1)} %closing.2), channel_id=1, source_target_pairs={{0,8},{1,9},{2,10},{3,11},{4,12},{5,13},{6,14},{7,15},{8,0},{9,1},... | collective-permute-start | bytes 1572872 | tf_op jit(solution)/shard_map/ppermute | solution.py:37
  68.9 2.7 %collective-permute-done.16.refs_9_ = bf16[512,512]{1,0:T(8,128)(2,1)S(1)} collective-permute-done((bf16[512,512]{1,0:T(8,128)(2,1)S(1)}, bf16[512,512]{1,0:T(8,128)(2,1)S(1)}, u32[]{:S(2)}, u32[]{:S(2)}) %collective-permute-start.16) | collective-permute-done | bytes 524320 | tf_op jit(solution)/shard_map/ppermute | solution.py:37
  71.7 3.3 %collective-permute-start.18 = (bf16[256,512]{1,0:T(8,128)(2,1)S(1)}, bf16[256,512]{1,0:T(8,128)(2,1)S(1)}, u32[]{:S(2)}, u32[]{:S(2)}) collective-permute-start(bf16[256,512]{1,0:T(8,128)(2,1)S(1)} %slice.19), channel_id=1, source_target_pairs={{0,6},{1,7},{2,0},{3,1},{4,2},{5,3},{6,4},{7,5},{8,14},{9,15},{10,... | collective-permute-start | bytes 786440 | tf_op jit(solution)/shard_map/ppermute | solution.py:37
  76.3 1.5 %place.2.refs_12_ = bf16[256,8192]{1,0:T(8,128)(2,1)} custom-call(s32[8]{0:T(128)S(1)} %broadcast_add_fusion.1.places.refs_0_, bf16[2,256,512]{2,1,0:T(8,128)(2,1)S(1)} %collective-permute-done.19.refs_1_, bf16[2,256,512]{2,1,0:T(8,128)(2,1)S(1)} %collective-permute-done.20.refs_2_, ...), custom_call_target="tpu_custom_call", output_to_operand_aliasing={{}: (3, {})} | custom-call | bytes 5242880 | tf_op jit(solution)/shard_map/place/pallas_call | solution.py:45
  77.9 2.2 %collective-permute-done.17.refs_7_ = bf16[256,512]{1,0:T(8,128)(2,1)S(1)} collective-permute-done((bf16[256,512]{1,0:T(8,128)(2,1)S(1)}, bf16[256,512]{1,0:T(8,128)(2,1)S(1)}, u32[]{:S(2)}, u32[]{:S(2)}) %collective-permute-start.17) | collective-permute-done | bytes 262176 | tf_op jit(solution)/shard_map/ppermute | solution.py:37
  80.2 3.5 %apply_weight.3 = (f32[256,512]{1,0:T(8,128)S(1)}, bf16[256,8192]{1,0:T(8,128)(2,1)}, bf16[320,512]{1,0:T(8,128)(2,1)S(1)}, bf16[320,512]{1,0:T(8,128)(2,1)S(1)}...) custom-call(s32[8]{0:T(128)S(1)} %broadcast_add_fusion.places.refs_0_, ...), custom_call_target="tpu_custom_call", output_to_operand_aliasing={{1}: (12, {})} | custom-call | bytes 4194304 | tf_op jit(solution)/shard_map/apply_weight/pallas_call | solution.py:45
  83.8 2.5 %collective-permute-start.27 = (bf16[256,512]{1,0:T(8,128)(2,1)S(1)}, bf16[256,512]{1,0:T(8,128)(2,1)S(1)}, u32[]{:S(2)}, u32[]{:S(2)}) collective-permute-start(bf16[256,512]{1,0:T(8,128)(2,1)S(1)} %get-tuple-element.83), channel_id=1, source_target_pairs={{0,6},{1,7},{2,0},{3,1},{4,2},{5,3},{6,4},{7,5},{8,14},{9,15},{10,... | collective-permute-start | bytes 786440 | tf_op jit(solution)/shard_map/ppermute | solution.py:37
  86.2 2.3 %collective-permute-start.28 = (f32[16,1024]{1,0:T(8,128)S(1)}, f32[16,1024]{1,0:T(8,128)S(1)}, u32[]{:S(2)}, u32[]{:S(2)}) collective-permute-start(f32[16,1024]{1,0:T(8,128)S(1)} %add_add_fusion), channel_id=1, source_target_pairs={{0,32},{16,48},{32,0},{48,16},{64,96},{80,112},{96,64},{112,80},{1... | collective-permute-start | bytes 196616 | tf_op jit(solution)/shard_map/ppermute | solution.py:293
  88.5 3.5 %collective-permute-done.28 = f32[16,1024]{1,0:T(8,128)S(1)} collective-permute-done((f32[16,1024]{1,0:T(8,128)S(1)}, f32[16,1024]{1,0:T(8,128)S(1)}, u32[]{:S(2)}, u32[]{:S(2)}) %collective-permute-start.28) | collective-permute-done | bytes 65568 | tf_op jit(solution)/shard_map/ppermute | solution.py:293
  92.0 1.5 %collective-permute-done.25.refs_5_ = bf16[512,512]{1,0:T(8,128)(2,1)S(1)} collective-permute-done((bf16[512,512]{1,0:T(8,128)(2,1)S(1)}, bf16[512,512]{1,0:T(8,128)(2,1)S(1)}, u32[]{:S(2)}, u32[]{:S(2)}) %collective-permute-start.25) | collective-permute-done | bytes 524320 | tf_op jit(solution)/shard_map/ppermute | solution.py:37
  94.0 2.1 %collective-permute-start.30 = (bf16[256,512]{1,0:T(8,128)(2,1)S(1)}, bf16[256,512]{1,0:T(8,128)(2,1)S(1)}, u32[]{:S(2)}, u32[]{:S(2)}) collective-permute-start(bf16[256,512]{1,0:T(8,128)(2,1)S(1)} %get-tuple-element.88), channel_id=1, source_target_pairs={{0,6},{1,7},{2,0},{3,1},{4,2},{5,3},{6,4},{7,5},{8,14},{9,15},{10,... | collective-permute-start | bytes 786440 | tf_op jit(solution)/shard_map/ppermute | solution.py:37
  97.5 2.2 %place.3 = (bf16[256,8192]{1,0:T(8,128)(2,1)}, bf16[256,512]{1,0:T(8,128)(2,1)}) custom-call(s32[8]{0:T(128)S(1)} %broadcast_add_fusion.1.places.refs_0_, bf16[320,512]{1,0:T(8,128)(2,1)S(1)} %collective-permute-done.21.refs_1_, bf16[320,512]{1,0:T(8,128)(2,1)S(1)} %collective-permute-done.22.refs_2_, ...), custom_call_target="tpu_custom_call", output_to_operand_aliasing={{0}: (6, {})} | custom-call | bytes 5242880 | tf_op jit(solution)/shard_map/place/pallas_call | solution.py:45
  99.8 2.5 %collective-permute-done.30.refs_9_ = bf16[256,512]{1,0:T(8,128)(2,1)S(1)} collective-permute-done((bf16[256,512]{1,0:T(8,128)(2,1)S(1)}, bf16[256,512]{1,0:T(8,128)(2,1)S(1)}, u32[]{:S(2)}, u32[]{:S(2)}) %collective-permute-start.30) | collective-permute-done | bytes 262176 | tf_op jit(solution)/shard_map/ppermute | solution.py:37
  102.3 2.6 %collective-permute-done.29.refs_8_ = bf16[256,512]{1,0:T(8,128)(2,1)S(1)} collective-permute-done((bf16[256,512]{1,0:T(8,128)(2,1)S(1)}, bf16[256,512]{1,0:T(8,128)(2,1)S(1)}, u32[]{:S(2)}, u32[]{:S(2)}) %collective-permute-start.29) | collective-permute-done | bytes 262176 | tf_op jit(solution)/shard_map/ppermute | solution.py:37
  104.9 2.1 %closing.3 = f32[512,512]{1,0:T(8,128)} custom-call(s32[8]{0:T(128)S(1)} %broadcast_add_fusion.places.refs_0_, bf16[256,8192]{1,0:T(8,128)(2,1)S(1)} %copy-done.1, bf16[256,512]{1,0:T(8,128)(2,1)S(1)} %copy-done.3, bf16[3,256,512]{2,1,0:T(8,128)(2,1)S(1)} %collective-permute-done.refs_3_, bf16[6,256,512]{2,1,0:T(8,128)(2,1)S(1)} %collective-permute-done.1.refs_4_, ...), custom_call_target="tpu_custom_call" | custom-call | bytes 4194304 | tf_op jit(solution)/shard_map/closing/pallas_call | solution.py:45
  (69 shorter events, 12.1 us)
Async XLA Ops:
  4.7 10.6 %collective-permute-start.1 = (bf16[6,256,512]{2,1,0:T(8,128)(2,1)S(1)}, bf16[6,256,512]{2,1,0:T(8,128)(2,1)S(1)}, u32[]{:S(2)}, u32[]{:S(2)}) collective-permute-start(bf16[6,256,512]{2,1,0:T(8,128)(2,1)S(1)} %get-tuple-element.50), channel_id=1, source_target_pairs={{0,1},{1,0},{2,3},{3,2},{4,5},{5,4},{6,7},{7,6},{8,9},{9,8},{10,11... | collective-permute-start | bytes 4718600 | tf_op jit(solution)/shard_map/ppermute | solution.py:37
  4.8 10.5 %collective-permute-start = (bf16[3,256,512]{2,1,0:T(8,128)(2,1)S(1)}, bf16[3,256,512]{2,1,0:T(8,128)(2,1)S(1)}, u32[]{:S(2)}, u32[]{:S(2)}) collective-permute-start(bf16[3,256,512]{2,1,0:T(8,128)(2,1)S(1)} %get-tuple-element.49), channel_id=1, source_target_pairs={{0,1},{1,0},{2,3},{3,2},{4,5},{5,4},{6,7},{7,6},{8,9},{9,8},{10,11... | collective-permute-start | bytes 2359304 | tf_op jit(solution)/shard_map/ppermute | solution.py:37
  5.3 14.8 %collective-permute-start.8 = (bf16[512,512]{1,0:T(8,128)(2,1)}, bf16[512,512]{1,0:T(8,128)(2,1)S(1)}, u32[]{:S(2)}, u32[]{:S(2)}) collective-permute-start(bf16[512,512]{1,0:T(8,128)(2,1)} %bitcast.3), channel_id=1, source_target_pairs={{0,6},{1,7},{2,0},{3,1},{4,2},{5,3},{6,4},{7,5},{8,14},{9,15},{10,... | collective-permute-start | bytes 1572872 | tf_op jit(solution)/shard_map/ppermute | solution.py:37
  8.0 16.2 %collective-permute-start.5 = (bf16[512,512]{1,0:T(8,128)(2,1)}, bf16[512,512]{1,0:T(8,128)(2,1)S(1)}, u32[]{:S(2)}, u32[]{:S(2)}) collective-permute-start(bf16[512,512]{1,0:T(8,128)(2,1)} %bitcast.4), channel_id=1, source_target_pairs={{0,2},{1,3},{2,4},{3,5},{4,6},{5,7},{6,0},{7,1},{8,10},{9,11},{10,... | collective-permute-start | bytes 1572872 | tf_op jit(solution)/shard_map/ppermute | solution.py:37
  8.0 21.6 %collective-permute-start.2 = (bf16[512,512]{1,0:T(8,128)(2,1)}, bf16[512,512]{1,0:T(8,128)(2,1)S(1)}, u32[]{:S(2)}, u32[]{:S(2)}) collective-permute-start(bf16[512,512]{1,0:T(8,128)(2,1)} %bitcast.5), channel_id=1, source_target_pairs={{0,8},{1,9},{2,10},{3,11},{4,12},{5,13},{6,14},{7,15},{8,0},{9,1},... | collective-permute-start | bytes 1572872 | tf_op jit(solution)/shard_map/ppermute | solution.py:37
  16.6 23.4 %collective-permute-start.3 = (bf16[2,256,512]{2,1,0:T(8,128)(2,1)S(1)}, bf16[2,256,512]{2,1,0:T(8,128)(2,1)S(1)}, u32[]{:S(2)}, u32[]{:S(2)}) collective-permute-start(bf16[2,256,512]{2,1,0:T(8,128)(2,1)S(1)} %get-tuple-element.51), channel_id=1, source_target_pairs={{0,2},{1,3},{2,4},{3,5},{4,6},{5,7},{6,0},{7,1},{8,10},{9,11},{10,... | collective-permute-start | bytes 1572872 | tf_op jit(solution)/shard_map/ppermute | solution.py:37
  17.4 22.6 %collective-permute-start.4 = (bf16[2,256,512]{2,1,0:T(8,128)(2,1)S(1)}, bf16[2,256,512]{2,1,0:T(8,128)(2,1)S(1)}, u32[]{:S(2)}, u32[]{:S(2)}) collective-permute-start(bf16[2,256,512]{2,1,0:T(8,128)(2,1)S(1)} %get-tuple-element.52), channel_id=1, source_target_pairs={{0,6},{1,7},{2,0},{3,1},{4,2},{5,3},{6,4},{7,5},{8,14},{9,15},{10,... | collective-permute-start | bytes 1572872 | tf_op jit(solution)/shard_map/ppermute | solution.py:37
  20.1 4.6 %collective-permute-start.6 = (f32[16,1024]{1,0:T(8,128)S(1)}, f32[16,1024]{1,0:T(8,128)S(1)}, u32[]{:S(2)}, u32[]{:S(2)}) collective-permute-start(f32[16,1024]{1,0:T(8,128)S(1)} %bitcast.8), channel_id=1, source_target_pairs={{0,16},{16,0},{32,48},{48,32},{64,80},{80,64},{96,112},{112,96},{1... | collective-permute-start | bytes 196616 | tf_op jit(solution)/shard_map/ppermute | solution.py:293
  24.7 11.8 %collective-permute-start.9 = (bf16[256,512]{1,0:T(8,128)(2,1)S(1)}, bf16[256,512]{1,0:T(8,128)(2,1)S(1)}, u32[]{:S(2)}, u32[]{:S(2)}) collective-permute-start(bf16[256,512]{1,0:T(8,128)(2,1)S(1)} %slice.17), channel_id=1, source_target_pairs={{0,6},{1,7},{2,0},{3,1},{4,2},{5,3},{6,4},{7,5},{8,14},{9,15},{10,... | collective-permute-start | bytes 786440 | tf_op jit(solution)/shard_map/ppermute | solution.py:37
  28.0 11.9 %collective-permute-start.7 = (bf16[256,512]{1,0:T(8,128)(2,1)S(1)}, bf16[256,512]{1,0:T(8,128)(2,1)S(1)}, u32[]{:S(2)}, u32[]{:S(2)}) collective-permute-start(bf16[256,512]{1,0:T(8,128)(2,1)S(1)} %slice.16), channel_id=1, source_target_pairs={{0,2},{1,3},{2,4},{3,5},{4,6},{5,7},{6,0},{7,1},{8,10},{9,11},{10,... | collective-permute-start | bytes 786440 | tf_op jit(solution)/shard_map/ppermute | solution.py:37
  30.8 25.0 %copy-start.4 = (bf16[1,512,512]{2,1,0:T(8,128)(2,1)S(1)}, bf16[1,512,512]{2,1,0:T(8,128)(2,1)}, u32[]{:S(2)}) copy-start(bf16[1,512,512]{2,1,0:T(8,128)(2,1)} %param.10) | copy-start | bytes 1572868
  41.2 18.1 %collective-permute-start.10 = (bf16[512,512]{1,0:T(8,128)(2,1)S(1)}, bf16[512,512]{1,0:T(8,128)(2,1)S(1)}, u32[]{:S(2)}, u32[]{:S(2)}) collective-permute-start(bf16[512,512]{1,0:T(8,128)(2,1)S(1)} %get-tuple-element.58), channel_id=1, source_target_pairs={{0,2},{1,3},{2,4},{3,5},{4,6},{5,7},{6,0},{7,1},{8,10},{9,11},{10,... | collective-permute-start | bytes 1572872 | tf_op jit(solution)/shard_map/ppermute | solution.py:37
  41.3 18.0 %collective-permute-start.11 = (bf16[512,512]{1,0:T(8,128)(2,1)S(1)}, bf16[512,512]{1,0:T(8,128)(2,1)S(1)}, u32[]{:S(2)}, u32[]{:S(2)}) collective-permute-start(bf16[512,512]{1,0:T(8,128)(2,1)S(1)} %get-tuple-element.59), channel_id=1, source_target_pairs={{0,6},{1,7},{2,0},{3,1},{4,2},{5,3},{6,4},{7,5},{8,14},{9,15},{10,... | collective-permute-start | bytes 1572872 | tf_op jit(solution)/shard_map/ppermute | solution.py:37
  44.6 5.2 %collective-permute-start.12 = (f32[16,1024]{1,0:T(8,128)S(1)}, f32[16,1024]{1,0:T(8,128)S(1)}, u32[]{:S(2)}, u32[]{:S(2)}) collective-permute-start(f32[16,1024]{1,0:T(8,128)S(1)} %add.54), channel_id=1, source_target_pairs={{0,64},{16,80},{32,96},{48,112},{64,0},{80,16},{96,32},{112,48},{1... | collective-permute-start | bytes 196616 | tf_op jit(solution)/shard_map/ppermute | solution.py:293
  46.5 6.9 %collective-permute-start.13 = (f32[16,1024]{1,0:T(8,128)S(1)}, f32[16,1024]{1,0:T(8,128)S(1)}, u32[]{:S(2)}, u32[]{:S(2)}) collective-permute-start(f32[16,1024]{1,0:T(8,128)S(1)} %add.54), channel_id=1, source_target_pairs={{0,128},{16,144},{32,160},{48,176},{64,192},{80,208},{96,224},{112... | collective-permute-start | bytes 196616 | tf_op jit(solution)/shard_map/ppermute | solution.py:293
  49.7 6.1 %collective-permute-start.14 = (f32[16,1024]{1,0:T(8,128)S(1)}, f32[16,1024]{1,0:T(8,128)S(1)}, u32[]{:S(2)}, u32[]{:S(2)}) collective-permute-start(f32[16,1024]{1,0:T(8,128)S(1)} %add.54), channel_id=1, source_target_pairs={{0,192},{16,208},{32,224},{48,240},{64,128},{80,144},{96,160},{112... | collective-permute-start | bytes 196616 | tf_op jit(solution)/shard_map/ppermute | solution.py:293
  59.4 12.2 %collective-permute-start.16 = (bf16[512,512]{1,0:T(8,128)(2,1)S(1)}, bf16[512,512]{1,0:T(8,128)(2,1)S(1)}, u32[]{:S(2)}, u32[]{:S(2)}) collective-permute-start(bf16[512,512]{1,0:T(8,128)(2,1)S(1)} %collective-permute-done.2._.refs_5_), channel_id=1, source_target_pairs={{0,2},{1,3},{2,4},{3,5},{4,6},{5,7},{6,0},{7,1},{8,10},{9,11},{10,... | collective-permute-start | bytes 1572872 | tf_op jit(solution)/shard_map/ppermute | solution.py:37
  59.5 12.2 %collective-permute-start.15 = (bf16[512,512]{1,0:T(8,128)(2,1)S(1)}, bf16[512,512]{1,0:T(8,128)(2,1)S(1)}, u32[]{:S(2)}, u32[]{:S(2)}) collective-permute-start(bf16[512,512]{1,0:T(8,128)(2,1)S(1)} %collective-permute-done.2._.refs_5_), channel_id=1, source_target_pairs={{0,6},{1,7},{2,0},{3,1},{4,2},{5,3},{6,4},{7,5},{8,14},{9,15},{10,... | collective-permute-start | bytes 1572872 | tf_op jit(solution)/shard_map/ppermute | solution.py:37
  62.7 13.6 %collective-permute-start.19 = (bf16[2,256,512]{2,1,0:T(8,128)(2,1)S(1)}, bf16[2,256,512]{2,1,0:T(8,128)(2,1)S(1)}, u32[]{:S(2)}, u32[]{:S(2)}) collective-permute-start(bf16[2,256,512]{2,1,0:T(8,128)(2,1)S(1)} %get-tuple-element.67), channel_id=1, source_target_pairs={{0,1},{1,0},{2,3},{3,2},{4,5},{5,4},{6,7},{7,6},{8,9},{9,8},{10,11... | collective-permute-start | bytes 1572872 | tf_op jit(solution)/shard_map/ppermute | solution.py:37
  62.7 13.6 %collective-permute-start.20 = (bf16[2,256,512]{2,1,0:T(8,128)(2,1)S(1)}, bf16[2,256,512]{2,1,0:T(8,128)(2,1)S(1)}, u32[]{:S(2)}, u32[]{:S(2)}) collective-permute-start(bf16[2,256,512]{2,1,0:T(8,128)(2,1)S(1)} %get-tuple-element.68), channel_id=1, source_target_pairs={{0,1},{1,0},{2,3},{3,2},{4,5},{5,4},{6,7},{7,6},{8,9},{9,8},{10,11... | collective-permute-start | bytes 1572872 | tf_op jit(solution)/shard_map/ppermute | solution.py:37
  64.2 29.2 %collective-permute-start.25 = (bf16[512,512]{1,0:T(8,128)(2,1)S(1)}, bf16[512,512]{1,0:T(8,128)(2,1)S(1)}, u32[]{:S(2)}, u32[]{:S(2)}) collective-permute-start(bf16[512,512]{1,0:T(8,128)(2,1)S(1)} %closing.2), channel_id=1, source_target_pairs={{0,8},{1,9},{2,10},{3,11},{4,12},{5,13},{6,14},{7,15},{8,0},{9,1},... | collective-permute-start | bytes 1572872 | tf_op jit(solution)/shard_map/ppermute | solution.py:37
  71.6 8.6 %collective-permute-start.17 = (bf16[256,512]{1,0:T(8,128)(2,1)S(1)}, bf16[256,512]{1,0:T(8,128)(2,1)S(1)}, u32[]{:S(2)}, u32[]{:S(2)}) collective-permute-start(bf16[256,512]{1,0:T(8,128)(2,1)S(1)} %slice.18), channel_id=1, source_target_pairs={{0,2},{1,3},{2,4},{3,5},{4,6},{5,7},{6,0},{7,1},{8,10},{9,11},{10,... | collective-permute-start | bytes 786440 | tf_op jit(solution)/shard_map/ppermute | solution.py:37
  71.7 8.5 %collective-permute-start.18 = (bf16[256,512]{1,0:T(8,128)(2,1)S(1)}, bf16[256,512]{1,0:T(8,128)(2,1)S(1)}, u32[]{:S(2)}, u32[]{:S(2)}) collective-permute-start(bf16[256,512]{1,0:T(8,128)(2,1)S(1)} %slice.19), channel_id=1, source_target_pairs={{0,6},{1,7},{2,0},{3,1},{4,2},{5,3},{6,4},{7,5},{8,14},{9,15},{10,... | collective-permute-start | bytes 786440 | tf_op jit(solution)/shard_map/ppermute | solution.py:37
  77.8 15.6 %collective-permute-start.26 = (bf16[256,512]{1,0:T(8,128)(2,1)S(1)}, bf16[256,512]{1,0:T(8,128)(2,1)S(1)}, u32[]{:S(2)}, u32[]{:S(2)}) collective-permute-start(bf16[256,512]{1,0:T(8,128)(2,1)S(1)} %get-tuple-element.81), channel_id=1, source_target_pairs={{0,2},{1,3},{2,4},{3,5},{4,6},{5,7},{6,0},{7,1},{8,10},{9,11},{10,... | collective-permute-start | bytes 786440 | tf_op jit(solution)/shard_map/ppermute | solution.py:37
  83.7 12.4 %collective-permute-start.21 = (bf16[320,512]{1,0:T(8,128)(2,1)S(1)}, bf16[320,512]{1,0:T(8,128)(2,1)S(1)}, u32[]{:S(2)}, u32[]{:S(2)}) collective-permute-start(bf16[320,512]{1,0:T(8,128)(2,1)S(1)} %get-tuple-element.70), channel_id=1, source_target_pairs={{0,1},{1,0},{2,3},{3,2},{4,5},{5,4},{6,7},{7,6},{8,9},{9,8},{10,11... | collective-permute-start | bytes 983048 | tf_op jit(solution)/shard_map/ppermute | solution.py:37
  83.8 10.2 %collective-permute-start.27 = (bf16[256,512]{1,0:T(8,128)(2,1)S(1)}, bf16[256,512]{1,0:T(8,128)(2,1)S(1)}, u32[]{:S(2)}, u32[]{:S(2)}) collective-permute-start(bf16[256,512]{1,0:T(8,128)(2,1)S(1)} %get-tuple-element.83), channel_id=1, source_target_pairs={{0,6},{1,7},{2,0},{3,1},{4,2},{5,3},{6,4},{7,5},{8,14},{9,15},{10,... | collective-permute-start | bytes 786440 | tf_op jit(solution)/shard_map/ppermute | solution.py:37
  86.2 5.8 %collective-permute-start.28 = (f32[16,1024]{1,0:T(8,128)S(1)}, f32[16,1024]{1,0:T(8,128)S(1)}, u32[]{:S(2)}, u32[]{:S(2)}) collective-permute-start(f32[16,1024]{1,0:T(8,128)S(1)} %add_add_fusion), channel_id=1, source_target_pairs={{0,32},{16,48},{32,0},{48,16},{64,96},{80,112},{96,64},{112,80},{1... | collective-permute-start | bytes 196616 | tf_op jit(solution)/shard_map/ppermute | solution.py:293
  92.0 5.5 %collective-permute-start.22 = (bf16[320,512]{1,0:T(8,128)(2,1)S(1)}, bf16[320,512]{1,0:T(8,128)(2,1)S(1)}, u32[]{:S(2)}, u32[]{:S(2)}) collective-permute-start(bf16[320,512]{1,0:T(8,128)(2,1)S(1)} %get-tuple-element.71), channel_id=1, source_target_pairs={{0,1},{1,0},{2,3},{3,2},{4,5},{5,4},{6,7},{7,6},{8,9},{9,8},{10,11... | collective-permute-start | bytes 983048 | tf_op jit(solution)/shard_map/ppermute | solution.py:37
  93.5 4.0 %collective-permute-start.23 = (bf16[320,512]{1,0:T(8,128)(2,1)S(1)}, bf16[320,512]{1,0:T(8,128)(2,1)S(1)}, u32[]{:S(2)}, u32[]{:S(2)}) collective-permute-start(bf16[320,512]{1,0:T(8,128)(2,1)S(1)} %get-tuple-element.72), channel_id=1, source_target_pairs={{0,1},{1,0},{2,3},{3,2},{4,5},{5,4},{6,7},{7,6},{8,9},{9,8},{10,11... | collective-permute-start | bytes 983048 | tf_op jit(solution)/shard_map/ppermute | solution.py:37
  93.5 4.0 %collective-permute-start.24 = (bf16[320,512]{1,0:T(8,128)(2,1)S(1)}, bf16[320,512]{1,0:T(8,128)(2,1)S(1)}, u32[]{:S(2)}, u32[]{:S(2)}) collective-permute-start(bf16[320,512]{1,0:T(8,128)(2,1)S(1)} %get-tuple-element.73), channel_id=1, source_target_pairs={{0,1},{1,0},{2,3},{3,2},{4,5},{5,4},{6,7},{7,6},{8,9},{9,8},{10,11... | collective-permute-start | bytes 983048 | tf_op jit(solution)/shard_map/ppermute | solution.py:37
  94.0 8.3 %collective-permute-start.30 = (bf16[256,512]{1,0:T(8,128)(2,1)S(1)}, bf16[256,512]{1,0:T(8,128)(2,1)S(1)}, u32[]{:S(2)}, u32[]{:S(2)}) collective-permute-start(bf16[256,512]{1,0:T(8,128)(2,1)S(1)} %get-tuple-element.88), channel_id=1, source_target_pairs={{0,6},{1,7},{2,0},{3,1},{4,2},{5,3},{6,4},{7,5},{8,14},{9,15},{10,... | collective-permute-start | bytes 786440 | tf_op jit(solution)/shard_map/ppermute | solution.py:37
  96.1 8.8 %collective-permute-start.29 = (bf16[256,512]{1,0:T(8,128)(2,1)S(1)}, bf16[256,512]{1,0:T(8,128)(2,1)S(1)}, u32[]{:S(2)}, u32[]{:S(2)}) collective-permute-start(bf16[256,512]{1,0:T(8,128)(2,1)S(1)} %get-tuple-element.86), channel_id=1, source_target_pairs={{0,2},{1,3},{2,4},{3,5},{4,6},{5,7},{6,0},{7,1},{8,10},{9,11},{10,... | collective-permute-start | bytes 786440 | tf_op jit(solution)/shard_map/ppermute | solution.py:37
  (8 other events, 91.3 us)

commit v3 on v2

--- a/solution.py
+++ b/solution.py
@@ -165,28 +165,42 @@
 
 
 def closing_kernel(part, *refs):
-    rows, arrived, out = refs[:5], refs[5:-1], refs[-1]
+    *rows, left, right, out = refs
     total = partial(4 - 4 * part, *rows)
-    if part:
-        total += arrived[0][...].astype(f32)
-        arrived = arrived[1:]
-    row = 0
-    for left, right in zip(arrived[::2], arrived[1::2]):
-        at = slice(row, row + left.shape[0])
-        out[at] = (total[at] + left[...].astype(f32) + right[...].astype(f32)).astype(out.dtype)
-        row += left.shape[0]
-
-
-def closing(rows, arrived, part, dtype):
+    count = left.shape[0]
+    added = total[:count] + left[...].astype(f32) + right[...].astype(f32)
+    out[:count] = added.astype(out.dtype)
+    if count < out.shape[0]:
+        out[count:] = total[count:].astype(out.dtype)
+
+
+def closing(rows, left, right, part):
     width = rows[2].shape[1]
     return call(
         lambda *refs: closing_kernel(part, *refs),
         "closing",
-        ROWS + [WHOLE] * len(arrived),
+        ROWS + [WHOLE] * 2,
         WHOLE,
-        jax.ShapeDtypeStruct((width, width), dtype),
-        (*rows, *arrived),
+        jax.ShapeDtypeStruct((width, width), f32 if part else bf16),
+        (*rows, left, right),
         traffic=4,
+    )
+
+
+def finish_kernel(total, across, left, right, out):
+    out[:CUT] = total[:CUT] + across[:CUT].astype(f32)
+    late = left[...].astype(f32) + right[...].astype(f32)
+    out[CUT:] = total[CUT:] + across[CUT:].astype(f32) + late
+
+
+def finish(total, across, left, right):
+    return call(
+        finish_kernel,
+        "finish",
+        [WHOLE] * 4,
+        WHOLE,
+        jax.ShapeDtypeStruct(total.shape, f32),
+        (total, across, left, right),
     )
 
 
@@ -375,7 +389,7 @@
 
     shard_across = after(shard_across, from_left, from_right, v_own, across_in)
     behind, ahead = send(shard_across, PLUS), send(shard_across, MINUS)
-    across = closing((across_in, *rows[1:]), (from_left, from_right), 0, bf16)
+    across = closing((across_in, *rows[1:]), from_left, from_right, 0)
     from_across = send(across, ACROSS)
     delta = delta + partner(after(delta, v_own), 2)
     plus, plus_late, minus, minus_late = relay(rows, after(top, across), bottom, 1, (CUT, width - CUT))
@@ -389,9 +403,9 @@
     left_late = send(after(plus_late, *everything), PLUS)
     right_late = send(after(minus_late, *everything), MINUS)
     back = [send(piece, OTHER_CORE) for piece in back]
-    grad, values = place(other, back, grad, v_own, 1)
-    rows = (after(own, grad, values), *rows[1:])
-    grad_weight = closing(rows, (from_across, left, right, left_late, right_late), 1, f32)
+    total = closing(rows, left, right, 1)
+    grad, values = place(after(other, total), back, grad, v_own, 1)
+    grad_weight = finish(after(total, grad, values), from_across, left_late, right_late)
 
     new_global, new_momentum, new_local = outer_step(
         fragment, delta, outer_momentum, outer_global, local_params

time: 107 us -> 107 us (level)
  starting transfers between devices: 47.5 us -> 45.2 us
  waiting for transfers between devices: 34.1 us -> 35.8 us
    ppermute x26, starting transfers between devices: 37.7 us -> 35.2 us  [send(): return lax.ppermute(array, 'fsdp', pairs)]
    ppermute x26, waiting for transfers between devices: 24.2 us -> 25.9 us  [send(): return lax.ppermute(array, 'fsdp', pairs)]
    pallas_call x11 -> x12, Pallas kernels: 19.7 us -> 19.7 us  [call(): pl.pallas_call(kernel, in_specs=in_specs, out_specs=out_specs, out_shape=...]
  transfers between devices with their start and end apart: 31 -> 31, of which waited for: 14 -> 16; matrix products, arithmetic and copies ran while one was open for 0% -> 0% of each run, Pallas kernels for 15% -> 16%
where the time goes in v3:
time: 107 us; the launch traced here: 106 us
  starting transfers between devices  45.2 us (42%)
  waiting for transfers between devices  35.8 us (33%)
  Pallas kernels  20.4 us (19%)
  local copies, waits for them, and re-layouts  3.24 us (3%)
  between operations  1.64 us (2%)
    ppermute x26, starting transfers between devices, send(): return lax.ppermute(array, 'fsdp', pairs)  35.2 us
    ppermute x26, waiting for transfers between devices, send(): return lax.ppermute(array, 'fsdp', pairs)  25.9 us
    pallas_call x12, Pallas kernels, call(): pl.pallas_call(kernel, in_specs=in_specs, out_specs=out_specs, out_shape=...  19.7 us
    ppermute x5, waiting for transfers between devices, partner(): return lax.ppermute(part, 'replica', [(i, i ^ bits) for i in range(16)])  9.99 us
    ppermute x5, starting transfers between devices, partner(): return lax.ppermute(part, 'replica', [(i, i ^ bits) for i in range(16)])  9.93 us
    unnamed x18, local copies, waits for them, and re-layouts  3.16 us
  transfers between devices with their start and end apart: 31, of which 16 were waited for; matrix products, arithmetic and copies ran while one was open for 0% of the time, Pallas kernels for 16%

profile of v3, /device:TPU:8, one launch (start us, length us, event | category | flops | bytes accessed | tf_op | source)
XLA Modules:
  0.0 106.4 jit_solution(17986935152009857981)
XLA Ops:
  0.7 2.2 %copy-done = bf16[256,8192]{1,0:T(8,128)(2,1)S(1)} copy-done((bf16[256,8192]{1,0:T(8,128)(2,1)S(1)}, bf16[256,8192]{1,0:T(8,128)(2,1)}, u32[]{:S(2)}) %copy-start) | copy-done | bytes 4194328
  5.3 2.8 %collective-permute-start.7 = (bf16[512,512]{1,0:T(8,128)(2,1)}, bf16[512,512]{1,0:T(8,128)(2,1)S(1)}, u32[]{:S(2)}, u32[]{:S(2)}) collective-permute-start(bf16[512,512]{1,0:T(8,128)(2,1)} %bitcast.3), channel_id=1, source_target_pairs={{0,6},{1,7},{2,0},{3,1},{4,2},{5,3},{6,4},{7,5},{8,14},{9,15},{10,... | collective-permute-start | bytes 1572872 | tf_op jit(solution)/shard_map/ppermute | solution.py:37
  8.0 7.2 %collective-permute-start.9 = (bf16[512,512]{1,0:T(8,128)(2,1)}, bf16[512,512]{1,0:T(8,128)(2,1)S(1)}, u32[]{:S(2)}, u32[]{:S(2)}) collective-permute-start(bf16[512,512]{1,0:T(8,128)(2,1)} %bitcast.5), channel_id=1, source_target_pairs={{0,8},{1,9},{2,10},{3,11},{4,12},{5,13},{6,14},{7,15},{8,0},{9,1},... | collective-permute-start | bytes 1572872 | tf_op jit(solution)/shard_map/ppermute | solution.py:37
  15.3 1.3 %far_partials.1 = (bf16[2,256,512]{2,1,0:T(8,128)(2,1)S(1)}, bf16[2,256,512]{2,1,0:T(8,128)(2,1)S(1)}) custom-call(s32[8]{0:T(128)S(1)} %broadcast_add_fusion.refs_0_.places, bf16[256,8192]{1,0:T(8,128)(2,1)S(1)} %copy-done.1, bf16[256,512]{1,0:T(8,128)(2,1)S(1)} %copy-done.3, bf16[3,256,512]{2,1,0:T(8,128)(2,1)S(1)} %collective-permute-done.refs_3_, ...), custom_call_target="tpu_custom_call" | custom-call | bytes 5242880 | tf_op jit(solution)/shard_map/far_partials/pallas_call | solution.py:45
  17.4 2.6 %collective-permute-start.3 = (bf16[2,256,512]{2,1,0:T(8,128)(2,1)S(1)}, bf16[2,256,512]{2,1,0:T(8,128)(2,1)S(1)}, u32[]{:S(2)}, u32[]{:S(2)}) collective-permute-start(bf16[2,256,512]{2,1,0:T(8,128)(2,1)S(1)} %get-tuple-element.53), channel_id=1, source_target_pairs={{0,6},{1,7},{2,0},{3,1},{4,2},{5,3},{6,4},{7,5},{8,14},{9,15},{10,... | collective-permute-start | bytes 1572872 | tf_op jit(solution)/shard_map/ppermute | solution.py:37
  20.1 2.4 %collective-permute-start.5 = (f32[16,1024]{1,0:T(8,128)S(1)}, f32[16,1024]{1,0:T(8,128)S(1)}, u32[]{:S(2)}, u32[]{:S(2)}) collective-permute-start(f32[16,1024]{1,0:T(8,128)S(1)} %bitcast.8), channel_id=1, source_target_pairs={{0,16},{16,0},{32,48},{48,32},{64,80},{80,64},{96,112},{112,96},{1... | collective-permute-start | bytes 196616 | tf_op jit(solution)/shard_map/ppermute | solution.py:307
  22.5 1.8 %collective-permute-done.4.refs_9_ = bf16[512,512]{1,0:T(8,128)(2,1)S(1)} collective-permute-done((bf16[512,512]{1,0:T(8,128)(2,1)}, bf16[512,512]{1,0:T(8,128)(2,1)S(1)}, u32[]{:S(2)}, u32[]{:S(2)}) %collective-permute-start.4) | collective-permute-done | bytes 524320 | tf_op jit(solution)/shard_map/ppermute | solution.py:37
  24.7 3.3 %collective-permute-start.8 = (bf16[256,512]{1,0:T(8,128)(2,1)S(1)}, bf16[256,512]{1,0:T(8,128)(2,1)S(1)}, u32[]{:S(2)}, u32[]{:S(2)}) collective-permute-start(bf16[256,512]{1,0:T(8,128)(2,1)S(1)} %slice.17), channel_id=1, source_target_pairs={{0,6},{1,7},{2,0},{3,1},{4,2},{5,3},{6,4},{7,5},{8,14},{9,15},{10,... | collective-permute-start | bytes 786440 | tf_op jit(solution)/shard_map/ppermute | solution.py:37
  28.0 1.6 %collective-permute-done.9._.refs_5_ = bf16[512,512]{1,0:T(8,128)(2,1)S(1)} collective-permute-done((bf16[512,512]{1,0:T(8,128)(2,1)}, bf16[512,512]{1,0:T(8,128)(2,1)S(1)}, u32[]{:S(2)}, u32[]{:S(2)}) %collective-permute-start.9) | collective-permute-done | bytes 524320 | tf_op jit(solution)/shard_map/ppermute | solution.py:37
  30.8 5.7 %collective-permute-done.8.refs_8_ = bf16[256,512]{1,0:T(8,128)(2,1)S(1)} collective-permute-done((bf16[256,512]{1,0:T(8,128)(2,1)S(1)}, bf16[256,512]{1,0:T(8,128)(2,1)S(1)}, u32[]{:S(2)}, u32[]{:S(2)}) %collective-permute-start.8) | collective-permute-done | bytes 262176 | tf_op jit(solution)/shard_map/ppermute | solution.py:37
  36.5 3.4 %collective-permute-done.6.refs_7_ = bf16[256,512]{1,0:T(8,128)(2,1)S(1)} collective-permute-done((bf16[256,512]{1,0:T(8,128)(2,1)S(1)}, bf16[256,512]{1,0:T(8,128)(2,1)S(1)}, u32[]{:S(2)}, u32[]{:S(2)}) %collective-permute-start.6) | collective-permute-done | bytes 262176 | tf_op jit(solution)/shard_map/ppermute | solution.py:37
  40.0 1.3 %relay.2 = (bf16[512,512]{1,0:T(8,128)(2,1)S(1)}, bf16[512,512]{1,0:T(8,128)(2,1)S(1)}) custom-call(s32[8]{0:T(128)S(1)} %hold.1.refs_0_, bf16[256,8192]{1,0:T(8,128)(2,1)S(1)} %copy-done.1, bf16[256,512]{1,0:T(8,128)(2,1)S(1)} %copy-done.3, bf16[3,256,512]{2,1,0:T(8,128)(2,1)S(1)} %collective-permute-done.refs_3_, ...), custom_call_target="tpu_custom_call" | custom-call | bytes 5242880 | tf_op jit(solution)/shard_map/relay/pallas_call | solution.py:45
  41.3 3.2 %collective-permute-start.11 = (bf16[512,512]{1,0:T(8,128)(2,1)S(1)}, bf16[512,512]{1,0:T(8,128)(2,1)S(1)}, u32[]{:S(2)}, u32[]{:S(2)}) collective-permute-start(bf16[512,512]{1,0:T(8,128)(2,1)S(1)} %get-tuple-element.60), channel_id=1, source_target_pairs={{0,6},{1,7},{2,0},{3,1},{4,2},{5,3},{6,4},{7,5},{8,14},{9,15},{10,... | collective-permute-start | bytes 1572872 | tf_op jit(solution)/shard_map/ppermute | solution.py:37
  44.6 1.9 %collective-permute-start.12 = (f32[16,1024]{1,0:T(8,128)S(1)}, f32[16,1024]{1,0:T(8,128)S(1)}, u32[]{:S(2)}, u32[]{:S(2)}) collective-permute-start(f32[16,1024]{1,0:T(8,128)S(1)} %add.54), channel_id=1, source_target_pairs={{0,64},{16,80},{32,96},{48,112},{64,0},{80,16},{96,32},{112,48},{1... | collective-permute-start | bytes 196616 | tf_op jit(solution)/shard_map/ppermute | solution.py:307
  46.5 3.3 %collective-permute-start.13 = (f32[16,1024]{1,0:T(8,128)S(1)}, f32[16,1024]{1,0:T(8,128)S(1)}, u32[]{:S(2)}, u32[]{:S(2)}) collective-permute-start(f32[16,1024]{1,0:T(8,128)S(1)} %add.54), channel_id=1, source_target_pairs={{0,128},{16,144},{32,160},{48,176},{64,192},{80,208},{96,224},{112... | collective-permute-start | bytes 196616 | tf_op jit(solution)/shard_map/ppermute | solution.py:307
  49.8 3.6 %collective-permute-done.13 = f32[16,1024]{1,0:T(8,128)S(1)} collective-permute-done((f32[16,1024]{1,0:T(8,128)S(1)}, f32[16,1024]{1,0:T(8,128)S(1)}, u32[]{:S(2)}, u32[]{:S(2)}) %collective-permute-start.13) | collective-permute-done | bytes 65568 | tf_op jit(solution)/shard_map/ppermute | solution.py:307
  53.4 2.4 %collective-permute-done.14 = f32[16,1024]{1,0:T(8,128)S(1)} collective-permute-done((f32[16,1024]{1,0:T(8,128)S(1)}, f32[16,1024]{1,0:T(8,128)S(1)}, u32[]{:S(2)}, u32[]{:S(2)}) %collective-permute-start.14) | collective-permute-done | bytes 65568 | tf_op jit(solution)/shard_map/ppermute | solution.py:307
  55.8 3.5 %apply_weight.2 = (f32[256,512]{1,0:T(8,128)S(1)}, f32[256,512]{1,0:T(8,128)S(1)}, bf16[256,8192]{1,0:T(8,128)(2,1)}, bf16[2,256,512]{2,1,0:T(8,128)(2,1)S(1)}, bf16[2,256,512]{2,1,0:T(8,128)(2,1)S(1)}) custom-call(s32[8]{0:T(128)S(1)} %broadcast_add_fusion.refs_0_.places, bf16[256,8192]{1,0:T(8,128)(2,1)S(1)} %copy-done.1, bf16[256,512]{1,0:T(8,128)(2,1)S(1)} %copy-done.3, ...), custom_call_target="tpu_custom_call" | custom-call | bytes 4194304 | tf_op jit(solution)/shard_map/apply_weight/pallas_call | solution.py:45
  59.5 3.2 %collective-permute-start.17 = (bf16[512,512]{1,0:T(8,128)(2,1)S(1)}, bf16[512,512]{1,0:T(8,128)(2,1)S(1)}, u32[]{:S(2)}, u32[]{:S(2)}) collective-permute-start(bf16[512,512]{1,0:T(8,128)(2,1)S(1)} %collective-permute-done.9._.refs_5_), channel_id=1, source_target_pairs={{0,6},{1,7},{2,0},{3,1},{4,2},{5,3},{6,4},{7,5},{8,14},{9,15},{10,... | collective-permute-start | bytes 1572872 | tf_op jit(solution)/shard_map/ppermute | solution.py:37
  64.2 4.6 %collective-permute-start.27 = (bf16[512,512]{1,0:T(8,128)(2,1)S(1)}, bf16[512,512]{1,0:T(8,128)(2,1)S(1)}, u32[]{:S(2)}, u32[]{:S(2)}) collective-permute-start(bf16[512,512]{1,0:T(8,128)(2,1)S(1)} %closing.2), channel_id=1, source_target_pairs={{0,8},{1,9},{2,10},{3,11},{4,12},{5,13},{6,14},{7,15},{8,0},{9,1},... | collective-permute-start | bytes 1572872 | tf_op jit(solution)/shard_map/ppermute | solution.py:37
  68.9 2.7 %collective-permute-done.15.refs_9_ = bf16[512,512]{1,0:T(8,128)(2,1)S(1)} collective-permute-done((bf16[512,512]{1,0:T(8,128)(2,1)S(1)}, bf16[512,512]{1,0:T(8,128)(2,1)S(1)}, u32[]{:S(2)}, u32[]{:S(2)}) %collective-permute-start.15) | collective-permute-done | bytes 524320 | tf_op jit(solution)/shard_map/ppermute | solution.py:37
  71.7 3.3 %collective-permute-start.22 = (bf16[256,512]{1,0:T(8,128)(2,1)S(1)}, bf16[256,512]{1,0:T(8,128)(2,1)S(1)}, u32[]{:S(2)}, u32[]{:S(2)}) collective-permute-start(bf16[256,512]{1,0:T(8,128)(2,1)S(1)} %slice.19), channel_id=1, source_target_pairs={{0,6},{1,7},{2,0},{3,1},{4,2},{5,3},{6,4},{7,5},{8,14},{9,15},{10,... | collective-permute-start | bytes 786440 | tf_op jit(solution)/shard_map/ppermute | solution.py:37
  76.3 1.5 %place.2.refs_12_ = bf16[256,8192]{1,0:T(8,128)(2,1)} custom-call(s32[8]{0:T(128)S(1)} %broadcast_add_fusion.1.places.refs_0_, bf16[2,256,512]{2,1,0:T(8,128)(2,1)S(1)} %collective-permute-done.18.refs_1_, bf16[2,256,512]{2,1,0:T(8,128)(2,1)S(1)} %collective-permute-done.19.refs_2_, ...), custom_call_target="tpu_custom_call", output_to_operand_aliasing={{}: (3, {})} | custom-call | bytes 5242880 | tf_op jit(solution)/shard_map/place/pallas_call | solution.py:45
  77.9 1.3 %collective-permute-done.21.refs_7_ = bf16[256,512]{1,0:T(8,128)(2,1)S(1)} collective-permute-done((bf16[256,512]{1,0:T(8,128)(2,1)S(1)}, bf16[256,512]{1,0:T(8,128)(2,1)S(1)}, u32[]{:S(2)}, u32[]{:S(2)}) %collective-permute-start.21) | collective-permute-done | bytes 262176 | tf_op jit(solution)/shard_map/ppermute | solution.py:37
  80.5 3.5 %apply_weight.3 = (f32[256,512]{1,0:T(8,128)S(1)}, bf16[256,8192]{1,0:T(8,128)(2,1)}, bf16[320,512]{1,0:T(8,128)(2,1)S(1)}, bf16[320,512]{1,0:T(8,128)(2,1)S(1)}...) custom-call(s32[8]{0:T(128)S(1)} %broadcast_add_fusion.refs_0_.places, ...), custom_call_target="tpu_custom_call", output_to_operand_aliasing={{1}: (12, {})} | custom-call | bytes 4194304 | tf_op jit(solution)/shard_map/apply_weight/pallas_call | solution.py:45
  84.1 2.4 %collective-permute-start.28 = (f32[16,1024]{1,0:T(8,128)S(1)}, f32[16,1024]{1,0:T(8,128)S(1)}, u32[]{:S(2)}, u32[]{:S(2)}) collective-permute-start(f32[16,1024]{1,0:T(8,128)S(1)} %add_add_fusion), channel_id=1, source_target_pairs={{0,32},{16,48},{32,0},{48,16},{64,96},{80,112},{96,64},{112,80},{1... | collective-permute-start | bytes 196616 | tf_op jit(solution)/shard_map/ppermute | solution.py:307
  86.5 3.5 %collective-permute-done.28 = f32[16,1024]{1,0:T(8,128)S(1)} collective-permute-done((f32[16,1024]{1,0:T(8,128)S(1)}, f32[16,1024]{1,0:T(8,128)S(1)}, u32[]{:S(2)}, u32[]{:S(2)}) %collective-permute-start.28) | collective-permute-done | bytes 65568 | tf_op jit(solution)/shard_map/ppermute | solution.py:307
  90.1 3.4 %collective-permute-done.27.across = bf16[512,512]{1,0:T(8,128)(2,1)S(1)} collective-permute-done((bf16[512,512]{1,0:T(8,128)(2,1)S(1)}, bf16[512,512]{1,0:T(8,128)(2,1)S(1)}, u32[]{:S(2)}, u32[]{:S(2)}) %collective-permute-start.27) | collective-permute-done | bytes 524320 | tf_op jit(solution)/shard_map/ppermute | solution.py:37
  94.7 1.8 %collective-permute-start.30 = (bf16[256,512]{1,0:T(8,128)(2,1)S(1)}, bf16[256,512]{1,0:T(8,128)(2,1)S(1)}, u32[]{:S(2)}, u32[]{:S(2)}) collective-permute-start(bf16[256,512]{1,0:T(8,128)(2,1)S(1)} %get-tuple-element.90), channel_id=1, source_target_pairs={{0,6},{1,7},{2,0},{3,1},{4,2},{5,3},{6,4},{7,5},{8,14},{9,15},{10,... | collective-permute-start | bytes 786440 | tf_op jit(solution)/shard_map/ppermute | solution.py:37
  99.1 2.2 %place.3 = (bf16[256,8192]{1,0:T(8,128)(2,1)}, bf16[256,512]{1,0:T(8,128)(2,1)}) custom-call(s32[8]{0:T(128)S(1)} %broadcast_add_fusion.1.places.refs_0_, bf16[320,512]{1,0:T(8,128)(2,1)S(1)} %collective-permute-done.23.refs_1_, bf16[320,512]{1,0:T(8,128)(2,1)S(1)} %collective-permute-done.24.refs_2_, ...), custom_call_target="tpu_custom_call", output_to_operand_aliasing={{0}: (6, {})} | custom-call | bytes 5242880 | tf_op jit(solution)/shard_map/place/pallas_call | solution.py:45
  101.4 1.4 %collective-permute-done.30.right = bf16[256,512]{1,0:T(8,128)(2,1)S(1)} collective-permute-done((bf16[256,512]{1,0:T(8,128)(2,1)S(1)}, bf16[256,512]{1,0:T(8,128)(2,1)S(1)}, u32[]{:S(2)}, u32[]{:S(2)}) %collective-permute-start.30) | collective-permute-done | bytes 262176 | tf_op jit(solution)/shard_map/ppermute | solution.py:37
  102.8 2.5 %collective-permute-done.29.left = bf16[256,512]{1,0:T(8,128)(2,1)S(1)} collective-permute-done((bf16[256,512]{1,0:T(8,128)(2,1)S(1)}, bf16[256,512]{1,0:T(8,128)(2,1)S(1)}, u32[]{:S(2)}, u32[]{:S(2)}) %collective-permute-start.29) | collective-permute-done | bytes 262176 | tf_op jit(solution)/shard_map/ppermute | solution.py:37
  (70 shorter events, 13.9 us)
Async XLA Ops:
  4.7 10.6 %collective-permute-start.1 = (bf16[6,256,512]{2,1,0:T(8,128)(2,1)S(1)}, bf16[6,256,512]{2,1,0:T(8,128)(2,1)S(1)}, u32[]{:S(2)}, u32[]{:S(2)}) collective-permute-start(bf16[6,256,512]{2,1,0:T(8,128)(2,1)S(1)} %get-tuple-element.51), channel_id=1, source_target_pairs={{0,1},{1,0},{2,3},{3,2},{4,5},{5,4},{6,7},{7,6},{8,9},{9,8},{10,11... | collective-permute-start | bytes 4718600 | tf_op jit(solution)/shard_map/ppermute | solution.py:37
  4.8 10.5 %collective-permute-start = (bf16[3,256,512]{2,1,0:T(8,128)(2,1)S(1)}, bf16[3,256,512]{2,1,0:T(8,128)(2,1)S(1)}, u32[]{:S(2)}, u32[]{:S(2)}) collective-permute-start(bf16[3,256,512]{2,1,0:T(8,128)(2,1)S(1)} %get-tuple-element.50), channel_id=1, source_target_pairs={{0,1},{1,0},{2,3},{3,2},{4,5},{5,4},{6,7},{7,6},{8,9},{9,8},{10,11... | collective-permute-start | bytes 2359304 | tf_op jit(solution)/shard_map/ppermute | solution.py:37
  5.3 14.8 %collective-permute-start.7 = (bf16[512,512]{1,0:T(8,128)(2,1)}, bf16[512,512]{1,0:T(8,128)(2,1)S(1)}, u32[]{:S(2)}, u32[]{:S(2)}) collective-permute-start(bf16[512,512]{1,0:T(8,128)(2,1)} %bitcast.3), channel_id=1, source_target_pairs={{0,6},{1,7},{2,0},{3,1},{4,2},{5,3},{6,4},{7,5},{8,14},{9,15},{10,... | collective-permute-start | bytes 1572872 | tf_op jit(solution)/shard_map/ppermute | solution.py:37
  8.0 16.2 %collective-permute-start.4 = (bf16[512,512]{1,0:T(8,128)(2,1)}, bf16[512,512]{1,0:T(8,128)(2,1)S(1)}, u32[]{:S(2)}, u32[]{:S(2)}) collective-permute-start(bf16[512,512]{1,0:T(8,128)(2,1)} %bitcast.4), channel_id=1, source_target_pairs={{0,2},{1,3},{2,4},{3,5},{4,6},{5,7},{6,0},{7,1},{8,10},{9,11},{10,... | collective-permute-start | bytes 1572872 | tf_op jit(solution)/shard_map/ppermute | solution.py:37
  8.0 21.6 %collective-permute-start.9 = (bf16[512,512]{1,0:T(8,128)(2,1)}, bf16[512,512]{1,0:T(8,128)(2,1)S(1)}, u32[]{:S(2)}, u32[]{:S(2)}) collective-permute-start(bf16[512,512]{1,0:T(8,128)(2,1)} %bitcast.5), channel_id=1, source_target_pairs={{0,8},{1,9},{2,10},{3,11},{4,12},{5,13},{6,14},{7,15},{8,0},{9,1},... | collective-permute-start | bytes 1572872 | tf_op jit(solution)/shard_map/ppermute | solution.py:37
  16.6 23.4 %collective-permute-start.2 = (bf16[2,256,512]{2,1,0:T(8,128)(2,1)S(1)}, bf16[2,256,512]{2,1,0:T(8,128)(2,1)S(1)}, u32[]{:S(2)}, u32[]{:S(2)}) collective-permute-start(bf16[2,256,512]{2,1,0:T(8,128)(2,1)S(1)} %get-tuple-element.52), channel_id=1, source_target_pairs={{0,2},{1,3},{2,4},{3,5},{4,6},{5,7},{6,0},{7,1},{8,10},{9,11},{10,... | collective-permute-start | bytes 1572872 | tf_op jit(solution)/shard_map/ppermute | solution.py:37
  17.4 22.6 %collective-permute-start.3 = (bf16[2,256,512]{2,1,0:T(8,128)(2,1)S(1)}, bf16[2,256,512]{2,1,0:T(8,128)(2,1)S(1)}, u32[]{:S(2)}, u32[]{:S(2)}) collective-permute-start(bf16[2,256,512]{2,1,0:T(8,128)(2,1)S(1)} %get-tuple-element.53), channel_id=1, source_target_pairs={{0,6},{1,7},{2,0},{3,1},{4,2},{5,3},{6,4},{7,5},{8,14},{9,15},{10,... | collective-permute-start | bytes 1572872 | tf_op jit(solution)/shard_map/ppermute | solution.py:37
  20.1 4.6 %collective-permute-start.5 = (f32[16,1024]{1,0:T(8,128)S(1)}, f32[16,1024]{1,0:T(8,128)S(1)}, u32[]{:S(2)}, u32[]{:S(2)}) collective-permute-start(f32[16,1024]{1,0:T(8,128)S(1)} %bitcast.8), channel_id=1, source_target_pairs={{0,16},{16,0},{32,48},{48,32},{64,80},{80,64},{96,112},{112,96},{1... | collective-permute-start | bytes 196616 | tf_op jit(solution)/shard_map/ppermute | solution.py:307
  24.7 11.8 %collective-permute-start.8 = (bf16[256,512]{1,0:T(8,128)(2,1)S(1)}, bf16[256,512]{1,0:T(8,128)(2,1)S(1)}, u32[]{:S(2)}, u32[]{:S(2)}) collective-permute-start(bf16[256,512]{1,0:T(8,128)(2,1)S(1)} %slice.17), channel_id=1, source_target_pairs={{0,6},{1,7},{2,0},{3,1},{4,2},{5,3},{6,4},{7,5},{8,14},{9,15},{10,... | collective-permute-start | bytes 786440 | tf_op jit(solution)/shard_map/ppermute | solution.py:37
  28.0 11.9 %collective-permute-start.6 = (bf16[256,512]{1,0:T(8,128)(2,1)S(1)}, bf16[256,512]{1,0:T(8,128)(2,1)S(1)}, u32[]{:S(2)}, u32[]{:S(2)}) collective-permute-start(bf16[256,512]{1,0:T(8,128)(2,1)S(1)} %slice.16), channel_id=1, source_target_pairs={{0,2},{1,3},{2,4},{3,5},{4,6},{5,7},{6,0},{7,1},{8,10},{9,11},{10,... | collective-permute-start | bytes 786440 | tf_op jit(solution)/shard_map/ppermute | solution.py:37
  30.8 25.0 %copy-start.4 = (bf16[1,512,512]{2,1,0:T(8,128)(2,1)S(1)}, bf16[1,512,512]{2,1,0:T(8,128)(2,1)}, u32[]{:S(2)}) copy-start(bf16[1,512,512]{2,1,0:T(8,128)(2,1)} %param.10) | copy-start | bytes 1572868
  41.2 18.1 %collective-permute-start.10 = (bf16[512,512]{1,0:T(8,128)(2,1)S(1)}, bf16[512,512]{1,0:T(8,128)(2,1)S(1)}, u32[]{:S(2)}, u32[]{:S(2)}) collective-permute-start(bf16[512,512]{1,0:T(8,128)(2,1)S(1)} %get-tuple-element.59), channel_id=1, source_target_pairs={{0,2},{1,3},{2,4},{3,5},{4,6},{5,7},{6,0},{7,1},{8,10},{9,11},{10,... | collective-permute-start | bytes 1572872 | tf_op jit(solution)/shard_map/ppermute | solution.py:37
  41.3 18.0 %collective-permute-start.11 = (bf16[512,512]{1,0:T(8,128)(2,1)S(1)}, bf16[512,512]{1,0:T(8,128)(2,1)S(1)}, u32[]{:S(2)}, u32[]{:S(2)}) collective-permute-start(bf16[512,512]{1,0:T(8,128)(2,1)S(1)} %get-tuple-element.60), channel_id=1, source_target_pairs={{0,6},{1,7},{2,0},{3,1},{4,2},{5,3},{6,4},{7,5},{8,14},{9,15},{10,... | collective-permute-start | bytes 1572872 | tf_op jit(solution)/shard_map/ppermute | solution.py:37
  44.6 5.2 %collective-permute-start.12 = (f32[16,1024]{1,0:T(8,128)S(1)}, f32[16,1024]{1,0:T(8,128)S(1)}, u32[]{:S(2)}, u32[]{:S(2)}) collective-permute-start(f32[16,1024]{1,0:T(8,128)S(1)} %add.54), channel_id=1, source_target_pairs={{0,64},{16,80},{32,96},{48,112},{64,0},{80,16},{96,32},{112,48},{1... | collective-permute-start | bytes 196616 | tf_op jit(solution)/shard_map/ppermute | solution.py:307
  46.5 6.9 %collective-permute-start.13 = (f32[16,1024]{1,0:T(8,128)S(1)}, f32[16,1024]{1,0:T(8,128)S(1)}, u32[]{:S(2)}, u32[]{:S(2)}) collective-permute-start(f32[16,1024]{1,0:T(8,128)S(1)} %add.54), channel_id=1, source_target_pairs={{0,128},{16,144},{32,160},{48,176},{64,192},{80,208},{96,224},{112... | collective-permute-start | bytes 196616 | tf_op jit(solution)/shard_map/ppermute | solution.py:307
  49.7 6.1 %collective-permute-start.14 = (f32[16,1024]{1,0:T(8,128)S(1)}, f32[16,1024]{1,0:T(8,128)S(1)}, u32[]{:S(2)}, u32[]{:S(2)}) collective-permute-start(f32[16,1024]{1,0:T(8,128)S(1)} %add.54), channel_id=1, source_target_pairs={{0,192},{16,208},{32,224},{48,240},{64,128},{80,144},{96,160},{112... | collective-permute-start | bytes 196616 | tf_op jit(solution)/shard_map/ppermute | solution.py:307
  59.4 12.2 %collective-permute-start.15 = (bf16[512,512]{1,0:T(8,128)(2,1)S(1)}, bf16[512,512]{1,0:T(8,128)(2,1)S(1)}, u32[]{:S(2)}, u32[]{:S(2)}) collective-permute-start(bf16[512,512]{1,0:T(8,128)(2,1)S(1)} %collective-permute-done.9._.refs_5_), channel_id=1, source_target_pairs={{0,2},{1,3},{2,4},{3,5},{4,6},{5,7},{6,0},{7,1},{8,10},{9,11},{10,... | collective-permute-start | bytes 1572872 | tf_op jit(solution)/shard_map/ppermute | solution.py:37
  59.5 12.2 %collective-permute-start.17 = (bf16[512,512]{1,0:T(8,128)(2,1)S(1)}, bf16[512,512]{1,0:T(8,128)(2,1)S(1)}, u32[]{:S(2)}, u32[]{:S(2)}) collective-permute-start(bf16[512,512]{1,0:T(8,128)(2,1)S(1)} %collective-permute-done.9._.refs_5_), channel_id=1, source_target_pairs={{0,6},{1,7},{2,0},{3,1},{4,2},{5,3},{6,4},{7,5},{8,14},{9,15},{10,... | collective-permute-start | bytes 1572872 | tf_op jit(solution)/shard_map/ppermute | solution.py:37
  62.7 13.6 %collective-permute-start.18 = (bf16[2,256,512]{2,1,0:T(8,128)(2,1)S(1)}, bf16[2,256,512]{2,1,0:T(8,128)(2,1)S(1)}, u32[]{:S(2)}, u32[]{:S(2)}) collective-permute-start(bf16[2,256,512]{2,1,0:T(8,128)(2,1)S(1)} %get-tuple-element.71), channel_id=1, source_target_pairs={{0,1},{1,0},{2,3},{3,2},{4,5},{5,4},{6,7},{7,6},{8,9},{9,8},{10,11... | collective-permute-start | bytes 1572872 | tf_op jit(solution)/shard_map/ppermute | solution.py:37
  62.7 13.6 %collective-permute-start.19 = (bf16[2,256,512]{2,1,0:T(8,128)(2,1)S(1)}, bf16[2,256,512]{2,1,0:T(8,128)(2,1)S(1)}, u32[]{:S(2)}, u32[]{:S(2)}) collective-permute-start(bf16[2,256,512]{2,1,0:T(8,128)(2,1)S(1)} %get-tuple-element.72), channel_id=1, source_target_pairs={{0,1},{1,0},{2,3},{3,2},{4,5},{5,4},{6,7},{7,6},{8,9},{9,8},{10,11... | collective-permute-start | bytes 1572872 | tf_op jit(solution)/shard_map/ppermute | solution.py:37
  64.2 29.2 %collective-permute-start.27 = (bf16[512,512]{1,0:T(8,128)(2,1)S(1)}, bf16[512,512]{1,0:T(8,128)(2,1)S(1)}, u32[]{:S(2)}, u32[]{:S(2)}) collective-permute-start(bf16[512,512]{1,0:T(8,128)(2,1)S(1)} %closing.2), channel_id=1, source_target_pairs={{0,8},{1,9},{2,10},{3,11},{4,12},{5,13},{6,14},{7,15},{8,0},{9,1},... | collective-permute-start | bytes 1572872 | tf_op jit(solution)/shard_map/ppermute | solution.py:37
  71.6 7.7 %collective-permute-start.21 = (bf16[256,512]{1,0:T(8,128)(2,1)S(1)}, bf16[256,512]{1,0:T(8,128)(2,1)S(1)}, u32[]{:S(2)}, u32[]{:S(2)}) collective-permute-start(bf16[256,512]{1,0:T(8,128)(2,1)S(1)} %slice.18), channel_id=1, source_target_pairs={{0,2},{1,3},{2,4},{3,5},{4,6},{5,7},{6,0},{7,1},{8,10},{9,11},{10,... | collective-permute-start | bytes 786440 | tf_op jit(solution)/shard_map/ppermute | solution.py:37
  71.7 8.8 %collective-permute-start.22 = (bf16[256,512]{1,0:T(8,128)(2,1)S(1)}, bf16[256,512]{1,0:T(8,128)(2,1)S(1)}, u32[]{:S(2)}, u32[]{:S(2)}) collective-permute-start(bf16[256,512]{1,0:T(8,128)(2,1)S(1)} %slice.19), channel_id=1, source_target_pairs={{0,6},{1,7},{2,0},{3,1},{4,2},{5,3},{6,4},{7,5},{8,14},{9,15},{10,... | collective-permute-start | bytes 786440 | tf_op jit(solution)/shard_map/ppermute | solution.py:37
  77.8 15.6 %collective-permute-start.20 = (bf16[256,512]{1,0:T(8,128)(2,1)S(1)}, bf16[256,512]{1,0:T(8,128)(2,1)S(1)}, u32[]{:S(2)}, u32[]{:S(2)}) collective-permute-start(bf16[256,512]{1,0:T(8,128)(2,1)S(1)} %get-tuple-element.74), channel_id=1, source_target_pairs={{0,6},{1,7},{2,0},{3,1},{4,2},{5,3},{6,4},{7,5},{8,14},{9,15},{10,... | collective-permute-start | bytes 786440 | tf_op jit(solution)/shard_map/ppermute | solution.py:37
  83.9 12.5 %collective-permute-start.23 = (bf16[320,512]{1,0:T(8,128)(2,1)S(1)}, bf16[320,512]{1,0:T(8,128)(2,1)S(1)}, u32[]{:S(2)}, u32[]{:S(2)}) collective-permute-start(bf16[320,512]{1,0:T(8,128)(2,1)S(1)} %get-tuple-element.77), channel_id=1, source_target_pairs={{0,1},{1,0},{2,3},{3,2},{4,5},{5,4},{6,7},{7,6},{8,9},{9,8},{10,11... | collective-permute-start | bytes 983048 | tf_op jit(solution)/shard_map/ppermute | solution.py:37
  84.0 10.7 %collective-permute-start.16 = (bf16[256,512]{1,0:T(8,128)(2,1)S(1)}, bf16[256,512]{1,0:T(8,128)(2,1)S(1)}, u32[]{:S(2)}, u32[]{:S(2)}) collective-permute-start(bf16[256,512]{1,0:T(8,128)(2,1)S(1)} %get-tuple-element.69), channel_id=1, source_target_pairs={{0,2},{1,3},{2,4},{3,5},{4,6},{5,7},{6,0},{7,1},{8,10},{9,11},{10,... | collective-permute-start | bytes 786440 | tf_op jit(solution)/shard_map/ppermute | solution.py:37
  84.1 5.9 %collective-permute-start.28 = (f32[16,1024]{1,0:T(8,128)S(1)}, f32[16,1024]{1,0:T(8,128)S(1)}, u32[]{:S(2)}, u32[]{:S(2)}) collective-permute-start(f32[16,1024]{1,0:T(8,128)S(1)} %add_add_fusion), channel_id=1, source_target_pairs={{0,32},{16,48},{32,0},{48,16},{64,96},{80,112},{96,64},{112,80},{1... | collective-permute-start | bytes 196616 | tf_op jit(solution)/shard_map/ppermute | solution.py:307
  90.0 9.1 %collective-permute-start.24 = (bf16[320,512]{1,0:T(8,128)(2,1)S(1)}, bf16[320,512]{1,0:T(8,128)(2,1)S(1)}, u32[]{:S(2)}, u32[]{:S(2)}) collective-permute-start(bf16[320,512]{1,0:T(8,128)(2,1)S(1)} %get-tuple-element.78), channel_id=1, source_target_pairs={{0,1},{1,0},{2,3},{3,2},{4,5},{5,4},{6,7},{7,6},{8,9},{9,8},{10,11... | collective-permute-start | bytes 983048 | tf_op jit(solution)/shard_map/ppermute | solution.py:37
  93.5 5.7 %collective-permute-start.25 = (bf16[320,512]{1,0:T(8,128)(2,1)S(1)}, bf16[320,512]{1,0:T(8,128)(2,1)S(1)}, u32[]{:S(2)}, u32[]{:S(2)}) collective-permute-start(bf16[320,512]{1,0:T(8,128)(2,1)S(1)} %get-tuple-element.79), channel_id=1, source_target_pairs={{0,1},{1,0},{2,3},{3,2},{4,5},{5,4},{6,7},{7,6},{8,9},{9,8},{10,11... | collective-permute-start | bytes 983048 | tf_op jit(solution)/shard_map/ppermute | solution.py:37
  93.5 5.7 %collective-permute-start.26 = (bf16[320,512]{1,0:T(8,128)(2,1)S(1)}, bf16[320,512]{1,0:T(8,128)(2,1)S(1)}, u32[]{:S(2)}, u32[]{:S(2)}) collective-permute-start(bf16[320,512]{1,0:T(8,128)(2,1)S(1)} %get-tuple-element.80), channel_id=1, source_target_pairs={{0,1},{1,0},{2,3},{3,2},{4,5},{5,4},{6,7},{7,6},{8,9},{9,8},{10,11... | collective-permute-start | bytes 983048 | tf_op jit(solution)/shard_map/ppermute | solution.py:37
  94.7 8.1 %collective-permute-start.30 = (bf16[256,512]{1,0:T(8,128)(2,1)S(1)}, bf16[256,512]{1,0:T(8,128)(2,1)S(1)}, u32[]{:S(2)}, u32[]{:S(2)}) collective-permute-start(bf16[256,512]{1,0:T(8,128)(2,1)S(1)} %get-tuple-element.90), channel_id=1, source_target_pairs={{0,6},{1,7},{2,0},{3,1},{4,2},{5,3},{6,4},{7,5},{8,14},{9,15},{10,... | collective-permute-start | bytes 786440 | tf_op jit(solution)/shard_map/ppermute | solution.py:37
  96.5 8.8 %collective-permute-start.29 = (bf16[256,512]{1,0:T(8,128)(2,1)S(1)}, bf16[256,512]{1,0:T(8,128)(2,1)S(1)}, u32[]{:S(2)}, u32[]{:S(2)}) collective-permute-start(bf16[256,512]{1,0:T(8,128)(2,1)S(1)} %get-tuple-element.88), channel_id=1, source_target_pairs={{0,2},{1,3},{2,4},{3,5},{4,6},{5,7},{6,0},{7,1},{8,10},{9,11},{10,... | collective-permute-start | bytes 786440 | tf_op jit(solution)/shard_map/ppermute | solution.py:37
  (8 other events, 92.3 us)

commit v4 on v3

--- a/solution.py
+++ b/solution.py
@@ -371,13 +371,13 @@
 
     rows = (own, tokens, cotangent, *par)
     top, bottom = far_partials(*rows)
-    delta = after(outer_delta[0], top)
-    delta = delta + partner(delta, 1)
+    delta = outer_delta[0] + partner(outer_delta[0], 1)
+    gate = top
     top, bottom = send(top, PLUS), send(bottom, MINUS)
-    far_top = send(after(behind[:half], delta), PLUS)
-    far_bottom = send(after(ahead[half:], delta), MINUS)
-
-    across_in = hold(own, shard_across, HOLD)
+    far_top = send(after(behind[:half], gate), PLUS)
+    far_bottom = send(after(ahead[half:], gate), MINUS)
+
+    across_in = hold(own, after(shard_across, delta), HOLD)
     top, bottom, far_top, far_bottom = lax.optimization_barrier((top, bottom, far_top, far_bottom))
     plus, minus = relay((across_in, *rows[1:]), top, bottom, 0, (width,))
     from_left, from_right = send(plus, PLUS), send(minus, MINUS)

time: 107 us -> 104 us (0.972)
  waiting for transfers between devices: 35.8 us -> 33.3 us
    ppermute x26, waiting for transfers between devices: 25.9 us -> 22.4 us  [send(): return lax.ppermute(array, 'fsdp', pairs)]
    ppermute x5, starting transfers between devices: 9.93 us -> 11 us  [partner(): return lax.ppermute(part, 'replica', [(i, i ^ bits) for i in range(16)])]
  transfers between devices with their start and end apart: 31 -> 31, of which waited for: 16 -> 14; matrix products, arithmetic and copies ran while one was open for 0% -> 0% of each run, Pallas kernels for 16% -> 17%
where the time goes in v4:
time: 104 us
  starting transfers between devices  45.5 us (44%)
  waiting for transfers between devices  33.3 us (32%)
  Pallas kernels  20.4 us (20%)
  local copies, waits for them, and re-layouts  3.24 us (3%)
  between operations  1.64 us (2%)
    ppermute x26, starting transfers between devices, send(): return lax.ppermute(array, 'fsdp', pairs)  34.5 us
    ppermute x26, waiting for transfers between devices, send(): return lax.ppermute(array, 'fsdp', pairs)  22.4 us
    pallas_call x12, Pallas kernels, call(): pl.pallas_call(kernel, in_specs=in_specs, out_specs=out_specs, out_shape=...  19.7 us
    ppermute x5, starting transfers between devices, partner(): return lax.ppermute(part, 'replica', [(i, i ^ bits) for i in range(16)])  11 us
    ppermute x5, waiting for transfers between devices, partner(): return lax.ppermute(part, 'replica', [(i, i ^ bits) for i in range(16)])  10.9 us
    unnamed x18, local copies, waits for them, and re-layouts  3.16 us
  transfers between devices with their start and end apart: 31, of which 14 were waited for; matrix products, arithmetic and copies ran while one was open for 0% of the time, Pallas kernels for 17%

profile of v4, /device:TPU:8, one launch (start us, length us, event | category | flops | bytes accessed | tf_op | source)
XLA Modules:
  0.0 104.2 jit_solution(13849130344827651979)
XLA Ops:
  0.7 2.2 %copy-done = bf16[256,8192]{1,0:T(8,128)(2,1)S(1)} copy-done((bf16[256,8192]{1,0:T(8,128)(2,1)S(1)}, bf16[256,8192]{1,0:T(8,128)(2,1)}, u32[]{:S(2)}) %copy-start) | copy-done | bytes 4194328
  5.3 1.5 %collective-permute-start.4 = (bf16[512,512]{1,0:T(8,128)(2,1)}, bf16[512,512]{1,0:T(8,128)(2,1)S(1)}, u32[]{:S(2)}, u32[]{:S(2)}) collective-permute-start(bf16[512,512]{1,0:T(8,128)(2,1)} %bitcast.4), channel_id=1, source_target_pairs={{0,2},{1,3},{2,4},{3,5},{4,6},{5,7},{6,0},{7,1},{8,10},{9,11},{10,... | collective-permute-start | bytes 1572872 | tf_op jit(solution)/shard_map/ppermute | solution.py:37
  6.8 1.7 %collective-permute-start.6 = (bf16[512,512]{1,0:T(8,128)(2,1)}, bf16[512,512]{1,0:T(8,128)(2,1)S(1)}, u32[]{:S(2)}, u32[]{:S(2)}) collective-permute-start(bf16[512,512]{1,0:T(8,128)(2,1)} %bitcast.5), channel_id=1, source_target_pairs={{0,6},{1,7},{2,0},{3,1},{4,2},{5,3},{6,4},{7,5},{8,14},{9,15},{10,... | collective-permute-start | bytes 1572872 | tf_op jit(solution)/shard_map/ppermute | solution.py:37
  8.5 7.2 %collective-permute-start.8 = (bf16[512,512]{1,0:T(8,128)(2,1)}, bf16[512,512]{1,0:T(8,128)(2,1)S(1)}, u32[]{:S(2)}, u32[]{:S(2)}) collective-permute-start(bf16[512,512]{1,0:T(8,128)(2,1)} %bitcast.6), channel_id=1, source_target_pairs={{0,8},{1,9},{2,10},{3,11},{4,12},{5,13},{6,14},{7,15},{8,0},{9,1},... | collective-permute-start | bytes 1572872 | tf_op jit(solution)/shard_map/ppermute | solution.py:37
  17.4 3.0 %collective-permute-start.3 = (bf16[2,256,512]{2,1,0:T(8,128)(2,1)S(1)}, bf16[2,256,512]{2,1,0:T(8,128)(2,1)S(1)}, u32[]{:S(2)}, u32[]{:S(2)}) collective-permute-start(bf16[2,256,512]{2,1,0:T(8,128)(2,1)S(1)} %get-tuple-element.53), channel_id=1, source_target_pairs={{0,6},{1,7},{2,0},{3,1},{4,2},{5,3},{6,4},{7,5},{8,14},{9,15},{10,... | collective-permute-start | bytes 1572872 | tf_op jit(solution)/shard_map/ppermute | solution.py:37
  21.0 2.7 %collective-permute-start.9 = (f32[16,1024]{1,0:T(8,128)S(1)}, f32[16,1024]{1,0:T(8,128)S(1)}, u32[]{:S(2)}, u32[]{:S(2)}) collective-permute-start(f32[16,1024]{1,0:T(8,128)S(1)} %bitcast.9), channel_id=1, source_target_pairs={{0,16},{16,0},{32,48},{48,32},{64,80},{80,64},{96,112},{112,96},{1... | collective-permute-start | bytes 196616 | tf_op jit(solution)/shard_map/ppermute | solution.py:307
  23.8 2.1 %collective-permute-done.9 = f32[16,1024]{1,0:T(8,128)S(1)} collective-permute-done((f32[16,1024]{1,0:T(8,128)S(1)}, f32[16,1024]{1,0:T(8,128)S(1)}, u32[]{:S(2)}, u32[]{:S(2)}) %collective-permute-start.9) | collective-permute-done | bytes 65568 | tf_op jit(solution)/shard_map/ppermute | solution.py:307
  25.9 1.4 %collective-permute-start.7 = (bf16[256,512]{1,0:T(8,128)(2,1)S(1)}, bf16[256,512]{1,0:T(8,128)(2,1)S(1)}, u32[]{:S(2)}, u32[]{:S(2)}) collective-permute-start(bf16[256,512]{1,0:T(8,128)(2,1)S(1)} %slice.17), channel_id=1, source_target_pairs={{0,6},{1,7},{2,0},{3,1},{4,2},{5,3},{6,4},{7,5},{8,14},{9,15},{10,... | collective-permute-start | bytes 786440 | tf_op jit(solution)/shard_map/ppermute | solution.py:37
  27.3 2.5 %collective-permute-done.8._.refs_5_ = bf16[512,512]{1,0:T(8,128)(2,1)S(1)} collective-permute-done((bf16[512,512]{1,0:T(8,128)(2,1)}, bf16[512,512]{1,0:T(8,128)(2,1)S(1)}, u32[]{:S(2)}, u32[]{:S(2)}) %collective-permute-start.8) | collective-permute-done | bytes 524320 | tf_op jit(solution)/shard_map/ppermute | solution.py:37
  31.0 6.5 %collective-permute-done.5.refs_7_ = bf16[256,512]{1,0:T(8,128)(2,1)S(1)} collective-permute-done((bf16[256,512]{1,0:T(8,128)(2,1)S(1)}, bf16[256,512]{1,0:T(8,128)(2,1)S(1)}, u32[]{:S(2)}, u32[]{:S(2)}) %collective-permute-start.5) | collective-permute-done | bytes 262176 | tf_op jit(solution)/shard_map/ppermute | solution.py:37
  37.5 1.3 %relay.2 = (bf16[512,512]{1,0:T(8,128)(2,1)S(1)}, bf16[512,512]{1,0:T(8,128)(2,1)S(1)}) custom-call(s32[8]{0:T(128)S(1)} %hold.1.refs_0_, bf16[256,8192]{1,0:T(8,128)(2,1)S(1)} %copy-done.1, bf16[256,512]{1,0:T(8,128)(2,1)S(1)} %copy-done.3, bf16[3,256,512]{2,1,0:T(8,128)(2,1)S(1)} %collective-permute-done.refs_3_, ...), custom_call_target="tpu_custom_call" | custom-call | bytes 5242880 | tf_op jit(solution)/shard_map/relay/pallas_call | solution.py:45
  38.8 1.6 %collective-permute-start.10 = (bf16[512,512]{1,0:T(8,128)(2,1)S(1)}, bf16[512,512]{1,0:T(8,128)(2,1)S(1)}, u32[]{:S(2)}, u32[]{:S(2)}) collective-permute-start(bf16[512,512]{1,0:T(8,128)(2,1)S(1)} %get-tuple-element.59), channel_id=1, source_target_pairs={{0,2},{1,3},{2,4},{3,5},{4,6},{5,7},{6,0},{7,1},{8,10},{9,11},{10,... | collective-permute-start | bytes 1572872 | tf_op jit(solution)/shard_map/ppermute | solution.py:37
  40.3 1.8 %collective-permute-start.11 = (bf16[512,512]{1,0:T(8,128)(2,1)S(1)}, bf16[512,512]{1,0:T(8,128)(2,1)S(1)}, u32[]{:S(2)}, u32[]{:S(2)}) collective-permute-start(bf16[512,512]{1,0:T(8,128)(2,1)S(1)} %get-tuple-element.60), channel_id=1, source_target_pairs={{0,6},{1,7},{2,0},{3,1},{4,2},{5,3},{6,4},{7,5},{8,14},{9,15},{10,... | collective-permute-start | bytes 1572872 | tf_op jit(solution)/shard_map/ppermute | solution.py:37
  42.1 3.7 %collective-permute-start.12 = (f32[16,1024]{1,0:T(8,128)S(1)}, f32[16,1024]{1,0:T(8,128)S(1)}, u32[]{:S(2)}, u32[]{:S(2)}) collective-permute-start(f32[16,1024]{1,0:T(8,128)S(1)} %bitcast_add_fusion), channel_id=1, source_target_pairs={{0,64},{16,80},{32,96},{48,112},{64,0},{80,16},{96,32},{112,48},{1... | collective-permute-start | bytes 196616 | tf_op jit(solution)/shard_map/ppermute | solution.py:307
  45.8 1.5 %collective-permute-start.13 = (f32[16,1024]{1,0:T(8,128)S(1)}, f32[16,1024]{1,0:T(8,128)S(1)}, u32[]{:S(2)}, u32[]{:S(2)}) collective-permute-start(f32[16,1024]{1,0:T(8,128)S(1)} %bitcast_add_fusion), channel_id=1, source_target_pairs={{0,128},{16,144},{32,160},{48,176},{64,192},{80,208},{96,224},{112... | collective-permute-start | bytes 196616 | tf_op jit(solution)/shard_map/ppermute | solution.py:307
  48.6 3.5 %collective-permute-done.13 = f32[16,1024]{1,0:T(8,128)S(1)} collective-permute-done((f32[16,1024]{1,0:T(8,128)S(1)}, f32[16,1024]{1,0:T(8,128)S(1)}, u32[]{:S(2)}, u32[]{:S(2)}) %collective-permute-start.13) | collective-permute-done | bytes 65568 | tf_op jit(solution)/shard_map/ppermute | solution.py:307
  52.1 1.4 %collective-permute-done.14 = f32[16,1024]{1,0:T(8,128)S(1)} collective-permute-done((f32[16,1024]{1,0:T(8,128)S(1)}, f32[16,1024]{1,0:T(8,128)S(1)}, u32[]{:S(2)}, u32[]{:S(2)}) %collective-permute-start.14) | collective-permute-done | bytes 65568 | tf_op jit(solution)/shard_map/ppermute | solution.py:307
  53.5 3.5 %apply_weight.2 = (f32[256,512]{1,0:T(8,128)S(1)}, f32[256,512]{1,0:T(8,128)S(1)}, bf16[256,8192]{1,0:T(8,128)(2,1)}, bf16[2,256,512]{2,1,0:T(8,128)(2,1)S(1)}, bf16[2,256,512]{2,1,0:T(8,128)(2,1)S(1)}) custom-call(s32[8]{0:T(128)S(1)} %broadcast_add_fusion.refs_0_.places, bf16[256,8192]{1,0:T(8,128)(2,1)S(1)} %copy-done.1, bf16[256,512]{1,0:T(8,128)(2,1)S(1)} %copy-done.3, ...), custom_call_target="tpu_custom_call" | custom-call | bytes 4194304 | tf_op jit(solution)/shard_map/apply_weight/pallas_call | solution.py:45
  57.3 3.1 %collective-permute-start.17 = (bf16[512,512]{1,0:T(8,128)(2,1)S(1)}, bf16[512,512]{1,0:T(8,128)(2,1)S(1)}, u32[]{:S(2)}, u32[]{:S(2)}) collective-permute-start(bf16[512,512]{1,0:T(8,128)(2,1)S(1)} %collective-permute-done.8._.refs_5_), channel_id=1, source_target_pairs={{0,6},{1,7},{2,0},{3,1},{4,2},{5,3},{6,4},{7,5},{8,14},{9,15},{10,... | collective-permute-start | bytes 1572872 | tf_op jit(solution)/shard_map/ppermute | solution.py:37
  61.9 4.6 %collective-permute-start.27 = (bf16[512,512]{1,0:T(8,128)(2,1)S(1)}, bf16[512,512]{1,0:T(8,128)(2,1)S(1)}, u32[]{:S(2)}, u32[]{:S(2)}) collective-permute-start(bf16[512,512]{1,0:T(8,128)(2,1)S(1)} %closing.2), channel_id=1, source_target_pairs={{0,8},{1,9},{2,10},{3,11},{4,12},{5,13},{6,14},{7,15},{8,0},{9,1},... | collective-permute-start | bytes 1572872 | tf_op jit(solution)/shard_map/ppermute | solution.py:37
  66.5 3.3 %collective-permute-done.15.refs_9_ = bf16[512,512]{1,0:T(8,128)(2,1)S(1)} collective-permute-done((bf16[512,512]{1,0:T(8,128)(2,1)S(1)}, bf16[512,512]{1,0:T(8,128)(2,1)S(1)}, u32[]{:S(2)}, u32[]{:S(2)}) %collective-permute-start.15) | collective-permute-done | bytes 524320 | tf_op jit(solution)/shard_map/ppermute | solution.py:37
  69.9 3.3 %collective-permute-start.22 = (bf16[256,512]{1,0:T(8,128)(2,1)S(1)}, bf16[256,512]{1,0:T(8,128)(2,1)S(1)}, u32[]{:S(2)}, u32[]{:S(2)}) collective-permute-start(bf16[256,512]{1,0:T(8,128)(2,1)S(1)} %slice.19), channel_id=1, source_target_pairs={{0,6},{1,7},{2,0},{3,1},{4,2},{5,3},{6,4},{7,5},{8,14},{9,15},{10,... | collective-permute-start | bytes 786440 | tf_op jit(solution)/shard_map/ppermute | solution.py:37
  74.5 1.5 %place.2.refs_12_ = bf16[256,8192]{1,0:T(8,128)(2,1)} custom-call(s32[8]{0:T(128)S(1)} %broadcast_add_fusion.1.places.refs_0_, bf16[2,256,512]{2,1,0:T(8,128)(2,1)S(1)} %collective-permute-done.18.refs_1_, bf16[2,256,512]{2,1,0:T(8,128)(2,1)S(1)} %collective-permute-done.19.refs_2_, ...), custom_call_target="tpu_custom_call", output_to_operand_aliasing={{}: (3, {})} | custom-call | bytes 5242880 | tf_op jit(solution)/shard_map/place/pallas_call | solution.py:45
  76.1 1.3 %collective-permute-done.21.refs_7_ = bf16[256,512]{1,0:T(8,128)(2,1)S(1)} collective-permute-done((bf16[256,512]{1,0:T(8,128)(2,1)S(1)}, bf16[256,512]{1,0:T(8,128)(2,1)S(1)}, u32[]{:S(2)}, u32[]{:S(2)}) %collective-permute-start.21) | collective-permute-done | bytes 262176 | tf_op jit(solution)/shard_map/ppermute | solution.py:37
  78.3 3.5 %apply_weight.3 = (f32[256,512]{1,0:T(8,128)S(1)}, bf16[256,8192]{1,0:T(8,128)(2,1)}, bf16[320,512]{1,0:T(8,128)(2,1)S(1)}, bf16[320,512]{1,0:T(8,128)(2,1)S(1)}...) custom-call(s32[8]{0:T(128)S(1)} %broadcast_add_fusion.refs_0_.places, ...), custom_call_target="tpu_custom_call", output_to_operand_aliasing={{1}: (12, {})} | custom-call | bytes 4194304 | tf_op jit(solution)/shard_map/apply_weight/pallas_call | solution.py:45
  82.6 2.3 %collective-permute-start.28 = (f32[16,1024]{1,0:T(8,128)S(1)}, f32[16,1024]{1,0:T(8,128)S(1)}, u32[]{:S(2)}, u32[]{:S(2)}) collective-permute-start(f32[16,1024]{1,0:T(8,128)S(1)} %add_add_fusion), channel_id=1, source_target_pairs={{0,32},{16,48},{32,0},{48,16},{64,96},{80,112},{96,64},{112,80},{1... | collective-permute-start | bytes 196616 | tf_op jit(solution)/shard_map/ppermute | solution.py:307
  85.0 3.5 %collective-permute-done.28 = f32[16,1024]{1,0:T(8,128)S(1)} collective-permute-done((f32[16,1024]{1,0:T(8,128)S(1)}, f32[16,1024]{1,0:T(8,128)S(1)}, u32[]{:S(2)}, u32[]{:S(2)}) %collective-permute-start.28) | collective-permute-done | bytes 65568 | tf_op jit(solution)/shard_map/ppermute | solution.py:307
  89.0 3.5 %collective-permute-done.16.refs_5_ = bf16[256,512]{1,0:T(8,128)(2,1)S(1)} collective-permute-done((bf16[256,512]{1,0:T(8,128)(2,1)S(1)}, bf16[256,512]{1,0:T(8,128)(2,1)S(1)}, u32[]{:S(2)}, u32[]{:S(2)}) %collective-permute-start.16) | collective-permute-done | bytes 262176 | tf_op jit(solution)/shard_map/ppermute | solution.py:37
  92.5 1.8 %collective-permute-start.30 = (bf16[256,512]{1,0:T(8,128)(2,1)S(1)}, bf16[256,512]{1,0:T(8,128)(2,1)S(1)}, u32[]{:S(2)}, u32[]{:S(2)}) collective-permute-start(bf16[256,512]{1,0:T(8,128)(2,1)S(1)} %get-tuple-element.90), channel_id=1, source_target_pairs={{0,6},{1,7},{2,0},{3,1},{4,2},{5,3},{6,4},{7,5},{8,14},{9,15},{10,... | collective-permute-start | bytes 786440 | tf_op jit(solution)/shard_map/ppermute | solution.py:37
  96.9 2.2 %place.3 = (bf16[256,8192]{1,0:T(8,128)(2,1)}, bf16[256,512]{1,0:T(8,128)(2,1)}) custom-call(s32[8]{0:T(128)S(1)} %broadcast_add_fusion.1.places.refs_0_, bf16[320,512]{1,0:T(8,128)(2,1)S(1)} %collective-permute-done.23.refs_1_, bf16[320,512]{1,0:T(8,128)(2,1)S(1)} %collective-permute-done.24.refs_2_, ...), custom_call_target="tpu_custom_call", output_to_operand_aliasing={{0}: (6, {})} | custom-call | bytes 5242880 | tf_op jit(solution)/shard_map/place/pallas_call | solution.py:45
  99.2 1.4 %collective-permute-done.30.right = bf16[256,512]{1,0:T(8,128)(2,1)S(1)} collective-permute-done((bf16[256,512]{1,0:T(8,128)(2,1)S(1)}, bf16[256,512]{1,0:T(8,128)(2,1)S(1)}, u32[]{:S(2)}, u32[]{:S(2)}) %collective-permute-start.30) | collective-permute-done | bytes 262176 | tf_op jit(solution)/shard_map/ppermute | solution.py:37
  100.6 2.5 %collective-permute-done.29.left = bf16[256,512]{1,0:T(8,128)(2,1)S(1)} collective-permute-done((bf16[256,512]{1,0:T(8,128)(2,1)S(1)}, bf16[256,512]{1,0:T(8,128)(2,1)S(1)}, u32[]{:S(2)}, u32[]{:S(2)}) %collective-permute-start.29) | collective-permute-done | bytes 262176 | tf_op jit(solution)/shard_map/ppermute | solution.py:37
  (70 shorter events, 16.0 us)
Async XLA Ops:
  4.7 11.0 %collective-permute-start.1 = (bf16[6,256,512]{2,1,0:T(8,128)(2,1)S(1)}, bf16[6,256,512]{2,1,0:T(8,128)(2,1)S(1)}, u32[]{:S(2)}, u32[]{:S(2)}) collective-permute-start(bf16[6,256,512]{2,1,0:T(8,128)(2,1)S(1)} %get-tuple-element.51), channel_id=1, source_target_pairs={{0,1},{1,0},{2,3},{3,2},{4,5},{5,4},{6,7},{7,6},{8,9},{9,8},{10,11... | collective-permute-start | bytes 4718600 | tf_op jit(solution)/shard_map/ppermute | solution.py:37
  4.8 10.9 %collective-permute-start = (bf16[3,256,512]{2,1,0:T(8,128)(2,1)S(1)}, bf16[3,256,512]{2,1,0:T(8,128)(2,1)S(1)}, u32[]{:S(2)}, u32[]{:S(2)}) collective-permute-start(bf16[3,256,512]{2,1,0:T(8,128)(2,1)S(1)} %get-tuple-element.50), channel_id=1, source_target_pairs={{0,1},{1,0},{2,3},{3,2},{4,5},{5,4},{6,7},{7,6},{8,9},{9,8},{10,11... | collective-permute-start | bytes 2359304 | tf_op jit(solution)/shard_map/ppermute | solution.py:37
  5.3 15.7 %collective-permute-start.4 = (bf16[512,512]{1,0:T(8,128)(2,1)}, bf16[512,512]{1,0:T(8,128)(2,1)S(1)}, u32[]{:S(2)}, u32[]{:S(2)}) collective-permute-start(bf16[512,512]{1,0:T(8,128)(2,1)} %bitcast.4), channel_id=1, source_target_pairs={{0,2},{1,3},{2,4},{3,5},{4,6},{5,7},{6,0},{7,1},{8,10},{9,11},{10,... | collective-permute-start | bytes 1572872 | tf_op jit(solution)/shard_map/ppermute | solution.py:37
  6.8 16.9 %collective-permute-start.6 = (bf16[512,512]{1,0:T(8,128)(2,1)}, bf16[512,512]{1,0:T(8,128)(2,1)S(1)}, u32[]{:S(2)}, u32[]{:S(2)}) collective-permute-start(bf16[512,512]{1,0:T(8,128)(2,1)} %bitcast.5), channel_id=1, source_target_pairs={{0,6},{1,7},{2,0},{3,1},{4,2},{5,3},{6,4},{7,5},{8,14},{9,15},{10,... | collective-permute-start | bytes 1572872 | tf_op jit(solution)/shard_map/ppermute | solution.py:37
  8.5 21.3 %collective-permute-start.8 = (bf16[512,512]{1,0:T(8,128)(2,1)}, bf16[512,512]{1,0:T(8,128)(2,1)S(1)}, u32[]{:S(2)}, u32[]{:S(2)}) collective-permute-start(bf16[512,512]{1,0:T(8,128)(2,1)} %bitcast.6), channel_id=1, source_target_pairs={{0,8},{1,9},{2,10},{3,11},{4,12},{5,13},{6,14},{7,15},{8,0},{9,1},... | collective-permute-start | bytes 1572872 | tf_op jit(solution)/shard_map/ppermute | solution.py:37
  17.0 20.4 %collective-permute-start.2 = (bf16[2,256,512]{2,1,0:T(8,128)(2,1)S(1)}, bf16[2,256,512]{2,1,0:T(8,128)(2,1)S(1)}, u32[]{:S(2)}, u32[]{:S(2)}) collective-permute-start(bf16[2,256,512]{2,1,0:T(8,128)(2,1)S(1)} %get-tuple-element.52), channel_id=1, source_target_pairs={{0,2},{1,3},{2,4},{3,5},{4,6},{5,7},{6,0},{7,1},{8,10},{9,11},{10,... | collective-permute-start | bytes 1572872 | tf_op jit(solution)/shard_map/ppermute | solution.py:37
  17.4 20.1 %collective-permute-start.3 = (bf16[2,256,512]{2,1,0:T(8,128)(2,1)S(1)}, bf16[2,256,512]{2,1,0:T(8,128)(2,1)S(1)}, u32[]{:S(2)}, u32[]{:S(2)}) collective-permute-start(bf16[2,256,512]{2,1,0:T(8,128)(2,1)S(1)} %get-tuple-element.53), channel_id=1, source_target_pairs={{0,6},{1,7},{2,0},{3,1},{4,2},{5,3},{6,4},{7,5},{8,14},{9,15},{10,... | collective-permute-start | bytes 1572872 | tf_op jit(solution)/shard_map/ppermute | solution.py:37
  21.0 4.9 %collective-permute-start.9 = (f32[16,1024]{1,0:T(8,128)S(1)}, f32[16,1024]{1,0:T(8,128)S(1)}, u32[]{:S(2)}, u32[]{:S(2)}) collective-permute-start(f32[16,1024]{1,0:T(8,128)S(1)} %bitcast.9), channel_id=1, source_target_pairs={{0,16},{16,0},{32,48},{48,32},{64,80},{80,64},{96,112},{112,96},{1... | collective-permute-start | bytes 196616 | tf_op jit(solution)/shard_map/ppermute | solution.py:307
  23.7 13.8 %collective-permute-start.5 = (bf16[256,512]{1,0:T(8,128)(2,1)S(1)}, bf16[256,512]{1,0:T(8,128)(2,1)S(1)}, u32[]{:S(2)}, u32[]{:S(2)}) collective-permute-start(bf16[256,512]{1,0:T(8,128)(2,1)S(1)} %slice.16), channel_id=1, source_target_pairs={{0,2},{1,3},{2,4},{3,5},{4,6},{5,7},{6,0},{7,1},{8,10},{9,11},{10,... | collective-permute-start | bytes 786440 | tf_op jit(solution)/shard_map/ppermute | solution.py:37
  25.9 11.6 %collective-permute-start.7 = (bf16[256,512]{1,0:T(8,128)(2,1)S(1)}, bf16[256,512]{1,0:T(8,128)(2,1)S(1)}, u32[]{:S(2)}, u32[]{:S(2)}) collective-permute-start(bf16[256,512]{1,0:T(8,128)(2,1)S(1)} %slice.17), channel_id=1, source_target_pairs={{0,6},{1,7},{2,0},{3,1},{4,2},{5,3},{6,4},{7,5},{8,14},{9,15},{10,... | collective-permute-start | bytes 786440 | tf_op jit(solution)/shard_map/ppermute | solution.py:37
  31.0 22.5 %copy-start.4 = (bf16[1,512,512]{2,1,0:T(8,128)(2,1)S(1)}, bf16[1,512,512]{2,1,0:T(8,128)(2,1)}, u32[]{:S(2)}) copy-start(bf16[1,512,512]{2,1,0:T(8,128)(2,1)} %param.10) | copy-start | bytes 1572868
  38.8 18.2 %collective-permute-start.10 = (bf16[512,512]{1,0:T(8,128)(2,1)S(1)}, bf16[512,512]{1,0:T(8,128)(2,1)S(1)}, u32[]{:S(2)}, u32[]{:S(2)}) collective-permute-start(bf16[512,512]{1,0:T(8,128)(2,1)S(1)} %get-tuple-element.59), channel_id=1, source_target_pairs={{0,2},{1,3},{2,4},{3,5},{4,6},{5,7},{6,0},{7,1},{8,10},{9,11},{10,... | collective-permute-start | bytes 1572872 | tf_op jit(solution)/shard_map/ppermute | solution.py:37
  40.3 16.7 %collective-permute-start.11 = (bf16[512,512]{1,0:T(8,128)(2,1)S(1)}, bf16[512,512]{1,0:T(8,128)(2,1)S(1)}, u32[]{:S(2)}, u32[]{:S(2)}) collective-permute-start(bf16[512,512]{1,0:T(8,128)(2,1)S(1)} %get-tuple-element.60), channel_id=1, source_target_pairs={{0,6},{1,7},{2,0},{3,1},{4,2},{5,3},{6,4},{7,5},{8,14},{9,15},{10,... | collective-permute-start | bytes 1572872 | tf_op jit(solution)/shard_map/ppermute | solution.py:37
  42.1 6.5 %collective-permute-start.12 = (f32[16,1024]{1,0:T(8,128)S(1)}, f32[16,1024]{1,0:T(8,128)S(1)}, u32[]{:S(2)}, u32[]{:S(2)}) collective-permute-start(f32[16,1024]{1,0:T(8,128)S(1)} %bitcast_add_fusion), channel_id=1, source_target_pairs={{0,64},{16,80},{32,96},{48,112},{64,0},{80,16},{96,32},{112,48},{1... | collective-permute-start | bytes 196616 | tf_op jit(solution)/shard_map/ppermute | solution.py:307
  45.8 6.3 %collective-permute-start.13 = (f32[16,1024]{1,0:T(8,128)S(1)}, f32[16,1024]{1,0:T(8,128)S(1)}, u32[]{:S(2)}, u32[]{:S(2)}) collective-permute-start(f32[16,1024]{1,0:T(8,128)S(1)} %bitcast_add_fusion), channel_id=1, source_target_pairs={{0,128},{16,144},{32,160},{48,176},{64,192},{80,208},{96,224},{112... | collective-permute-start | bytes 196616 | tf_op jit(solution)/shard_map/ppermute | solution.py:307
  47.3 6.2 %collective-permute-start.14 = (f32[16,1024]{1,0:T(8,128)S(1)}, f32[16,1024]{1,0:T(8,128)S(1)}, u32[]{:S(2)}, u32[]{:S(2)}) collective-permute-start(f32[16,1024]{1,0:T(8,128)S(1)} %bitcast_add_fusion), channel_id=1, source_target_pairs={{0,192},{16,208},{32,224},{48,240},{64,128},{80,144},{96,160},{112... | collective-permute-start | bytes 196616 | tf_op jit(solution)/shard_map/ppermute | solution.py:307
  57.0 12.7 %collective-permute-start.15 = (bf16[512,512]{1,0:T(8,128)(2,1)S(1)}, bf16[512,512]{1,0:T(8,128)(2,1)S(1)}, u32[]{:S(2)}, u32[]{:S(2)}) collective-permute-start(bf16[512,512]{1,0:T(8,128)(2,1)S(1)} %collective-permute-done.8._.refs_5_), channel_id=1, source_target_pairs={{0,2},{1,3},{2,4},{3,5},{4,6},{5,7},{6,0},{7,1},{8,10},{9,11},{10,... | collective-permute-start | bytes 1572872 | tf_op jit(solution)/shard_map/ppermute | solution.py:37
  57.3 12.6 %collective-permute-start.17 = (bf16[512,512]{1,0:T(8,128)(2,1)S(1)}, bf16[512,512]{1,0:T(8,128)(2,1)S(1)}, u32[]{:S(2)}, u32[]{:S(2)}) collective-permute-start(bf16[512,512]{1,0:T(8,128)(2,1)S(1)} %collective-permute-done.8._.refs_5_), channel_id=1, source_target_pairs={{0,6},{1,7},{2,0},{3,1},{4,2},{5,3},{6,4},{7,5},{8,14},{9,15},{10,... | collective-permute-start | bytes 1572872 | tf_op jit(solution)/shard_map/ppermute | solution.py:37
  60.3 14.1 %collective-permute-start.18 = (bf16[2,256,512]{2,1,0:T(8,128)(2,1)S(1)}, bf16[2,256,512]{2,1,0:T(8,128)(2,1)S(1)}, u32[]{:S(2)}, u32[]{:S(2)}) collective-permute-start(bf16[2,256,512]{2,1,0:T(8,128)(2,1)S(1)} %get-tuple-element.71), channel_id=1, source_target_pairs={{0,1},{1,0},{2,3},{3,2},{4,5},{5,4},{6,7},{7,6},{8,9},{9,8},{10,11... | collective-permute-start | bytes 1572872 | tf_op jit(solution)/shard_map/ppermute | solution.py:37
  60.3 14.1 %collective-permute-start.19 = (bf16[2,256,512]{2,1,0:T(8,128)(2,1)S(1)}, bf16[2,256,512]{2,1,0:T(8,128)(2,1)S(1)}, u32[]{:S(2)}, u32[]{:S(2)}) collective-permute-start(bf16[2,256,512]{2,1,0:T(8,128)(2,1)S(1)} %get-tuple-element.72), channel_id=1, source_target_pairs={{0,1},{1,0},{2,3},{3,2},{4,5},{5,4},{6,7},{7,6},{8,9},{9,8},{10,11... | collective-permute-start | bytes 1572872 | tf_op jit(solution)/shard_map/ppermute | solution.py:37
  61.9 26.5 %collective-permute-start.27 = (bf16[512,512]{1,0:T(8,128)(2,1)S(1)}, bf16[512,512]{1,0:T(8,128)(2,1)S(1)}, u32[]{:S(2)}, u32[]{:S(2)}) collective-permute-start(bf16[512,512]{1,0:T(8,128)(2,1)S(1)} %closing.2), channel_id=1, source_target_pairs={{0,8},{1,9},{2,10},{3,11},{4,12},{5,13},{6,14},{7,15},{8,0},{9,1},... | collective-permute-start | bytes 1572872 | tf_op jit(solution)/shard_map/ppermute | solution.py:37
  69.8 7.7 %collective-permute-start.21 = (bf16[256,512]{1,0:T(8,128)(2,1)S(1)}, bf16[256,512]{1,0:T(8,128)(2,1)S(1)}, u32[]{:S(2)}, u32[]{:S(2)}) collective-permute-start(bf16[256,512]{1,0:T(8,128)(2,1)S(1)} %slice.18), channel_id=1, source_target_pairs={{0,2},{1,3},{2,4},{3,5},{4,6},{5,7},{6,0},{7,1},{8,10},{9,11},{10,... | collective-permute-start | bytes 786440 | tf_op jit(solution)/shard_map/ppermute | solution.py:37
  69.9 8.4 %collective-permute-start.22 = (bf16[256,512]{1,0:T(8,128)(2,1)S(1)}, bf16[256,512]{1,0:T(8,128)(2,1)S(1)}, u32[]{:S(2)}, u32[]{:S(2)}) collective-permute-start(bf16[256,512]{1,0:T(8,128)(2,1)S(1)} %slice.19), channel_id=1, source_target_pairs={{0,6},{1,7},{2,0},{3,1},{4,2},{5,3},{6,4},{7,5},{8,14},{9,15},{10,... | collective-permute-start | bytes 786440 | tf_op jit(solution)/shard_map/ppermute | solution.py:37
  76.0 12.9 %collective-permute-start.20 = (bf16[256,512]{1,0:T(8,128)(2,1)S(1)}, bf16[256,512]{1,0:T(8,128)(2,1)S(1)}, u32[]{:S(2)}, u32[]{:S(2)}) collective-permute-start(bf16[256,512]{1,0:T(8,128)(2,1)S(1)} %get-tuple-element.74), channel_id=1, source_target_pairs={{0,6},{1,7},{2,0},{3,1},{4,2},{5,3},{6,4},{7,5},{8,14},{9,15},{10,... | collective-permute-start | bytes 786440 | tf_op jit(solution)/shard_map/ppermute | solution.py:37
  81.7 12.5 %collective-permute-start.23 = (bf16[320,512]{1,0:T(8,128)(2,1)S(1)}, bf16[320,512]{1,0:T(8,128)(2,1)S(1)}, u32[]{:S(2)}, u32[]{:S(2)}) collective-permute-start(bf16[320,512]{1,0:T(8,128)(2,1)S(1)} %get-tuple-element.77), channel_id=1, source_target_pairs={{0,1},{1,0},{2,3},{3,2},{4,5},{5,4},{6,7},{7,6},{8,9},{9,8},{10,11... | collective-permute-start | bytes 983048 | tf_op jit(solution)/shard_map/ppermute | solution.py:37
  81.8 10.7 %collective-permute-start.16 = (bf16[256,512]{1,0:T(8,128)(2,1)S(1)}, bf16[256,512]{1,0:T(8,128)(2,1)S(1)}, u32[]{:S(2)}, u32[]{:S(2)}) collective-permute-start(bf16[256,512]{1,0:T(8,128)(2,1)S(1)} %get-tuple-element.69), channel_id=1, source_target_pairs={{0,2},{1,3},{2,4},{3,5},{4,6},{5,7},{6,0},{7,1},{8,10},{9,11},{10,... | collective-permute-start | bytes 786440 | tf_op jit(solution)/shard_map/ppermute | solution.py:37
  82.6 5.8 %collective-permute-start.28 = (f32[16,1024]{1,0:T(8,128)S(1)}, f32[16,1024]{1,0:T(8,128)S(1)}, u32[]{:S(2)}, u32[]{:S(2)}) collective-permute-start(f32[16,1024]{1,0:T(8,128)S(1)} %add_add_fusion), channel_id=1, source_target_pairs={{0,32},{16,48},{32,0},{48,16},{64,96},{80,112},{96,64},{112,80},{1... | collective-permute-start | bytes 196616 | tf_op jit(solution)/shard_map/ppermute | solution.py:307
  88.4 8.5 %collective-permute-start.24 = (bf16[320,512]{1,0:T(8,128)(2,1)S(1)}, bf16[320,512]{1,0:T(8,128)(2,1)S(1)}, u32[]{:S(2)}, u32[]{:S(2)}) collective-permute-start(bf16[320,512]{1,0:T(8,128)(2,1)S(1)} %get-tuple-element.78), channel_id=1, source_target_pairs={{0,1},{1,0},{2,3},{3,2},{4,5},{5,4},{6,7},{7,6},{8,9},{9,8},{10,11... | collective-permute-start | bytes 983048 | tf_op jit(solution)/shard_map/ppermute | solution.py:37
  88.4 8.5 %collective-permute-start.25 = (bf16[320,512]{1,0:T(8,128)(2,1)S(1)}, bf16[320,512]{1,0:T(8,128)(2,1)S(1)}, u32[]{:S(2)}, u32[]{:S(2)}) collective-permute-start(bf16[320,512]{1,0:T(8,128)(2,1)S(1)} %get-tuple-element.79), channel_id=1, source_target_pairs={{0,1},{1,0},{2,3},{3,2},{4,5},{5,4},{6,7},{7,6},{8,9},{9,8},{10,11... | collective-permute-start | bytes 983048 | tf_op jit(solution)/shard_map/ppermute | solution.py:37
  88.9 8.0 %collective-permute-start.26 = (bf16[320,512]{1,0:T(8,128)(2,1)S(1)}, bf16[320,512]{1,0:T(8,128)(2,1)S(1)}, u32[]{:S(2)}, u32[]{:S(2)}) collective-permute-start(bf16[320,512]{1,0:T(8,128)(2,1)S(1)} %get-tuple-element.80), channel_id=1, source_target_pairs={{0,1},{1,0},{2,3},{3,2},{4,5},{5,4},{6,7},{7,6},{8,9},{9,8},{10,11... | collective-permute-start | bytes 983048 | tf_op jit(solution)/shard_map/ppermute | solution.py:37
  92.5 8.1 %collective-permute-start.30 = (bf16[256,512]{1,0:T(8,128)(2,1)S(1)}, bf16[256,512]{1,0:T(8,128)(2,1)S(1)}, u32[]{:S(2)}, u32[]{:S(2)}) collective-permute-start(bf16[256,512]{1,0:T(8,128)(2,1)S(1)} %get-tuple-element.90), channel_id=1, source_target_pairs={{0,6},{1,7},{2,0},{3,1},{4,2},{5,3},{6,4},{7,5},{8,14},{9,15},{10,... | collective-permute-start | bytes 786440 | tf_op jit(solution)/shard_map/ppermute | solution.py:37
  94.3 8.8 %collective-permute-start.29 = (bf16[256,512]{1,0:T(8,128)(2,1)S(1)}, bf16[256,512]{1,0:T(8,128)(2,1)S(1)}, u32[]{:S(2)}, u32[]{:S(2)}) collective-permute-start(bf16[256,512]{1,0:T(8,128)(2,1)S(1)} %get-tuple-element.88), channel_id=1, source_target_pairs={{0,2},{1,3},{2,4},{3,5},{4,6},{5,7},{6,0},{7,1},{8,10},{9,11},{10,... | collective-permute-start | bytes 786440 | tf_op jit(solution)/shard_map/ppermute | solution.py:37
  (8 other events, 94.1 us)
